TPU v7x, 32 devices: a whole 2x2x4 slice. The times are simulated.
32 devices in a mesh: dp: 8 (over y, x, core), tensor: 4 (over z).
Axes of the slice: x: 2, y: 2, z: 4, core: 2. Of those that a mesh axis runs over, the one named last changes fastest.
Arguments:
- patches: bfloat16 [32, 256, 768], P('dp', None, 'tensor'), may hold values from -6 to 6
- ctx_idx: int32 [32, 128], P('dp'), may hold values from 0 to 255, as said below
- tgt_idx: int32 [32, 64], P('dp'), may hold values from 0 to 255, as said below
- owner: int32 [19], replicated, may hold values from 0 to 22, as said below
- weights: float32 [4, 24, 384, 384], P('tensor', 'dp'), may hold values from -0.3125 to 0.3125
- stats_left: float32 [4, 24, 384, 384], P('tensor', 'dp')
- stats_right: float32 [4, 24, 384, 384], P('tensor', 'dp')
- root_left: float32 [4, 24, 384, 384], P('tensor', 'dp')
- root_right: float32 [4, 24, 384, 384], P('tensor', 'dp')
- teacher_slot_blocks: float32 [4, 24, 384, 384], P('tensor', 'dp'), may hold values from -0.3125 to 0.3125
- embed: float32 [768, 768], P('tensor', 'dp'), may hold values from -0.21875 to 0.21875
- embed_m: float32 [768, 768], P('tensor', 'dp')
- embed_v: float32 [768, 768], P('tensor', 'dp')
- teacher_embed: float32 [768, 768], P('tensor', 'dp'), may hold values from -0.21875 to 0.21875
- enc_vectors: float32 [7, 768], replicated
- enc_m: float32 [7, 768], replicated
- enc_v: float32 [7, 768], replicated
- pred_vectors: float32 [11, 384], replicated
- pred_m: float32 [11, 384], replicated
- pred_v: float32 [11, 384], replicated
- teacher_vectors: float32 [7, 768], replicated
Outputs:
- loss: float32 [], replicated
- block_grads: float32 [4, 24, 384, 384], P('tensor', 'dp')
- new_weights: float32 [4, 24, 384, 384], P('tensor', 'dp')
- new_left: float32 [4, 24, 384, 384], P('tensor', 'dp')
- new_right: float32 [4, 24, 384, 384], P('tensor', 'dp')
- new_teacher_blocks: float32 [4, 24, 384, 384], P('tensor', 'dp')
- new_embed: float32 [768, 768], P('tensor', 'dp')
- new_embed_m: float32 [768, 768], P('tensor', 'dp')
- new_embed_v: float32 [768, 768], P('tensor', 'dp')
- new_teacher_embed: float32 [768, 768], P('tensor', 'dp')
- new_enc_vectors: float32 [7, 768], replicated
- new_enc_m: float32 [7, 768], replicated
- new_enc_v: float32 [7, 768], replicated
- new_pred_vectors: float32 [11, 384], replicated
- new_pred_m: float32 [11, 384], replicated
- new_pred_v: float32 [11, 384], replicated
- new_teacher_vectors: float32 [7, 768], replicated
Inputs may be any that keep to these rules, and one draw needn't show every extreme that they name: `ctx_idx`: within an image the 128 context patches and the 64 target patches are all distinct, and the two sets share none. `tgt_idx`: see ctx_idx. `owner`: the 19 slots are distinct; slot s lies on index s // 3 of dp. The filled slots are, for k below 19, local slot k // 8 of index k % 8; which block takes which of them is drawn.
All inputs are finite; a program needn't handle non-finite values.
Results may differ from a plain program's by a relative error of at most 0.012.
The roundings to bfloat16 on the way count: a program that leaves them out, or rounds other values in their place, can miss the bound.
Values may be sent and summed in bfloat16 or wider, within the bound.
A program may use at most 192 MiB of HBM per device.

v0:
```python
import math

import jax
import jax.numpy as jnp
from jax import lax
from jax.sharding import PartitionSpec as P

HD = 64
PHD = 32
SIDE = 16
STEP = 10


exact = lax.Precision.HIGHEST


def gather_rows(values):
    return lax.all_gather(values, "tensor", axis=0, tiled=True)


def sum_rows(values):
    return lax.psum_scatter(values, "tensor", scatter_dimension=0, tiled=True)


def gelu_exact(values):
    return jax.nn.gelu(values, approximate=False)


def layer_norm(values, gain_row, shift_row):
    centre = values - jnp.mean(values, -1, keepdims=True)
    return (
        centre * lax.rsqrt(jnp.mean(centre * centre, -1, keepdims=True) + 1e-06) * gain_row
        + shift_row
    )


def sincos(cell_index, columns):
    quarter = columns // 4
    frequency = 1.0 / 10000.0 ** (jnp.arange(quarter).astype(jnp.float32) / quarter)
    col_angle = (cell_index % SIDE).astype(jnp.float32)[..., None] * frequency
    row_angle = (cell_index // SIDE).astype(jnp.float32)[..., None] * frequency
    return jnp.concatenate(
        [jnp.sin(col_angle), jnp.cos(col_angle), jnp.sin(row_angle), jnp.cos(row_angle)], -1
    )


def tile(blocks, first_block, per_side):
    edge_size = blocks.shape[-1]
    picked = blocks[first_block : first_block + per_side * per_side]
    return (
        picked.reshape(per_side, per_side, edge_size, edge_size)
        .transpose(0, 2, 1, 3)
        .reshape(per_side * edge_size, per_side * edge_size)
    )


def untile(matrix, per_side):
    edge_size = matrix.shape[0] // per_side
    return (
        matrix.reshape(per_side, edge_size, per_side, edge_size)
        .transpose(0, 2, 1, 3)
        .reshape(per_side * per_side, edge_size, edge_size)
    )


def encoder_mats(blocks, depth, per_side):
    count_per = per_side * per_side
    first_block = 3 * count_per * depth
    return (
        tile(blocks, first_block, per_side),
        tile(blocks, first_block + count_per, per_side),
        tile(blocks, first_block + 2 * count_per, per_side),
    )


def split_heads(qkv_rows, columns, head_size, images):
    shaped = qkv_rows.reshape(images, -1, 3, columns // head_size, head_size)
    return (shaped[:, :, 0], shaped[:, :, 1], shaped[:, :, 2])


def attend_forward(resid, attn_w, gain_row, shift_row, head_size, images):
    full_in = gather_rows(layer_norm(resid, gain_row, shift_row).astype(jnp.bfloat16))
    columns = attn_w.shape[1] // 4
    qkv_rows = jnp.dot(
        full_in, attn_w[:, : 3 * columns], preferred_element_type=jnp.float32
    ).astype(jnp.bfloat16)
    queries, keys_all, values_all = split_heads(qkv_rows, columns, head_size, images)
    scores = jnp.einsum(
        "gqhe,gkhe->ghqk", queries, keys_all, preferred_element_type=jnp.float32
    ) / math.sqrt(head_size)
    highest = jnp.max(scores, -1, keepdims=True)
    expo = jnp.exp(scores - highest)
    total = jnp.sum(expo, -1, keepdims=True)
    log_total = highest + jnp.log(total)
    attended = (
        jnp.einsum(
            "ghqk,gkhe->gqhe",
            (expo / total).astype(jnp.bfloat16),
            values_all,
            preferred_element_type=jnp.float32,
        )
        .astype(jnp.bfloat16)
        .reshape(-1, columns)
    )
    partial_out = jnp.einsum(
        "nc,dc->nd", attended, attn_w[:, 3 * columns :], preferred_element_type=jnp.float32
    )
    return (resid + sum_rows(partial_out), (full_in, qkv_rows, log_total, attended))


def attend_backward(grad_out, resid, attn_w, gain_row, shift_row, kept, head_size, images):
    full_in, qkv_rows, log_total, attended = kept
    columns = attn_w.shape[1] // 4
    grad_full = gather_rows(grad_out.astype(jnp.bfloat16))
    grad_out_w = jnp.einsum("nd,nc->dc", grad_full, attended, preferred_element_type=jnp.float32)
    grad_attended = jnp.dot(
        grad_full, attn_w[:, 3 * columns :], preferred_element_type=jnp.float32
    ).astype(jnp.bfloat16)
    queries, keys_all, values_all = split_heads(qkv_rows, columns, head_size, images)
    grad_heads = grad_attended.reshape(queries.shape)
    scores = jnp.einsum(
        "gqhe,gkhe->ghqk", queries, keys_all, preferred_element_type=jnp.float32
    ) / math.sqrt(head_size)
    softened = jnp.exp(scores - log_total)
    grad_values = jnp.einsum(
        "ghqk,gqhe->gkhe",
        softened.astype(jnp.bfloat16),
        grad_heads,
        preferred_element_type=jnp.float32,
    ).astype(jnp.bfloat16)
    grad_soft = jnp.einsum(
        "gqhe,gkhe->ghqk", grad_heads, values_all, preferred_element_type=jnp.float32
    )
    grad_scores = (
        softened * (grad_soft - jnp.sum(grad_soft * softened, -1, keepdims=True))
    ).astype(jnp.bfloat16)
    grad_queries = (
        jnp.einsum("ghqk,gkhe->gqhe", grad_scores, keys_all, preferred_element_type=jnp.float32)
        / math.sqrt(head_size)
    ).astype(jnp.bfloat16)
    grad_keys = (
        jnp.einsum("ghqk,gqhe->gkhe", grad_scores, queries, preferred_element_type=jnp.float32)
        / math.sqrt(head_size)
    ).astype(jnp.bfloat16)
    grad_qkv = jnp.stack([grad_queries, grad_keys, grad_values], 2).reshape(-1, 3 * columns)
    grad_in_w = jnp.einsum("nd,nc->dc", full_in, grad_qkv, preferred_element_type=jnp.float32)
    grad_normed = sum_rows(
        jnp.einsum(
            "nc,dc->nd", grad_qkv, attn_w[:, : 3 * columns], preferred_element_type=jnp.float32
        )
    )
    _, norm_back = jax.vjp(layer_norm, resid, gain_row, shift_row)
    grad_resid, grad_gain, grad_shift = norm_back(grad_normed)
    return (
        grad_out + grad_resid,
        jnp.concatenate([grad_in_w, grad_out_w], 1),
        grad_gain,
        grad_shift,
    )


def feed_forward(resid, up_w, down_t, gain_row, shift_row):
    full_in = gather_rows(layer_norm(resid, gain_row, shift_row).astype(jnp.bfloat16))
    hidden = jnp.dot(full_in, up_w, preferred_element_type=jnp.float32)
    active = gelu_exact(hidden).astype(jnp.bfloat16)
    partial_out = jnp.einsum("nc,dc->nd", active, down_t, preferred_element_type=jnp.float32)
    return (resid + sum_rows(partial_out), (full_in, hidden))


def feed_backward(grad_out, resid, up_w, down_t, gain_row, shift_row, kept):
    full_in, hidden = kept
    grad_full = gather_rows(grad_out.astype(jnp.bfloat16))
    active, gelu_back = jax.vjp(gelu_exact, hidden)
    grad_down = jnp.einsum(
        "nd,nc->dc", grad_full, active.astype(jnp.bfloat16), preferred_element_type=jnp.float32
    )
    grad_hidden = gelu_back(jnp.dot(grad_full, down_t, preferred_element_type=jnp.float32))[
        0
    ].astype(jnp.bfloat16)
    grad_up = jnp.einsum("nd,nc->dc", full_in, grad_hidden, preferred_element_type=jnp.float32)
    grad_normed = sum_rows(
        jnp.einsum("nc,dc->nd", grad_hidden, up_w, preferred_element_type=jnp.float32)
    )
    _, norm_back = jax.vjp(layer_norm, resid, gain_row, shift_row)
    grad_resid, grad_gain, grad_shift = norm_back(grad_normed)
    return (grad_out + grad_resid, grad_up, grad_down, grad_gain, grad_shift)


def block_forward(resid, mats, vector_rows, head_size, images):
    attn_w, up_w, down_t = mats
    middle, kept_attn = attend_forward(
        resid, attn_w, vector_rows[0], vector_rows[1], head_size, images
    )
    output, kept_feed = feed_forward(middle, up_w, down_t, vector_rows[2], vector_rows[3])
    return (output, (resid, kept_attn, middle, kept_feed))


def block_backward(grad_out, mats, vector_rows, kept, head_size, images):
    attn_w, up_w, down_t = mats
    resid, kept_attn, middle, kept_feed = kept
    grad_mid, grad_up, grad_down, gain_two, shift_two = feed_backward(
        grad_out, middle, up_w, down_t, vector_rows[2], vector_rows[3], kept_feed
    )
    grad_in, grad_attn, gain_one, shift_one = attend_backward(
        grad_mid, resid, attn_w, vector_rows[0], vector_rows[1], kept_attn, head_size, images
    )
    return (
        grad_in,
        (grad_attn, grad_up, grad_down),
        jnp.stack([gain_one, shift_one, gain_two, shift_two]),
    )


def adamw(master, moment, second, gradient, step_rate, weight_decay):
    moment = 0.9 * moment + 0.1 * gradient
    second = 0.999 * second + 0.001 * gradient * gradient
    unbiased_first = moment / (1.0 - 0.9**STEP)
    unbiased_second = second / (1.0 - 0.999**STEP)
    return (
        master
        - step_rate
        * (unbiased_first / (jnp.sqrt(unbiased_second) + 1e-08) + weight_decay * master),
        moment,
        second,
    )


def shards(
    patches,
    ctx_idx,
    tgt_idx,
    owner,
    weights,
    stats_left,
    stats_right,
    root_left,
    root_right,
    teacher_slot_blocks,
    embed,
    embed_m,
    embed_v,
    teacher_embed,
    enc_vectors,
    enc_m,
    enc_v,
    pred_vectors,
    pred_m,
    pred_v,
    teacher_vectors,
):
    tensor_size = lax.axis_size("tensor")
    group_list = lax.axis_size("dp")
    rank_index = lax.axis_index("tensor")
    images, npatches, pix_part = patches.shape
    slots_per_device = weights.shape[1]
    edge_size = weights.shape[-1]
    slot_count = slots_per_device * group_list
    block_count = owner.shape[0]
    model_width = enc_vectors.shape[1]
    pred_width = pred_vectors.shape[1]
    layers = (enc_vectors.shape[0] - 3) // 4
    players = (pred_vectors.shape[0] - 3) // 4
    per_side = model_width // edge_size
    teach_count = 3 * per_side * per_side * layers
    quarter_width = model_width // tensor_size
    context_len = ctx_idx.shape[1]
    target_len = tgt_idx.shape[1]
    seq_len = context_len + target_len
    slot_all, teach_all, embed_low, teach_embed_low = (
        lax.all_gather(weights.astype(jnp.bfloat16), "dp", axis=1, tiled=True),
        lax.all_gather(teacher_slot_blocks.astype(jnp.bfloat16), "dp", axis=1, tiled=True),
        lax.all_gather(embed.astype(jnp.bfloat16), "dp", axis=1, tiled=True),
        lax.all_gather(teacher_embed.astype(jnp.bfloat16), "dp", axis=1, tiled=True),
    )
    blocks = slot_all[0][owner]
    teach = teach_all[0][owner[:teach_count]]
    ctx_patch = jnp.take_along_axis(patches, ctx_idx[:, :, None], 1).reshape(-1, pix_part)
    all_patch = patches.reshape(-1, pix_part)
    student_in, teacher_in = sum_rows(
        (
            jnp.dot(ctx_patch, embed_low, preferred_element_type=jnp.float32),
            jnp.dot(all_patch, teach_embed_low, preferred_element_type=jnp.float32),
        )
    )
    ctx_rows = student_in.shape[0]
    ctx_pos = lax.dynamic_slice_in_dim(ctx_idx.reshape(-1), rank_index * ctx_rows, ctx_rows)
    resid = student_in + enc_vectors[4 * layers + 2] + sincos(ctx_pos, model_width)
    teach_rows_dev = teacher_in.shape[0]
    teach_pos = (rank_index * teach_rows_dev + jnp.arange(teach_rows_dev)) % npatches
    teach_resid = teacher_in + teacher_vectors[4 * layers + 2] + sincos(teach_pos, model_width)
    depth = 0
    mats = encoder_mats(blocks, depth, per_side)
    enc_mats = [mats]
    resid, kept = block_forward(resid, mats, enc_vectors[4 * depth : 4 * depth + 4], HD, images)
    enc_kept = [kept]
    teach_resid, _ = block_forward(
        teach_resid,
        encoder_mats(teach, depth, per_side),
        teacher_vectors[4 * depth : 4 * depth + 4],
        HD,
        images,
    )
    enc_out, enc_norm_back = jax.vjp(
        layer_norm, resid, enc_vectors[4 * layers], enc_vectors[4 * layers + 1]
    )
    target = layer_norm(
        layer_norm(teach_resid, teacher_vectors[4 * layers], teacher_vectors[4 * layers + 1]),
        1.0,
        0.0,
    ).astype(jnp.bfloat16)
    inout = blocks[block_count - 1]
    enc_feat, target_feat = (
        lax.all_to_all(
            enc_out.astype(jnp.bfloat16), "tensor", split_axis=1, concat_axis=0, tiled=True
        ),
        lax.all_to_all(target, "tensor", split_axis=1, concat_axis=0, tiled=True),
    )
    target_rows = (
        jnp.take_along_axis(
            target_feat.reshape(images, npatches, quarter_width), tgt_idx[:, :, None], 1
        )
        .reshape(-1, quarter_width)
        .astype(jnp.float32)
    )
    projected = jnp.einsum(
        "nc,pc->np", enc_feat, inout[:, :quarter_width], preferred_element_type=jnp.float32
    )
    padded = jnp.concatenate(
        [
            projected.reshape(images, context_len, pred_width),
            jnp.zeros((images, target_len, pred_width), jnp.float32),
        ],
        1,
    ).reshape(-1, pred_width)
    tokens = sum_rows(padded)
    pred_rows = tokens.shape[0]
    local_rows = rank_index * pred_rows + jnp.arange(pred_rows)
    pred_pos = lax.dynamic_slice_in_dim(
        jnp.concatenate([ctx_idx, tgt_idx], 1).reshape(-1), rank_index * pred_rows, pred_rows
    )
    is_target = (local_rows % seq_len >= context_len).astype(jnp.float32)[:, None]
    tokens = tokens + sincos(pred_pos, pred_width) + is_target * pred_vectors[4 * players + 2]
    pred_kept = []
    for depth in range(players):
        first_block = teach_count + 3 * depth
        mats = (blocks[first_block], blocks[first_block + 1], blocks[first_block + 2])
        tokens, kept = block_forward(
            tokens, mats, pred_vectors[4 * depth : 4 * depth + 4], PHD, images
        )
        pred_kept.append(kept)
    pred_normed, pred_norm_back = jax.vjp(
        layer_norm, tokens, pred_vectors[4 * players], pred_vectors[4 * players + 1]
    )
    normed_full = gather_rows(pred_normed.astype(jnp.bfloat16))
    normed_tgt = normed_full.reshape(images, seq_len, pred_width)[:, context_len:].reshape(
        -1, pred_width
    )
    predicted = jnp.dot(normed_tgt, inout[:, quarter_width:], preferred_element_type=jnp.float32)
    denominator = images * group_list * target_len * model_width
    residual_gap = predicted - target_rows
    magnitude = jnp.abs(residual_gap)
    loss_part = (
        jnp.sum(jnp.where(magnitude < 1.0, 0.5 * residual_gap * residual_gap, magnitude - 0.5))
        / denominator
    )
    grad_pred = (jnp.clip(residual_gap, -1.0, 1.0) / denominator).astype(jnp.bfloat16)
    grad_wout = jnp.einsum("np,nc->pc", normed_tgt, grad_pred, preferred_element_type=jnp.float32)
    grad_normed_tgt = jnp.einsum(
        "nc,pc->np", grad_pred, inout[:, quarter_width:], preferred_element_type=jnp.float32
    )
    grad_normed_pad = jnp.concatenate(
        [
            jnp.zeros((images, context_len, pred_width), jnp.float32),
            grad_normed_tgt.reshape(images, target_len, pred_width),
        ],
        1,
    ).reshape(-1, pred_width)
    grad_tokens, pred_final_gain, pred_final_shift = pred_norm_back(sum_rows(grad_normed_pad))
    pred_block_grads = []
    pred_vec_grads = []
    for depth in reversed(range(players)):
        first_block = teach_count + 3 * depth
        mats = (blocks[first_block], blocks[first_block + 1], blocks[first_block + 2])
        grad_tokens, mat_grads, vec_grads = block_backward(
            grad_tokens,
            mats,
            pred_vectors[4 * depth : 4 * depth + 4],
            pred_kept[depth],
            PHD,
            images,
        )
        pred_block_grads = [jnp.stack(mat_grads)] + pred_block_grads
        pred_vec_grads = [vec_grads] + pred_vec_grads
    mask_grad = jnp.sum(grad_tokens * is_target, 0)
    grad_proj_full = gather_rows(grad_tokens.astype(jnp.bfloat16))
    grad_proj = grad_proj_full.reshape(images, seq_len, pred_width)[:, :context_len].reshape(
        -1, pred_width
    )
    grad_win = jnp.einsum("np,nc->pc", grad_proj, enc_feat, preferred_element_type=jnp.float32)
    grad_feat = jnp.dot(
        grad_proj, inout[:, :quarter_width], preferred_element_type=jnp.float32
    ).astype(jnp.bfloat16)
    grad_enc = lax.all_to_all(grad_feat, "tensor", split_axis=0, concat_axis=1, tiled=True).astype(
        jnp.float32
    )
    grad_resid, enc_final_gain, enc_final_shift = enc_norm_back(grad_enc)
    enc_block_grads = []
    enc_vec_grads = []
    for depth in reversed(range(layers)):
        grad_resid, mat_grads, vec_grads = block_backward(
            grad_resid,
            enc_mats[depth],
            enc_vectors[4 * depth : 4 * depth + 4],
            enc_kept[depth],
            HD,
            images,
        )
        enc_block_grads = [
            jnp.concatenate([untile(piece, per_side) for piece in mat_grads], 0)
        ] + enc_block_grads
        enc_vec_grads = [vec_grads] + enc_vec_grads
    grad_embed_rows = gather_rows(grad_resid.astype(jnp.bfloat16))
    embed_full_grad = jnp.einsum(
        "np,nd->pd", ctx_patch, grad_embed_rows, preferred_element_type=jnp.float32
    )
    patch_bias_grad = jnp.sum(grad_resid, 0)
    block_grads = jnp.concatenate(
        enc_block_grads + pred_block_grads + [jnp.concatenate([grad_win, grad_wout], 1)[None]], 0
    )
    enc_grad = jnp.concatenate(
        enc_vec_grads + [jnp.stack([enc_final_gain, enc_final_shift, patch_bias_grad])], 0
    )
    pred_grad = jnp.concatenate(
        pred_vec_grads + [jnp.stack([pred_final_gain, pred_final_shift, mask_grad])], 0
    )
    enc_total, pred_total, loss_total = lax.psum((enc_grad, pred_grad, loss_part), ("dp", "tensor"))
    slot_of = (
        jnp.full((slot_count,), block_count, jnp.int32)
        .at[owner]
        .set(jnp.arange(block_count, dtype=jnp.int32))
    )
    padded_grads = jnp.concatenate(
        [block_grads, jnp.zeros((1,) + block_grads.shape[1:], jnp.float32)], 0
    )
    slot_sum, embed_grad = (
        lax.psum_scatter(padded_grads[slot_of], "dp", scatter_dimension=0, tiled=True),
        lax.psum_scatter(embed_full_grad, "dp", scatter_dimension=1, tiled=True),
    )
    slot_grads = slot_sum[None]
    new_left = 0.95 * stats_left + 0.05 * jnp.einsum(
        "tsij,tskj->tsik",
        slot_grads,
        slot_grads,
        precision=exact,
        preferred_element_type=jnp.float32,
    )
    new_right = 0.95 * stats_right + 0.05 * jnp.einsum(
        "tsji,tsjk->tsik",
        slot_grads,
        slot_grads,
        precision=exact,
        preferred_element_type=jnp.float32,
    )
    left_side = jnp.einsum(
        "tsij,tsjk->tsik",
        root_left,
        slot_grads,
        precision=exact,
        preferred_element_type=jnp.float32,
    )
    direction = jnp.einsum(
        "tsij,tsjk->tsik",
        left_side,
        root_right,
        precision=exact,
        preferred_element_type=jnp.float32,
    )
    direction = direction * lax.rsqrt(
        jnp.mean(direction * direction, axis=(2, 3), keepdims=True) + 1e-06
    )
    new_weights = weights - 0.05 * (direction + 0.05 * weights)
    new_teacher_blocks = 0.7 * teacher_slot_blocks + 0.3 * new_weights
    new_embed, new_embed_m, new_embed_v = adamw(embed, embed_m, embed_v, embed_grad, 0.05, 0.05)
    new_enc, new_enc_m, new_enc_v = adamw(enc_vectors, enc_m, enc_v, enc_total, 0.5, 0.0)
    new_pred, new_pred_m, new_pred_v = adamw(pred_vectors, pred_m, pred_v, pred_total, 0.5, 0.0)
    new_teacher_embed = 0.7 * teacher_embed + 0.3 * new_embed
    new_teacher_vectors = 0.7 * teacher_vectors + 0.3 * new_enc
    return (
        loss_total,
        slot_grads,
        new_weights,
        new_left,
        new_right,
        new_teacher_blocks,
        new_embed,
        new_embed_m,
        new_embed_v,
        new_teacher_embed,
        new_enc,
        new_enc_m,
        new_enc_v,
        new_pred,
        new_pred_m,
        new_pred_v,
        new_teacher_vectors,
    )


def solution(mesh):
    in_specs = (
        P("dp", None, "tensor"),
        P("dp", None),
        P("dp", None),
        P(),
        P("tensor", "dp", None, None),
        P("tensor", "dp", None, None),
        P("tensor", "dp", None, None),
        P("tensor", "dp", None, None),
        P("tensor", "dp", None, None),
        P("tensor", "dp", None, None),
        P("tensor", "dp"),
        P("tensor", "dp"),
        P("tensor", "dp"),
        P("tensor", "dp"),
        P(),
        P(),
        P(),
        P(),
        P(),
        P(),
        P(),
    )
    out_specs = (
        P(),
        P("tensor", "dp", None, None),
        P("tensor", "dp", None, None),
        P("tensor", "dp", None, None),
        P("tensor", "dp", None, None),
        P("tensor", "dp", None, None),
        P("tensor", "dp"),
        P("tensor", "dp"),
        P("tensor", "dp"),
        P("tensor", "dp"),
        P(),
        P(),
        P(),
        P(),
        P(),
        P(),
        P(),
    )
    return jax.shard_map(shards, mesh=mesh, in_specs=in_specs, out_specs=out_specs, check_vma=False)
```

profile of v0, /device:TPU:0, one launch (start us, length us, event | category | flops | bytes accessed | tf_op | source)
XLA Modules:
  0.0 1330.0 jit_solution(14188828751356873958)
XLA Ops:
  10.6 12.1 all_gather.63
  23.9 5.6 gather_fusion.3
  36.3 31.7 %reduce-scatter.23.cloned.1.call-done = f32[128,768]{1,0:T(8,128)} async-done(((f32[512,768]{1,0:T(8,128)}), f32[128,768]{1,0:T(8,128)}) %reduce-scatter.23.cloned.1.call-update) | async-done | bytes 393232 | tf_op jit(solution)/shard_map/reduce_scatter | solution.py:22
  70.1 18.2 %all_gather.64 = bf16[512,768]{1,0:T(8,128)(2,1)S(1)} all-gather(bf16[128,768]{1,0:T(8,128)(2,1)S(1)} %add_convert_fusion.7), channel_id=1, replica_groups=mesh['dp'=8,'tensor'=4] {'tensor'}, dimensions={0}, use_global_device_ids=true | all-gather | bytes 983040 | tf_op jit(solution)/shard_map/all_gather | solution.py:18
  88.2 7.9 gather_fusion
  115.3 27.9 %reduce-scatter.25.cloned.1.call-done = f32[128,768]{1,0:T(8,128)} async-done(((f32[512,768]{1,0:T(8,128)}), f32[128,768]{1,0:T(8,128)}) %reduce-scatter.25.cloned.1.call-update) | async-done | bytes 393232 | tf_op jit(solution)/shard_map/reduce_scatter | solution.py:22
  145.4 18.1 %all_gather.66 = bf16[512,768]{1,0:T(8,128)(2,1)S(1)} all-gather(bf16[128,768]{1,0:T(8,128)(2,1)S(1)} %add_convert_fusion.6), channel_id=1, replica_groups=mesh['dp'=8,'tensor'=4] {'tensor'}, dimensions={0}, use_global_device_ids=true | all-gather | bytes 983040 | tf_op jit(solution)/shard_map/all_gather | solution.py:18
  163.6 5.3 multiply_convert_fusion.2
  173.6 9.8 all_gather.72
  189.5 17.1 %reduce-scatter.27.cloned.1.call-done = f32[128,768]{1,0:T(8,128)} async-done(((f32[512,768]{1,0:T(8,128)}), f32[128,768]{1,0:T(8,128)}) %reduce-scatter.27.cloned.1.call-update) | async-done | bytes 393232 | tf_op jit(solution)/shard_map/reduce_scatter | solution.py:22
  220.9 8.1 all-to-all-done
  238.1 33.0 %reduce-scatter.39.cloned.1.call-done = f32[256,768]{1,0:T(8,128)} async-done(((f32[1024,768]{1,0:T(8,128)}), f32[256,768]{1,0:T(8,128)}) %reduce-scatter.39.cloned.1.call-update) | async-done | bytes 786448 | tf_op jit(solution)/shard_map/reduce_scatter | solution.py:22
  274.6 12.3 reduce-scatter.31.cloned.1.call-start
  287.0 6.0 gather_fusion.1
  293.1 27.9 %reduce-scatter.29.cloned.1.call-done = f32[192,384]{1,0:T(8,128)} async-done(((f32[768,384]{1,0:T(8,128)}), f32[192,384]{1,0:T(8,128)}) %reduce-scatter.29.cloned.1.call-update) | async-done | bytes 294928 | tf_op jit(solution)/shard_map/reduce_scatter | solution.py:22
  322.8 16.7 %all_gather.67 = bf16[768,384]{1,0:T(8,128)(2,1)S(1)} all-gather(bf16[192,384]{1,0:T(8,128)(2,1)S(1)} %add_convert_fusion.13), channel_id=1, replica_groups=mesh['dp'=8,'tensor'=4] {'tensor'}, dimensions={0}, use_global_device_ids=true | all-gather | bytes 737280 | tf_op jit(solution)/shard_map/all_gather | solution.py:18
  382.4 20.5 %all_gather.68 = bf16[768,384]{1,0:T(8,128)(2,1)S(1)} all-gather(bf16[192,384]{1,0:T(8,128)(2,1)S(1)} %add_convert_fusion.12), channel_id=1, replica_groups=mesh['dp'=8,'tensor'=4] {'tensor'}, dimensions={0}, use_global_device_ids=true | all-gather | bytes 737280 | tf_op jit(solution)/shard_map/all_gather | solution.py:18
  402.9 5.2 multiply_convert_fusion.4
  411.5 35.6 %reduce-scatter.41.cloned.1.call-done = f32[256,768]{1,0:T(8,128)} async-done(((f32[1024,768]{1,0:T(8,128)}), f32[256,768]{1,0:T(8,128)}) %reduce-scatter.41.cloned.1.call-update) | async-done | bytes 786448 | tf_op jit(solution)/shard_map/reduce_scatter | solution.py:22
  450.6 47.2 %reduce-scatter.33.cloned.1.call-done = f32[192,384]{1,0:T(8,128)} async-done(((f32[768,384]{1,0:T(8,128)}), f32[192,384]{1,0:T(8,128)}) %reduce-scatter.33.cloned.1.call-update) | async-done | bytes 294928 | tf_op jit(solution)/shard_map/reduce_scatter | solution.py:22
  499.9 16.7 %all_gather.69 = bf16[768,384]{1,0:T(8,128)(2,1)S(1)} all-gather(bf16[192,384]{1,0:T(8,128)(2,1)S(1)} %add_convert_fusion.11), channel_id=1, replica_groups=mesh['dp'=8,'tensor'=4] {'tensor'}, dimensions={0}, use_global_device_ids=true | all-gather | bytes 737280 | tf_op jit(solution)/shard_map/all_gather | solution.py:18
  538.1 12.4 fusion.29
  550.6 7.8 reduce-scatter.35.cloned.1.call-done
  560.5 20.6 %all_gather.70 = bf16[768,384]{1,0:T(8,128)(2,1)S(1)} all-gather(bf16[192,384]{1,0:T(8,128)(2,1)S(1)} %add_convert_fusion.10), channel_id=1, replica_groups=mesh['dp'=8,'tensor'=4] {'tensor'}, dimensions={0}, use_global_device_ids=true | all-gather | bytes 737280 | tf_op jit(solution)/shard_map/all_gather | solution.py:18
  581.1 5.1 multiply_convert_fusion.3
  589.6 35.7 %reduce-scatter.43.cloned.1.call-done = f32[256,768]{1,0:T(8,128)} async-done(((f32[1024,768]{1,0:T(8,128)}), f32[256,768]{1,0:T(8,128)}) %reduce-scatter.43.cloned.1.call-update) | async-done | bytes 786448 | tf_op jit(solution)/shard_map/reduce_scatter | solution.py:22
  635.1 22.6 %all-to-all-done.1 = bf16[256,4,192]{0,2,1:T(8,128)(2,1)} async-done(((bf16[256,4,192]{0,2,1:T(8,128)(2,1)}), bf16[256,4,192]{0,2,1:T(8,128)(2,1)}, u32[]{:S(2)}, u32[]{:S(2)}) %all-to-all-start.1) | async-done | bytes 393248 | tf_op jit(solution)/shard_map/all_to_all | solution.py:316
  666.3 15.9 %all_gather.71 = bf16[768,384]{1,0:T(8,128)(2,1)S(1)} all-gather(bf16[192,384]{1,0:T(8,128)(2,1)S(1)} %add_convert_fusion.9), channel_id=1, replica_groups=mesh['dp'=8,'tensor'=4] {'tensor'}, dimensions={0}, use_global_device_ids=true | all-gather | bytes 737280 | tf_op jit(solution)/shard_map/all_gather | solution.py:18
  685.9 29.2 %reduce-scatter.45.cloned.1.call-done = f32[192,384]{1,0:T(8,128)} async-done(((f32[768,384]{1,0:T(8,128)}), f32[192,384]{1,0:T(8,128)}) %reduce-scatter.45.cloned.1.call-update) | async-done | bytes 294928 | tf_op jit(solution)/shard_map/reduce_scatter | solution.py:22
  719.2 16.2 %all_gather.76 = bf16[768,384]{1,0:T(8,128)(2,1)S(1)} all-gather(bf16[192,384]{1,0:T(8,128)(2,1)S(1)} %add_convert_fusion.14), channel_id=1, replica_groups=mesh['dp'=8,'tensor'=4] {'tensor'}, dimensions={0}, use_global_device_ids=true | all-gather | bytes 737280 | tf_op jit(solution)/shard_map/all_gather | solution.py:18
  741.0 27.5 %reduce-scatter.47.cloned.1.call-done = f32[192,384]{1,0:T(8,128)} async-done(((f32[768,384]{1,0:T(8,128)}), f32[192,384]{1,0:T(8,128)}) %reduce-scatter.47.cloned.1.call-update) | async-done | bytes 294928 | tf_op jit(solution)/shard_map/reduce_scatter | solution.py:22
  774.1 16.4 %all_gather.77 = bf16[768,384]{1,0:T(8,128)(2,1)S(1)} all-gather(bf16[192,384]{1,0:T(8,128)(2,1)S(1)} %get-tuple-element.97), channel_id=1, replica_groups=mesh['dp'=8,'tensor'=4] {'tensor'}, dimensions={0}, use_global_device_ids=true | all-gather | bytes 737280 | tf_op jit(solution)/shard_map/all_gather | solution.py:18
  807.1 27.5 %reduce-scatter.49.cloned.1.call-done = f32[192,384]{1,0:T(8,128)} async-done(((f32[768,384]{1,0:T(8,128)}), f32[192,384]{1,0:T(8,128)}) %reduce-scatter.49.cloned.1.call-update) | async-done | bytes 294928 | tf_op jit(solution)/shard_map/reduce_scatter | solution.py:22
  839.8 16.2 %all_gather.78 = bf16[768,384]{1,0:T(8,128)(2,1)S(1)} all-gather(bf16[192,384]{1,0:T(8,128)(2,1)S(1)} %fusion.165), channel_id=1, replica_groups=mesh['dp'=8,'tensor'=4] {'tensor'}, dimensions={0}, use_global_device_ids=true | all-gather | bytes 737280 | tf_op jit(solution)/shard_map/all_gather | solution.py:18
  861.5 27.5 %reduce-scatter.51.cloned.1.call-done = f32[192,384]{1,0:T(8,128)} async-done(((f32[768,384]{1,0:T(8,128)}), f32[192,384]{1,0:T(8,128)}) %reduce-scatter.51.cloned.1.call-update) | async-done | bytes 294928 | tf_op jit(solution)/shard_map/reduce_scatter | solution.py:22
  894.1 16.2 %all_gather.79 = bf16[768,384]{1,0:T(8,128)(2,1)S(1)} all-gather(bf16[192,384]{1,0:T(8,128)(2,1)S(1)} %get-tuple-element.91), channel_id=1, replica_groups=mesh['dp'=8,'tensor'=4] {'tensor'}, dimensions={0}, use_global_device_ids=true | all-gather | bytes 737280 | tf_op jit(solution)/shard_map/all_gather | solution.py:18
  926.8 27.6 %reduce-scatter.53.cloned.1.call-done = f32[192,384]{1,0:T(8,128)} async-done(((f32[768,384]{1,0:T(8,128)}), f32[192,384]{1,0:T(8,128)}) %reduce-scatter.53.cloned.1.call-update) | async-done | bytes 294928 | tf_op jit(solution)/shard_map/reduce_scatter | solution.py:22
  958.2 16.6 %all_gather.80 = bf16[768,384]{1,0:T(8,128)(2,1)S(1)} all-gather(bf16[192,384]{1,0:T(8,128)(2,1)S(1)} %get-tuple-element.148), channel_id=1, replica_groups=mesh['dp'=8,'tensor'=4] {'tensor'}, dimensions={0}, use_global_device_ids=true | all-gather | bytes 737280 | tf_op jit(solution)/shard_map/all_gather | solution.py:18
  976.1 9.2 all_to_all.45
  993.4 16.7 %all_gather.81 = bf16[512,768]{1,0:T(8,128)(2,1)S(1)} all-gather(bf16[128,768]{1,0:T(8,128)(2,1)S(1)} %add_convert_fusion.8), channel_id=1, replica_groups=mesh['dp'=8,'tensor'=4] {'tensor'}, dimensions={0}, use_global_device_ids=true | all-gather | bytes 983040 | tf_op jit(solution)/shard_map/all_gather | solution.py:18
  1027.6 23.8 %reduce-scatter.55.cloned.1.call-done = f32[128,768]{1,0:T(8,128)} async-done(((f32[512,768]{1,0:T(8,128)}), f32[128,768]{1,0:T(8,128)}) %reduce-scatter.55.cloned.1.call-update) | async-done | bytes 393232 | tf_op jit(solution)/shard_map/reduce_scatter | solution.py:22
  1056.7 18.2 %all_gather.82 = bf16[512,768]{1,0:T(8,128)(2,1)S(1)} all-gather(bf16[128,768]{1,0:T(8,128)(2,1)S(1)} %get-tuple-element.83), channel_id=1, replica_groups=mesh['dp'=8,'tensor'=4] {'tensor'}, dimensions={0}, use_global_device_ids=true | all-gather | bytes 983040 | tf_op jit(solution)/shard_map/all_gather | solution.py:18
  1121.9 5.3 copy.196
  1141.0 17.5 %all_gather.83 = bf16[512,768]{1,0:T(8,128)(2,1)S(1)} all-gather(bf16[128,768]{1,0:T(8,128)(2,1)S(1)} %get-tuple-element.145), channel_id=1, replica_groups=mesh['dp'=8,'tensor'=4] {'tensor'}, dimensions={0}, use_global_device_ids=true | all-gather | bytes 983040 | tf_op jit(solution)/shard_map/all_gather | solution.py:18
  1166.5 12.5 gather_fusion.2
  1180.9 39.5 %all-reduce.2 = (f32[]{:T(128)}, f32[7,768]{1,0:T(8,128)S(1)}, f32[11,384]{1,0:T(8,128)S(1)}) all-reduce(f32[]{:T(128)S(6)} %div.415, f32[7,768]{1,0:T(8,128)S(1)} %concatenate.50, f32[11,384]{1,0:T(8,128)S(1)} %concatenate.51), channel_id=1, replica_groups=mesh['dp'=8,'tensor'=4] {'dp','tensor'}, use_global_device_ids=true, to_apply=%region_44.45 | all-reduce | flops 9601 | bytes 76808 | tf_op jit(solution)/shard_map/psum | solution.py:436
  1223.6 76.0 %reduce-scatter.57.cloned.1.call-done = f32[3,384,384]{2,1,0:T(8,128)} async-done(((f32[24,384,384]{2,1,0:T(8,128)}), f32[3,384,384]{2,1,0:T(8,128)}) %reduce-scatter.57.cloned.1.call-update) | async-done | bytes 1769488 | tf_op jit(solution)/shard_map/reduce_scatter | solution.py:446
  1299.6 5.6 fusion.20
  (770 shorter events, 361.9 us)
Async XLA Ops:
  8.0 1297.2 %copy-start = (f32[1,3,384,384]{3,2,1,0:T(8,128)S(1)}, f32[1,3,384,384]{3,2,1,0:T(8,128)}, u32[]{:S(2)}) copy-start(f32[1,3,384,384]{3,2,1,0:T(8,128)} %param.29) | copy-start | bytes 5308420
  8.0 59.9 %reduce-scatter.23.cloned.1.call-start = ((), (), s32[]{:S(2)}) async-start(), calls=%async_computation.23 | async-start | bytes 1966080 | tf_op jit(solution)/shard_map/reduce_scatter | solution.py:22
  32.2 56.0 %all-gather.5.cloned.1.call-start = ((), (), s32[]{:S(2)}) async-start(), calls=%async_computation.24 | async-start | bytes 7962624 | tf_op jit(solution)/shard_map/all_gather | solution.py:270
  33.3 109.8 %reduce-scatter.25.cloned.1.call-start = ((), (), s32[]{:S(2)}) async-start(), calls=%async_computation.25 | async-start | bytes 1966080 | tf_op jit(solution)/shard_map/reduce_scatter | solution.py:22
  33.4 54.9 %copy-start.184 = (f32[192]{0:T(256)}, f32[192]{0:T(256)S(1)}, u32[]{:S(2)}) copy-start(f32[192]{0:T(256)S(1)} %negate_power_fusion) | copy-start | bytes 2308
  35.2 34.2 %copy-start.114 = (f32[768]{0:T(1024)}, f32[768]{0:T(1024)S(1)}, u32[]{:S(2)}) copy-start(f32[768]{0:T(1024)S(1)} %get-tuple-element.62) | copy-start | bytes 9220
  35.2 109.4 %copy-start.116 = (f32[768]{0:T(1024)}, f32[768]{0:T(1024)S(1)}, u32[]{:S(2)}) copy-start(f32[768]{0:T(1024)S(1)} %get-tuple-element.60) | copy-start | bytes 9220
  69.2 74.0 %copy-start.6 = (f32[128,768]{1,0:T(8,128)}, f32[128,768]{1,0:T(8,128)S(1)}, u32[]{:S(2)}) copy-start(f32[128,768]{1,0:T(8,128)S(1)} %get-tuple-element.130) | copy-start | bytes 1179652
  108.5 98.1 %reduce-scatter.27.cloned.1.call-start = ((), (), s32[]{:S(2)}) async-start(), calls=%async_computation.26 | async-start | bytes 1966080 | tf_op jit(solution)/shard_map/reduce_scatter | solution.py:22
  171.8 99.2 %reduce-scatter.39.cloned.1.call-start = ((), (), s32[]{:S(2)}) async-start(), calls=%async_computation.32 | async-start | bytes 3932160 | tf_op jit(solution)/shard_map/reduce_scatter | solution.py:22
  185.7 101.3 %all-gather.9.cloned.1.call-start = ((), (), s32[]{:S(2)}) async-start(), calls=%async_computation.34 | async-start | bytes 7962624 | tf_op jit(solution)/shard_map/all_gather | solution.py:271
  212.3 16.6 %all-to-all-start = ((bf16[128,4,192]{0,2,1:T(8,128)(2,1)}), bf16[128,4,192]{0,2,1:T(8,128)(2,1)}, u32[]{:S(2)}, u32[]{:S(2)}) async-start(bf16[128,4,192]{0,2,1:T(8,128)(2,1)} %bitcast.441), calls=%async_computation.3 | async-start | bytes 393216 | tf_op jit(solution)/shard_map/all_to_all | solution.py:313
  216.3 104.7 %reduce-scatter.29.cloned.1.call-start = ((), (), s32[]{:S(2)}) async-start(), calls=%async_computation.27 | async-start | bytes 1474560 | tf_op jit(solution)/shard_map/reduce_scatter | solution.py:22
  231.4 127.9 %all-gather.7.cloned.1.call-start = ((), (), s32[]{:S(2)}) async-start(), calls=%async_computation.33 | async-start | bytes 1966080 | tf_op jit(solution)/shard_map/all_gather | solution.py:18
  232.9 266.4 %copy-start.118 = (f32[384]{0:T(512)}, f32[384]{0:T(512)S(1)}, u32[]{:S(2)}) copy-start(f32[384]{0:T(512)S(1)} %get-tuple-element.51) | copy-start | bytes 4612
  274.6 105.8 %reduce-scatter.31.cloned.1.call-start = ((), (), s32[]{:S(2)}) async-start(), calls=%async_computation.28 | async-start | bytes 1474560 | tf_op jit(solution)/shard_map/reduce_scatter | solution.py:22
  287.0 34.0 %copy-start.186 = (f32[192]{0:T(256)S(1)}, f32[192]{0:T(256)}, u32[]{:S(2)}) copy-start(f32[192]{0:T(256)} %compare_convert_fusion) | copy-start | bytes 2308
  353.0 94.1 %reduce-scatter.41.cloned.1.call-start = ((), (), s32[]{:S(2)}) async-start(), calls=%async_computation.35 | async-start | bytes 3932160 | tf_op jit(solution)/shard_map/reduce_scatter | solution.py:22
  375.6 122.3 %reduce-scatter.33.cloned.1.call-start = ((), (), s32[]{:S(2)}) async-start(), calls=%async_computation.29 | async-start | bytes 1474560 | tf_op jit(solution)/shard_map/reduce_scatter | solution.py:22
  411.4 126.7 %all-gather.11.cloned.1.call-start = ((), (), s32[]{:S(2)}) async-start(), calls=%async_computation.36 | async-start | bytes 1966080 | tf_op jit(solution)/shard_map/all_gather | solution.py:18
  450.6 107.8 %reduce-scatter.35.cloned.1.call-start = ((), (), s32[]{:S(2)}) async-start(), calls=%async_computation.30 | async-start | bytes 1474560 | tf_op jit(solution)/shard_map/reduce_scatter | solution.py:22
  531.1 94.2 %reduce-scatter.43.cloned.1.call-start = ((), (), s32[]{:S(2)}) async-start(), calls=%async_computation.37 | async-start | bytes 3932160 | tf_op jit(solution)/shard_map/reduce_scatter | solution.py:22
  550.5 114.1 %reduce-scatter.37.cloned.1.call-start = ((), (), s32[]{:S(2)}) async-start(), calls=%async_computation.31 | async-start | bytes 1474560 | tf_op jit(solution)/shard_map/reduce_scatter | solution.py:22
  630.7 26.9 %all-to-all-start.1 = ((bf16[256,4,192]{0,2,1:T(8,128)(2,1)}), bf16[256,4,192]{0,2,1:T(8,128)(2,1)}, u32[]{:S(2)}, u32[]{:S(2)}) async-start(bf16[256,4,192]{0,2,1:T(8,128)(2,1)} %bitcast.427), calls=%async_computation.12 | async-start | bytes 786432 | tf_op jit(solution)/shard_map/all_to_all | solution.py:316
  634.8 80.3 %reduce-scatter.45.cloned.1.call-start = ((), (), s32[]{:S(2)}) async-start(), calls=%async_computation.38 | async-start | bytes 1474560 | tf_op jit(solution)/shard_map/reduce_scatter | solution.py:22
  685.9 82.6 %reduce-scatter.47.cloned.1.call-start = ((), (), s32[]{:S(2)}) async-start(), calls=%async_computation.39 | async-start | bytes 1474560 | tf_op jit(solution)/shard_map/reduce_scatter | solution.py:22
  740.9 93.8 %reduce-scatter.49.cloned.1.call-start = ((), (), s32[]{:S(2)}) async-start(), calls=%async_computation.40 | async-start | bytes 1474560 | tf_op jit(solution)/shard_map/reduce_scatter | solution.py:22
  804.4 32.3 %copy-start.157 = (f32[192]{0:T(256)S(1)}, f32[192]{0:T(256)}, u32[]{:S(2)}) copy-start(f32[192]{0:T(256)} %copy-done.156) | copy-start | bytes 2308
  807.1 81.9 %reduce-scatter.51.cloned.1.call-start = ((), (), s32[]{:S(2)}) async-start(), calls=%async_computation.41 | async-start | bytes 1474560 | tf_op jit(solution)/shard_map/reduce_scatter | solution.py:22
  858.9 32.0 %copy-start.155 = (f32[192]{0:T(256)S(1)}, f32[192]{0:T(256)}, u32[]{:S(2)}) copy-start(f32[192]{0:T(256)} %copy-done.154) | copy-start | bytes 2308
  861.4 93.0 %reduce-scatter.53.cloned.1.call-start = ((), (), s32[]{:S(2)}) async-start(), calls=%async_computation.42 | async-start | bytes 1474560 | tf_op jit(solution)/shard_map/reduce_scatter | solution.py:22
  924.0 32.2 %copy-start.153 = (f32[192]{0:T(256)S(1)}, f32[192]{0:T(256)}, u32[]{:S(2)}) copy-start(f32[192]{0:T(256)} %copy-done.152) | copy-start | bytes 2308
  926.7 30.8 %copy-start.187 = (f32[192]{0:T(256)S(1)}, f32[192]{0:T(256)}, u32[]{:S(2)}) copy-start(f32[192]{0:T(256)} %compare_convert_fusion) | copy-start | bytes 2308
  926.7 124.6 %reduce-scatter.55.cloned.1.call-start = ((), (), s32[]{:S(2)}) async-start(), calls=%async_computation.43 | async-start | bytes 1966080 | tf_op jit(solution)/shard_map/reduce_scatter | solution.py:22
  1015.8 122.4 %reduce-scatter.59.cloned.1.call-start = ((), (), s32[]{:S(2)}) async-start(), calls=%async_computation.45 | async-start | bytes 1966080 | tf_op jit(solution)/shard_map/reduce_scatter | solution.py:22
  1085.6 136.1 %reduce-scatter.61.cloned.1.call-start = ((), (), s32[]{:S(2)}) async-start(), calls=%async_computation.46 | async-start | bytes 884736
  1159.9 139.7 %reduce-scatter.57.cloned.1.call-start = ((), (), s32[]{:S(2)}) async-start(), calls=%async_computation.44 | async-start | bytes 15925248 | tf_op jit(solution)/shard_map/reduce_scatter | solution.py:446
  1179.1 41.3 %copy-start.113 = (f32[11,384]{1,0:T(8,128)S(1)}, f32[11,384]{1,0:T(8,128)}, u32[]{:S(2)}) copy-start(f32[11,384]{1,0:T(8,128)} %param.38) | copy-start | bytes 50692
  1179.1 41.3 %copy-start.137 = (f32[11,384]{1,0:T(8,128)S(1)}, f32[11,384]{1,0:T(8,128)}, u32[]{:S(2)}) copy-start(f32[11,384]{1,0:T(8,128)} %param.39) | copy-start | bytes 50692
  1179.2 41.3 %copy-start.138 = (f32[11,384]{1,0:T(8,128)S(1)}, f32[11,384]{1,0:T(8,128)}, u32[]{:S(2)}) copy-start(f32[11,384]{1,0:T(8,128)} %param.40) | copy-start | bytes 50692
  1179.2 41.9 %copy-start.109 = (f32[7,768]{1,0:T(8,128)S(1)}, f32[7,768]{1,0:T(8,128)}, u32[]{:S(2)}) copy-start(f32[7,768]{1,0:T(8,128)} %param.35) | copy-start | bytes 64516
  1179.2 41.9 %copy-start.111 = (f32[7,768]{1,0:T(8,128)S(1)}, f32[7,768]{1,0:T(8,128)}, u32[]{:S(2)}) copy-start(f32[7,768]{1,0:T(8,128)} %param.41) | copy-start | bytes 64516
  1179.2 41.9 %copy-start.135 = (f32[7,768]{1,0:T(8,128)S(1)}, f32[7,768]{1,0:T(8,128)}, u32[]{:S(2)}) copy-start(f32[7,768]{1,0:T(8,128)} %param.36) | copy-start | bytes 64516
  1179.2 41.9 %copy-start.136 = (f32[7,768]{1,0:T(8,128)S(1)}, f32[7,768]{1,0:T(8,128)}, u32[]{:S(2)}) copy-start(f32[7,768]{1,0:T(8,128)} %param.37) | copy-start | bytes 64516
  1179.2 43.5 %copy-start.104 = (f32[192,96]{1,0:T(8,128)S(1)}, f32[192,96]{1,0:T(8,128)}, u32[]{:S(2)}) copy-start(f32[192,96]{1,0:T(8,128)} %param.31) | copy-start | bytes 221188
  1179.2 43.5 %copy-start.105 = (f32[192,96]{1,0:T(8,128)S(1)}, f32[192,96]{1,0:T(8,128)}, u32[]{:S(2)}) copy-start(f32[192,96]{1,0:T(8,128)} %param.34) | copy-start | bytes 221188
  1179.2 43.5 %copy-start.106 = (f32[192,96]{1,0:T(8,128)S(1)}, f32[192,96]{1,0:T(8,128)}, u32[]{:S(2)}) copy-start(f32[192,96]{1,0:T(8,128)} %param.32) | copy-start | bytes 221188
  1179.3 43.5 %copy-start.107 = (f32[192,96]{1,0:T(8,128)S(1)}, f32[192,96]{1,0:T(8,128)}, u32[]{:S(2)}) copy-start(f32[192,96]{1,0:T(8,128)} %param.33) | copy-start | bytes 221188
  (179 other events, 1440.5 us)
Sparse Core Ops, SparseCore 0:
  32.3 35.5 reduce-scatter.22
  108.6 34.4 reduce-scatter.24
  172.0 34.5 reduce-scatter.26
  208.7 62.3 reduce-scatter.38
  273.8 47.1 reduce-scatter.28
  353.1 27.2 reduce-scatter.30
  382.7 64.3 reduce-scatter.40
  450.0 47.8 reduce-scatter.32
  531.2 27.1 reduce-scatter.34
  560.5 64.7 reduce-scatter.42
  628.2 36.2 reduce-scatter.36
  1015.9 35.3 reduce-scatter.54
Sparse Core Ops, SparseCore 1:
  35.2 48.9 all-gather.4
  188.6 47.0 all-gather.8
  274.7 53.4 all-gather.6
  450.7 54.2 all-gather.10
  686.0 29.1 reduce-scatter.44
  741.0 27.5 reduce-scatter.46
  807.2 27.4 reduce-scatter.48
  861.5 27.4 reduce-scatter.50
  926.8 27.5 reduce-scatter.52
  1085.7 34.5 reduce-scatter.58
  1160.0 34.8 reduce-scatter.60
  1199.0 100.5 reduce-scatter.56
where the time goes:
time: 1340 us; the launch traced here: 1330 us
  waiting for transfers between devices  539 us (40%)
  blocking collectives  331 us (25%)
  local copies, waits for them, and re-layouts  183 us (14%)
  matrix products  147 us (11%)
  other arithmetic  88 us (7%)
  starting transfers between devices  22.2 us (2%)
  between operations  19.7 us (1%)
    reduce_scatter x18, waiting for transfers between devices, sum_rows(): return lax.psum_scatter(values, 'tensor', scatter_dimension=0, tiled=True)  432 us
    all_gather x15, blocking collectives, gather_rows(): return lax.all_gather(values, 'tensor', axis=0, tiled=True)  261 us
    reduce_scatter x1, waiting for transfers between devices, shards(): lax.psum_scatter(padded_grads[slot_of], 'dp', scatter_dimension=0, tiled=...  76 us
    unnamed x420, local copies, waits for them, and re-layouts  50.4 us
    psum x1, blocking collectives, shards(): lax.psum((enc_grad, pred_grad, loss_part), ('dp', 'tensor'))  39.5 us
  transfers between devices with their start and end apart: 26, of which 19 were waited for; matrix products, arithmetic and copies ran while one was open for 17% of the time, Pallas kernels for 0%

commit v1 on v0

v1 whole, which is shorter than its diff:
```python
import math

import jax
import jax.numpy as jnp
from jax import lax
from jax.sharding import PartitionSpec as P

HD = 64
PHD = 32
SIDE = 16
STEP = 10

AXES = ("dp", "tensor")
exact = lax.Precision.HIGHEST
f32 = jnp.float32
bf16 = jnp.bfloat16


def dot32(form, first, second):
    return jnp.einsum(form, first, second, preferred_element_type=f32)


def gelu_exact(values):
    return jax.nn.gelu(values, approximate=False)


def layer_norm(values, gain_row, shift_row):
    centre = values - jnp.mean(values, -1, keepdims=True)
    return (
        centre * lax.rsqrt(jnp.mean(centre * centre, -1, keepdims=True) + 1e-06) * gain_row
        + shift_row
    )


def norm_backward(grad, values, gain_row):
    centre = values - jnp.mean(values, -1, keepdims=True)
    scale = lax.rsqrt(jnp.mean(centre * centre, -1, keepdims=True) + 1e-06)
    unit = centre * scale
    weighted = grad * gain_row
    inner = (
        weighted
        - jnp.mean(weighted, -1, keepdims=True)
        - unit * jnp.mean(weighted * unit, -1, keepdims=True)
    )
    return (inner * scale, jnp.sum(grad * unit, 0), jnp.sum(grad, 0))


def sincos(cell_index, columns):
    quarter = columns // 4
    frequency = 1.0 / 10000.0 ** (jnp.arange(quarter).astype(f32) / quarter)
    col_angle = (cell_index % SIDE).astype(f32)[..., None] * frequency
    row_angle = (cell_index // SIDE).astype(f32)[..., None] * frequency
    return jnp.concatenate(
        [jnp.sin(col_angle), jnp.cos(col_angle), jnp.sin(row_angle), jnp.cos(row_angle)], -1
    )


def heads(rows, count, length, head_size):
    groups = rows.shape[0]
    columns = rows.shape[2] // 3
    shaped = rows.reshape(groups, count, length, 3, columns // head_size, head_size)
    shaped = shaped.transpose(3, 0, 1, 4, 2, 5)
    return (shaped[0], shaped[1], shaped[2])


def flat(pieces):
    groups, count, head_count, length, head_size = pieces.shape
    return pieces.transpose(0, 1, 3, 2, 4).reshape(groups, count * length, head_count * head_size)


def attend_forward(resid, attn_w, gain_row, shift_row, head_size, count, bias):
    normed = layer_norm(resid, gain_row, shift_row).astype(bf16)
    columns = attn_w.shape[2] // 4
    length = resid.shape[0] // count
    rows = dot32("nd,tdc->tnc", normed, attn_w[:, :, : 3 * columns]).astype(bf16)
    queries, keys_all, values_all = heads(rows, count, length, head_size)
    scores = dot32("tghqe,tghke->tghqk", queries, keys_all) / math.sqrt(head_size) + bias
    expo = jnp.exp(scores - jnp.max(scores, -1, keepdims=True))
    soft = expo / jnp.sum(expo, -1, keepdims=True)
    attended = flat(dot32("tghqk,tghke->tghqe", soft.astype(bf16), values_all).astype(bf16))
    mixed = dot32("tnc,tdc->nd", attended, attn_w[:, :, 3 * columns :])
    return (resid + mixed, (normed, queries, keys_all, values_all, soft, attended))


def attend_backward(grad_out, resid, attn_w, gain_row, kept, head_size, count):
    normed, queries, keys_all, values_all, soft, attended = kept
    columns = attn_w.shape[2] // 4
    root = math.sqrt(head_size)
    low = grad_out.astype(bf16)
    grad_out_w = dot32("nd,tnc->tdc", low, attended)
    grad_att = dot32("nd,tdc->tnc", low, attn_w[:, :, 3 * columns :]).astype(bf16)
    groups, _, head_count, length, _ = queries.shape
    grad_heads = grad_att.reshape(groups, count, length, head_count, head_size).transpose(
        0, 1, 3, 2, 4
    )
    grad_values = dot32("tghqk,tghqe->tghke", soft.astype(bf16), grad_heads).astype(bf16)
    grad_soft = dot32("tghqe,tghke->tghqk", grad_heads, values_all)
    grad_scores = (soft * (grad_soft - jnp.sum(grad_soft * soft, -1, keepdims=True))).astype(bf16)
    grad_queries = (dot32("tghqk,tghke->tghqe", grad_scores, keys_all) / root).astype(bf16)
    grad_keys = (dot32("tghqk,tghqe->tghke", grad_scores, queries) / root).astype(bf16)
    grad_rows = jnp.concatenate([flat(grad_queries), flat(grad_keys), flat(grad_values)], 2)
    grad_in_w = dot32("nd,tnc->tdc", normed, grad_rows)
    grad_normed = dot32("tnc,tdc->nd", grad_rows, attn_w[:, :, : 3 * columns])
    grad_resid, grad_gain, grad_shift = norm_backward(grad_normed, resid, gain_row)
    return (
        grad_out + grad_resid,
        jnp.concatenate([grad_in_w, grad_out_w], 2),
        grad_gain,
        grad_shift,
    )


def feed_forward(resid, up_w, down_t, gain_row, shift_row):
    normed = layer_norm(resid, gain_row, shift_row).astype(bf16)
    hidden = dot32("nd,tdc->tnc", normed, up_w)
    active = gelu_exact(hidden).astype(bf16)
    return (resid + dot32("tnc,tdc->nd", active, down_t), (normed, hidden))


def feed_backward(grad_out, resid, up_w, down_t, gain_row, kept):
    normed, hidden = kept
    low = grad_out.astype(bf16)
    active, gelu_back = jax.vjp(gelu_exact, hidden)
    grad_down = dot32("nd,tnc->tdc", low, active.astype(bf16))
    grad_hidden = gelu_back(dot32("nd,tdc->tnc", low, down_t))[0].astype(bf16)
    grad_up = dot32("nd,tnc->tdc", normed, grad_hidden)
    grad_normed = dot32("tnc,tdc->nd", grad_hidden, up_w)
    grad_resid, grad_gain, grad_shift = norm_backward(grad_normed, resid, gain_row)
    return (grad_out + grad_resid, grad_up, grad_down, grad_gain, grad_shift)


def adamw(master, moment, second, gradient, step_rate, weight_decay):
    moment = 0.9 * moment + 0.1 * gradient
    second = 0.999 * second + 0.001 * gradient * gradient
    unbiased_first = moment / (1.0 - 0.9**STEP)
    unbiased_second = second / (1.0 - 0.999**STEP)
    return (
        master
        - step_rate
        * (unbiased_first / (jnp.sqrt(unbiased_second) + 1e-08) + weight_decay * master),
        moment,
        second,
    )


class Routes:
    def __init__(self, nd, nt):
        self.nd, self.nt, self.half = nd, nt, nt // 2
        self.low_bits = [1 << s for s in range(1, nd.bit_length() - 1)]
        self.stages = len(self.low_bits)

    def order(self, core):
        return self.low_bits if core == 0 else self.low_bits[::-1]

    def pairs(self, target, keep):
        found = []
        for d in range(self.nd):
            for z in range(self.nt):
                if keep(d, z):
                    d2, z2 = target(d, z)
                    found.append((d * self.nt + z, d2 * self.nt + z2))
        return found

    def stage(self, number, values, role):
        def target(d, z):
            if number == self.stages:
                return d ^ 1, z
            return d ^ self.order(d & 1)[number], z

        return lax.ppermute(
            values,
            AXES,
            self.pairs(target, lambda d, z: role is None or z // self.half == role),
        )

    def across(self, r, values, from_role=None, to_role=None):
        def keep(d, z):
            return (from_role is None or z // self.half == from_role) and (
                to_role is None or (z ^ r) // self.half == to_role
            )

        return lax.ppermute(values, AXES, self.pairs(lambda d, z: (d, z ^ r), keep))

    def holders(self, d):
        place = jnp.arange(self.nd, dtype=jnp.int32)
        held = d ^ (place >> self.stages)
        core = held & 1
        for s in range(self.stages):
            bit = (place >> s) & 1
            held = held ^ (bit * jnp.where(core == 0, self.order(0)[s], self.order(1)[s]))
        return held

    def spread(self, stack, role):
        for number in range(self.stages + 1):
            stack = jnp.concatenate([stack, self.stage(number, stack, role)], 1)
        return stack

    def reduce(self, grads, role, is_role):
        current = grads
        for number in reversed(range(self.stages + 1)):
            middle = current.shape[1] // 2
            got = self.stage(number, current[:, middle:].astype(bf16), role)
            current = current[:, :middle].astype(f32) + got.astype(f32)
        total = jnp.where(is_role, current[0], 0.0)
        for r in range(1, self.nt):
            got = self.across(r, current[r].astype(bf16), from_role=role)
            total = total + got.astype(f32)
        return total

    def total(self, values):
        for bit in [1] + self.low_bits:
            values = values + lax.ppermute(
                values, AXES, self.pairs(lambda d, z, b=bit: (d ^ b, z), lambda d, z: True)
            )
        r = 1
        while r < self.nt:
            values = values + self.across(r, values)
            r *= 2
        return values


def shards(
    patches,
    ctx_idx,
    tgt_idx,
    owner,
    weights,
    stats_left,
    stats_right,
    root_left,
    root_right,
    teacher_slot_blocks,
    embed,
    embed_m,
    embed_v,
    teacher_embed,
    enc_vectors,
    enc_m,
    enc_v,
    pred_vectors,
    pred_m,
    pred_v,
    teacher_vectors,
):
    nt = lax.axis_size("tensor")
    nd = lax.axis_size("dp")
    routes = Routes(nd, nt)
    half = nt // 2
    d = lax.axis_index("dp")
    z = lax.axis_index("tensor")
    role = z // half
    student_role = role == 0
    images, npatches, pix_part = patches.shape
    slots = weights.shape[1]
    edge = weights.shape[-1]
    slot_count = slots * nd
    block_count = owner.shape[0]
    width = enc_vectors.shape[1]
    narrow = pred_vectors.shape[1]
    players = (pred_vectors.shape[0] - 3) // 4
    side = width // edge
    per_mat = side * side
    teach_count = 3 * per_mat
    quarter = width // nt
    context_len = ctx_idx.shape[1]
    target_len = tgt_idx.shape[1]
    seq_len = context_len + target_len
    share = images // half
    rows_part = edge // nd

    both = jnp.stack([weights[0], teacher_slot_blocks[0]]).astype(bf16)
    both = both.reshape(2, slots, nd, rows_part, edge)
    both = lax.all_to_all(both, "dp", split_axis=2, concat_axis=0, tiled=False)
    by_slot = both.transpose(1, 0, 2, 3, 4).reshape(2, slot_count, rows_part, edge)
    mine = by_slot[0][owner]
    teach = by_slot[1][owner[:teach_count]]

    chunk = rows_part
    wide_t = jnp.stack([embed, teacher_embed]).astype(bf16).transpose(0, 2, 1)
    high = d // (nd // 2)
    first = lax.dynamic_slice_in_dim(wide_t, high * chunk, chunk, 1)
    second = lax.dynamic_slice_in_dim(wide_t, (1 - high) * chunk, chunk, 1)

    def swap_pairs(flip, inverse):
        found = []
        for a in range(nd):
            h = a // (nd // 2)
            b = 2 * (a % (nd // 2)) + (h if not flip else 1 - h)
            found.append((b, a) if inverse else (a, b))
        return found

    got_first = lax.ppermute(first, "dp", swap_pairs(False, False))
    got_second = lax.ppermute(second, "dp", swap_pairs(True, False))
    odd = d % 2
    low_half = jnp.where(odd == 0, got_first, got_second)
    high_half = jnp.where(odd == 0, got_second, got_first)
    emb_rows = jnp.concatenate([low_half, high_half], 1)

    def square(blocks, number):
        picked = blocks[number * per_mat : (number + 1) * per_mat]
        return (
            picked.reshape(side, side, rows_part, edge)
            .transpose(0, 2, 1, 3)
            .reshape(side * rows_part, side * edge)
        )

    def gather_encoder(of_student, of_teacher):
        own = jnp.where(student_role, of_student, of_teacher)
        other = jnp.where(student_role, of_teacher, of_student)
        parts = [own]
        for r in range(1, nt):
            parts.append(routes.across(r, own if r < half else other))
        return routes.spread(jnp.stack(parts), None)

    attn_emb = gather_encoder(
        jnp.concatenate([square(mine, 0), emb_rows[0]], 1),
        jnp.concatenate([square(teach, 0), emb_rows[1]], 1),
    )
    attn_w = attn_emb[:, :, :width]
    emb_t = attn_emb[:, :, width:]
    up_w = gather_encoder(square(mine, 1), square(teach, 1))
    down_t = gather_encoder(square(mine, 2), square(teach, 2))
    pred_own = mine[teach_count:].transpose(1, 0, 2).reshape(rows_part, -1)
    pred_parts = [pred_own]
    for r in range(1, nt):
        pred_parts.append(routes.across(r, pred_own, to_role=1))
    pred_all = routes.spread(jnp.stack(pred_parts), 1)

    def pred_mat(number):
        return pred_all[:, :, number * edge : (number + 1) * edge]

    holder = routes.holders(d)
    inside = jnp.arange(rows_part, dtype=jnp.int32)
    feat = (
        jnp.arange(side, dtype=jnp.int32)[None, :, None] * edge
        + holder[:, None, None] * rows_part
        + inside[None, None, :]
    ).reshape(-1)
    feat_p = (holder[:, None] * rows_part + inside[None, :]).reshape(-1)
    one_hot = (feat[:, None] == jnp.arange(width)[None, :]).astype(f32)
    one_hot_p = (feat_p[:, None] == jnp.arange(narrow)[None, :]).astype(f32)

    def to_local(rows, hot):
        return jnp.einsum("nf,lf->nl", rows, hot, precision=exact, preferred_element_type=f32)

    def to_global(rows, hot):
        return jnp.einsum("nl,lf->nf", rows, hot, precision=exact, preferred_element_type=f32)

    vec = to_local(jnp.where(student_role, enc_vectors, teacher_vectors), one_hot)
    pvec = to_local(pred_vectors, one_hot_p)
    group_feat = (
        (z ^ jnp.arange(nt, dtype=jnp.int32))[:, None] * quarter
        + jnp.arange(quarter, dtype=jnp.int32)[None, :]
    ).reshape(-1)
    swap = (feat[:, None] == group_feat[None, :]).astype(bf16)

    part = z % half
    picked = jnp.take_along_axis(patches, ctx_idx[:, :, None], 1)

    def rows_for(target_z):
        where = (target_z % half) * share
        ctx_rows = lax.dynamic_slice_in_dim(picked, where, share, 0).reshape(-1, pix_part)
        all_rows = lax.dynamic_slice_in_dim(patches, where, share, 0).reshape(-1, pix_part)
        padded = jnp.pad(ctx_rows, ((0, all_rows.shape[0] - ctx_rows.shape[0]), (0, 0)))
        return jnp.where(target_z // half == 0, padded, all_rows)

    patch_rows = jnp.stack(
        [rows_for(z)] + [routes.across(r, rows_for(z ^ r)) for r in range(1, nt)]
    )
    my_ctx = lax.dynamic_slice_in_dim(ctx_idx, part * share, share, 0)
    my_tgt = lax.dynamic_slice_in_dim(tgt_idx, part * share, share, 0)
    full_rows = share * npatches
    ctx_rows = share * context_len
    ctx_places = jnp.pad(my_ctx.reshape(-1), (0, full_rows - ctx_rows))
    places = jnp.where(student_role, ctx_places, jnp.arange(full_rows) % npatches)
    table = to_local(sincos(jnp.arange(npatches), width), one_hot)
    table_p = to_local(sincos(jnp.arange(npatches), narrow), one_hot_p)
    count = full_rows // npatches
    span = jnp.arange(npatches) // context_len
    bias = jnp.where(student_role & (span[:, None] != span[None, :]), -1e30, 0.0).astype(f32)

    resid = dot32("rnp,rdp->nd", patch_rows, emb_t) + vec[6] + table[places]
    middle, kept_attn = attend_forward(resid, attn_w, vec[0], vec[1], HD, count, bias)
    output, kept_feed = feed_forward(middle, up_w, down_t, vec[2], vec[3])
    final = layer_norm(output, vec[4], vec[5])
    encoded = final[:ctx_rows].astype(bf16)
    target = layer_norm(final, 1.0, 0.0).astype(bf16).reshape(share, npatches, width)
    target = jnp.take_along_axis(target, my_tgt[:, :, None], 1).reshape(-1, width)
    target = jnp.dot(target, swap, preferred_element_type=f32)

    enc_feat = routes.across(half, encoded, from_role=0)
    enc_feat = jnp.dot(enc_feat, swap, preferred_element_type=f32).astype(bf16)
    enc_feat = enc_feat.reshape(ctx_rows, nt, quarter)
    inout = pred_mat(3 * players)
    in_w = inout[:, :, :quarter]
    out_w = inout[:, :, quarter:]
    projected = dot32("ntc,tpc->np", enc_feat, in_w).reshape(share, context_len, narrow)
    tokens = jnp.concatenate(
        [projected, jnp.broadcast_to(pvec[4 * players + 2], (share, target_len, narrow))], 1
    )
    tokens = (tokens + table_p[jnp.concatenate([my_ctx, my_tgt], 1)]).reshape(-1, narrow)
    zero = jnp.zeros((), f32)
    pred_kept = []
    for depth in range(players):
        mats = [pred_mat(3 * depth + i) for i in range(3)]
        rows = pvec[4 * depth : 4 * depth + 4]
        mid, kept_a = attend_forward(tokens, mats[0], rows[0], rows[1], PHD, share, zero)
        out, kept_f = feed_forward(mid, mats[1], mats[2], rows[2], rows[3])
        pred_kept.append((tokens, kept_a, mid, kept_f))
        tokens = out
    gain_last, shift_last = pvec[4 * players], pvec[4 * players + 1]
    normed = layer_norm(tokens, gain_last, shift_last).astype(bf16)
    normed_tgt = normed.reshape(share, seq_len, narrow)[:, context_len:].reshape(-1, narrow)
    predicted = dot32("np,tpc->ntc", normed_tgt, out_w).reshape(-1, width)
    denominator = images * nd * target_len * width
    gap = predicted - target
    magnitude = jnp.abs(gap)
    loss_part = jnp.sum(jnp.where(magnitude < 1.0, 0.5 * gap * gap, magnitude - 0.5)) / denominator
    grad_pred = (jnp.clip(gap, -1.0, 1.0) / denominator).astype(bf16).reshape(-1, nt, quarter)
    grad_out_w = dot32("np,ntc->tpc", normed_tgt, grad_pred)
    grad_tgt = dot32("ntc,tpc->np", grad_pred, out_w).reshape(share, target_len, narrow)
    grad_last = jnp.pad(grad_tgt, ((0, 0), (context_len, 0), (0, 0))).reshape(-1, narrow)
    grad_tokens, gain_g, shift_g = norm_backward(grad_last, tokens, gain_last)
    pred_vec_grads = {4 * players: gain_g, 4 * players + 1: shift_g}
    pred_mat_grads = {}
    for depth in reversed(range(players)):
        mats = [pred_mat(3 * depth + i) for i in range(3)]
        rows = pvec[4 * depth : 4 * depth + 4]
        before, kept_a, mid, kept_f = pred_kept[depth]
        grad_tokens, up_g, down_g, gain_two, shift_two = feed_backward(
            grad_tokens, mid, mats[1], mats[2], rows[2], kept_f
        )
        grad_tokens, attn_g, gain_one, shift_one = attend_backward(
            grad_tokens, before, mats[0], rows[0], kept_a, PHD, share
        )
        for i, value in enumerate([attn_g, up_g, down_g]):
            pred_mat_grads[3 * depth + i] = value
        for i, value in enumerate([gain_one, shift_one, gain_two, shift_two]):
            pred_vec_grads[4 * depth + i] = value
    grad_seq = grad_tokens.reshape(share, seq_len, narrow)
    pred_vec_grads[4 * players + 2] = jnp.sum(grad_seq[:, context_len:], (0, 1))
    grad_proj = grad_seq[:, :context_len].reshape(-1, narrow).astype(bf16)
    grad_in_w = dot32("np,ntc->tpc", grad_proj, enc_feat)
    pred_mat_grads[3 * players] = jnp.concatenate([grad_in_w, grad_out_w], 2)
    grad_enc = dot32("np,tpc->ntc", grad_proj, in_w).astype(bf16).reshape(-1, width)
    grad_enc = jnp.einsum("nf,lf->nl", grad_enc, swap, preferred_element_type=f32).astype(bf16)
    grad_enc = routes.across(half, grad_enc, from_role=1).astype(f32)
    pred_grads = jnp.concatenate([pred_mat_grads[i] for i in range(3 * players + 1)], 2)
    pred_sum = routes.reduce(pred_grads, 1, role == 1)

    def student_part(values, axis):
        return lax.slice_in_dim(values, 0, values.shape[axis] // count, axis=axis)

    grad_resid, gain_g, shift_g = norm_backward(grad_enc, output[:ctx_rows], vec[4])
    enc_vec_grads = {4: gain_g, 5: shift_g}
    grad_resid, up_g, down_g, gain_two, shift_two = feed_backward(
        grad_resid,
        middle[:ctx_rows],
        up_w,
        down_t,
        vec[2],
        (kept_feed[0][:ctx_rows], student_part(kept_feed[1], 1)),
    )
    kept = (kept_attn[0][:ctx_rows],) + tuple(student_part(v, 1) for v in kept_attn[1:])
    grad_resid, attn_g, gain_one, shift_one = attend_backward(
        grad_resid, resid[:ctx_rows], attn_w, vec[0], kept, HD, 1
    )
    for i, value in enumerate([gain_one, shift_one, gain_two, shift_two]):
        enc_vec_grads[i] = value
    enc_vec_grads[6] = jnp.sum(grad_resid, 0)
    emb_g = dot32("nd,rnp->rdp", grad_resid.astype(bf16), patch_rows[:, :ctx_rows])
    down_sum = routes.reduce(down_g, 0, student_role)
    up_sum = routes.reduce(up_g, 0, student_role)
    attn_emb_sum = routes.reduce(jnp.concatenate([attn_g, emb_g], 2), 0, student_role)
    attn_sum, emb_sum = attn_emb_sum[:, :width], attn_emb_sum[:, width:]

    enc_rows = to_global(jnp.stack([enc_vec_grads[i] for i in range(7)]), one_hot)
    pred_rows = to_global(
        jnp.stack([pred_vec_grads[i] for i in range(4 * players + 3)]), one_hot_p
    )
    enc_rows = jnp.where(student_role, enc_rows, 0.0)
    pred_rows = jnp.where(role == 1, pred_rows, 0.0)
    loss_row = jnp.where(role == 1, loss_part, 0.0)
    packed = jnp.concatenate([enc_rows.reshape(-1), pred_rows.reshape(-1), loss_row[None]])
    packed = jnp.pad(packed, (0, -packed.shape[0] % 1024)).reshape(-1, 128)
    packed = routes.total(packed).reshape(-1)
    enc_total = packed[: enc_rows.size].reshape(enc_rows.shape)
    pred_total = packed[enc_rows.size : enc_rows.size + pred_rows.size].reshape(pred_rows.shape)
    loss_total = packed[enc_rows.size + pred_rows.size]

    def unsquare(rows):
        return (
            rows.reshape(side, rows_part, side, edge)
            .transpose(0, 2, 1, 3)
            .reshape(per_mat, rows_part, edge)
        )

    by_block = jnp.concatenate(
        [
            unsquare(attn_sum),
            unsquare(up_sum),
            unsquare(down_sum),
            pred_sum.reshape(rows_part, -1, edge).transpose(1, 0, 2),
            jnp.zeros((1, rows_part, edge), f32),
        ],
        0,
    ).astype(bf16)
    slot_of = (
        jnp.full((slot_count,), block_count, jnp.int32)
        .at[owner]
        .set(jnp.arange(block_count, dtype=jnp.int32))
    )
    slot_rows = by_block[slot_of].reshape(nd, slots, rows_part, edge)
    slot_rows = lax.all_to_all(slot_rows, "dp", split_axis=0, concat_axis=1, tiled=False)
    low_grads = slot_rows.reshape(slots, edge, edge)
    slot_grads = low_grads.astype(f32)[None]

    emb_halves = emb_sum.reshape(side, chunk, pix_part)
    send_first = lax.dynamic_index_in_dim(emb_halves, odd, 0, keepdims=False)
    send_second = lax.dynamic_index_in_dim(emb_halves, 1 - odd, 0, keepdims=False)
    back_first = lax.ppermute(send_first, "dp", swap_pairs(False, True))
    back_second = lax.ppermute(send_second, "dp", swap_pairs(True, True))
    embed_grad = jnp.concatenate(
        [
            jnp.where(high == 0, back_first, back_second),
            jnp.where(high == 0, back_second, back_first),
        ],
        0,
    ).T

    new_left = 0.95 * stats_left + 0.05 * dot32("sij,skj->sik", low_grads, low_grads)[None]
    new_right = 0.95 * stats_right + 0.05 * dot32("sji,sjk->sik", low_grads, low_grads)[None]
    left_side = jnp.einsum(
        "tsij,tsjk->tsik", root_left, slot_grads, precision=exact, preferred_element_type=f32
    )
    direction = jnp.einsum(
        "tsij,tsjk->tsik", left_side, root_right, precision=exact, preferred_element_type=f32
    )
    direction = direction * lax.rsqrt(
        jnp.mean(direction * direction, axis=(2, 3), keepdims=True) + 1e-06
    )
    new_weights = weights - 0.05 * (direction + 0.05 * weights)
    new_teacher_blocks = 0.7 * teacher_slot_blocks + 0.3 * new_weights
    new_embed, new_embed_m, new_embed_v = adamw(embed, embed_m, embed_v, embed_grad, 0.05, 0.05)
    new_enc, new_enc_m, new_enc_v = adamw(enc_vectors, enc_m, enc_v, enc_total, 0.5, 0.0)
    new_pred, new_pred_m, new_pred_v = adamw(pred_vectors, pred_m, pred_v, pred_total, 0.5, 0.0)
    new_teacher_embed = 0.7 * teacher_embed + 0.3 * new_embed
    new_teacher_vectors = 0.7 * teacher_vectors + 0.3 * new_enc
    return (
        loss_total,
        slot_grads,
        new_weights,
        new_left,
        new_right,
        new_teacher_blocks,
        new_embed,
        new_embed_m,
        new_embed_v,
        new_teacher_embed,
        new_enc,
        new_enc_m,
        new_enc_v,
        new_pred,
        new_pred_m,
        new_pred_v,
        new_teacher_vectors,
    )


def solution(mesh):
    blocks = P("tensor", "dp", None, None)
    table = P("tensor", "dp")
    in_specs = (
        (P("dp", None, "tensor"), P("dp", None), P("dp", None), P())
        + (blocks,) * 6
        + (table,) * 4
        + (P(),) * 7
    )
    out_specs = (P(),) + (blocks,) * 5 + (table,) * 4 + (P(),) * 7
    return jax.shard_map(shards, mesh=mesh, in_specs=in_specs, out_specs=out_specs, check_vma=False)
```

time: 1340 us -> 951 us (0.71)
  waiting for transfers between devices: 539 us -> 81.3 us
  blocking collectives: 331 us -> 0 us
  other arithmetic: 88 us -> 209 us
  starting transfers between devices: 22.2 us -> 143 us
  local copies, waits for them, and re-layouts: 183 us -> 300 us
  matrix products: 147 us -> 194 us
  between operations: 19.7 us -> 5.71 us
    reduce_scatter x19 -> x0, waiting for transfers between devices: 508 us -> none  [the longest x18 432 us: sum_rows(): return lax.psum_scatter(values, 'tensor', scatter_dimension=0, tiled=True)]
    all_gather x17 -> x0, blocking collectives: 283 us -> none  [the longest x15 261 us: gather_rows(): return lax.all_gather(values, 'tensor', axis=0, tiled=True)]
    ppermute x0 -> x62, starting transfers between devices: none -> 134 us  [the longest x31 72.8 us: across(): return lax.ppermute(values, AXES, self.pairs(lambda d, z: (d, z ^ r), keep))]
    ppermute x0 -> x62, waiting for transfers between devices: none -> 72 us  [the longest x31 51.6 us: across(): return lax.ppermute(values, AXES, self.pairs(lambda d, z: (d, z ^ r), keep))]
    concatenate x2 -> x12, other arithmetic: 2.21 us -> 53.1 us  [the longest x10 48.8 us: spread(): stack = jnp.concatenate([stack, self.stage(number, stack, role)], 1)]
    another operation x5 -> x21, other arithmetic: 2.26 us -> 50.7 us  [the longest x4 23.8 us: gelu_exact(): return jax.nn.gelu(values, approximate=False)]
    psum x1 -> x0, blocking collectives: 39.5 us -> none  [shards(): lax.psum((enc_grad, pred_grad, loss_part), ('dp', 'tensor'))]
    dot_general x69, matrix products: 136 us -> 171 us  [the longest x60 159 us: dot32(): return jnp.einsum(form, first, second, preferred_element_type=f32)]
  transfers between devices with their start and end apart: 26 -> 64, of which waited for: 19 -> 17; matrix products, arithmetic and copies ran while one was open for 17% -> 39% of each run, Pallas kernels for 0% -> 0%
where the time goes in v1:
time: 951 us; the launch traced here: 933 us
  local copies, waits for them, and re-layouts  300 us (32%)
  other arithmetic  209 us (22%)
  matrix products  194 us (20%)
  starting transfers between devices  143 us (15%)
  waiting for transfers between devices  81.3 us (9%)
    dot_general x60, matrix products, dot32(): return jnp.einsum(form, first, second, preferred_element_type=f32)  159 us
    ppermute x31, starting transfers between devices, across(): return lax.ppermute(values, AXES, self.pairs(lambda d, z: (d, z ^ r), keep))  72.8 us
    unnamed x534, local copies, waits for them, and re-layouts  56.2 us
    ppermute x31, waiting for transfers between devices, across(): return lax.ppermute(values, AXES, self.pairs(lambda d, z: (d, z ^ r), keep))  51.6 us
    concatenate x10, other arithmetic, spread(): stack = jnp.concatenate([stack, self.stage(number, stack, role)], 1)  48.8 us
    ppermute x24, starting transfers between devices, stage(): lax.ppermute(values, AXES, self.pairs(target, lambda d, z: role is None o...  46.3 us
    ppermute x9, local copies, waits for them, and re-layouts, stage(): lax.ppermute(values, AXES, self.pairs(target, lambda d, z: role is None o...  30.7 us
    add x8, other arithmetic, reduce(): current = current[:, :middle].astype(f32) + got.astype(f32)  27.4 us
  transfers between devices with their start and end apart: 64, of which 17 were waited for; matrix products, arithmetic and copies ran while one was open for 39% of the time, Pallas kernels for 0%

profile of v1, /device:TPU:0, one launch (start us, length us, event | category | flops | bytes accessed | tf_op | source)
XLA Modules:
  0.0 933.4 jit_solution(10416031409629866906)
XLA Ops:
  12.4 4.5 all-to-all-start
  31.8 8.2 all-to-all-done
  53.9 5.0 collective-permute-done.4
  59.0 11.3 %collective-permute-done.3 = bf16[96,960]{0,1:T(8,128)(2,1)S(1)} collective-permute-done((bf16[96,960]{0,1:T(8,128)(2,1)}, bf16[96,960]{0,1:T(8,128)(2,1)S(1)}, u32[]{:S(2)}, u32[]{:S(2)}) %collective-permute-start.3) | collective-permute-done | bytes 184352 | tf_op jit(solution)/shard_map/ppermute | solution.py:182
  81.2 5.6 collective-permute-done.5
  99.0 5.1 collective-permute-start.26
  119.1 13.1 %collective-permute-start.19 = (bf16[96,768]{1,0:T(8,128)(2,1)}, bf16[96,768]{1,0:T(8,128)(2,1)}, u32[]{:S(2)}, u32[]{:S(2)}) collective-permute-start(bf16[96,768]{1,0:T(8,128)(2,1)} %bitcast.301), channel_id=1, source_target_pairs={{0,3},{1,2},{2,1},{3,0},{4,7},{5,6},{6,5},{7,4},{8,11},{9,10},{10,... | collective-permute-start | bytes 442376 | tf_op jit(solution)/shard_map/ppermute | solution.py:182
  141.6 3.8 collective-permute-start.13
  157.5 7.0 collective-permute-done.12
  174.8 4.5 pad_maximum_fusion.6
  222.4 3.8 copy.1152
  233.4 4.5 collective-permute-start.8
  240.7 4.3 pad_maximum_fusion.5
  245.0 4.5 copy.1153
  258.1 13.0 %pad_maximum_fusion.2 = bf16[4,768,960]{1,2,0:T(8,128)(2,1)S(1)} fusion(bf16[4,384,960]{1,2,0:T(8,128)(2,1)} %collective-permute-done.7, bf16[4,192,960]{1,2,0:T(8,128)(2,1)S(1)} %copy-done.13, bf16[4,96,960]{1,2,0:T(8,128)(2,1)S(1)} %copy-done.16, bf16[1,96,960]{1,2,0:T(8,128)(2,1)S(1)} %bitcast.861, bf16[1,96,960]{1,2,0:T(8,128)(2,1)S(1)} %bitcast.867, ...), kind=kLoop, calls=%fused_computation.38 | loop fusion | flops 41287680 | bytes 11796480 | tf_op jit(solution)/shard_map/concatenate | solution.py:195
  277.1 6.0 reshape.1064
  286.7 6.1 fusion.389
  309.1 5.4 convolution_bitcast_fusion.3
  314.5 20.9 %fusion.391 = (f32[512]{0:T(512)S(1)}, f32[512,768]{1,0:T(8,128)S(1)}) fusion(f32[512,768]{1,0:T(8,128)S(1)} %get-tuple-element.312, bf16[4,384,768]{2,1,0:T(8,128)(2,1)} %collective-permute-done.22, bf16[4,192,768]{2,1,0:T(8,128)(2,1)} %collective-permute-done.21, bf16[4,96,768]{2,1,0:T(8,128)(2,1)} %collective-permute-done.20, ...), kind=kOutput, calls=%fused_computation.814 | convolution fusion | flops 2551971328 | bytes 14157824 | tf_op jit(solution)/shard_map/tnc,tdc->nd/dot_general | solution.py:20
  350.8 8.6 fusion.26
  363.3 7.5 copy.1154
  380.4 8.9 pad_maximum_fusion.1
  394.1 4.3 reshape.1068
  400.9 5.1 fusion.392
  422.5 6.4 broadcast_subtract_fusion
  431.9 5.3 pad_maximum_fusion.13
  448.3 5.7 select_select_fusion
  465.8 4.1 reshape.1070
  472.5 5.8 fusion.395
  486.6 8.2 fusion.55
  510.2 5.8 fusion.53
  540.4 4.0 fusion.126
  564.6 4.6 fusion.58
  595.8 3.9 fusion.127
  644.2 18.9 %concatenate.173 = f32[4,384,2688]{2,1,0:T(8,128)} concatenate(f32[4,384,288]{2,1,0:T(8,128)} %convolution_bitcast_fusion.9, f32[4,384,96]{2,1,0:T(8,128)} %convolution_bitcast_fusion.17, f32[4,384,384]{2,1,0:T(8,128)} %convolution_bitcast_fusion.8, f32[4,384,384]{2,1,0:T(8,128)} %convolution_bitcast_fusion.7, f32[4,384,288]{2,1,0:T(8,128)} %convolution_bitcast_fusion.6, ...), dimensions={2} | concatenate | bytes 33030144 | tf_op jit(solution)/shard_map/concatenate | solution.py:448
  663.1 5.9 slice.896
  672.2 5.1 fusion.34
  677.4 4.1 multiply_reduce_fusion.10
  711.1 5.3 convolution_bitcast_fusion
  727.8 4.0 collective-permute-done.32
  731.8 4.2 collective-permute-start.33
  768.1 4.2 slice_add_fusion.1
  789.6 5.2 slice_add_fusion
  811.8 4.7 collective-permute-done.37
  875.2 11.9 %collective-permute-done.59 = bf16[48,2688]{1,0:T(8,128)(2,1)} collective-permute-done((bf16[48,2688]{1,0:T(8,128)(2,1)}, bf16[48,2688]{1,0:T(8,128)(2,1)}, u32[]{:S(2)}, u32[]{:S(2)}) %collective-permute-start.59) | collective-permute-done | bytes 258080 | tf_op jit(solution)/shard_map/ppermute | solution.py:182
  887.1 10.3 %collective-permute-done.58 = bf16[48,2688]{1,0:T(8,128)(2,1)} collective-permute-done((bf16[48,2688]{1,0:T(8,128)(2,1)}, bf16[48,2688]{1,0:T(8,128)(2,1)}, u32[]{:S(2)}, u32[]{:S(2)}) %collective-permute-start.58) | collective-permute-done | bytes 258080 | tf_op jit(solution)/shard_map/ppermute | solution.py:182
  900.6 4.3 all-to-all-start.1
  905.5 5.0 collective-permute-start.61
  (1040 shorter events, 609.8 us)
Async XLA Ops:
  4.1 26.0 %collective-permute-start = (bf16[2,48,192]{1,2,0:T(8,128)(2,1)}, bf16[2,48,192]{1,2,0:T(8,128)(2,1)}, u32[]{:S(2)}, u32[]{:S(2)}) collective-permute-start(bf16[2,48,192]{1,2,0:T(8,128)(2,1)} %get-tuple-element.291), channel_id=1, source_target_pairs={{0,0},{4,8},{8,16},{12,24},{16,4},{20,12},{24,20},{28,28},{1,1},{5... | collective-permute-start | bytes 110600 | tf_op jit(solution)/shard_map/ppermute | solution.py:292
  6.3 23.9 %collective-permute-start.1 = (bf16[2,48,192]{1,2,0:T(8,128)(2,1)}, bf16[2,48,192]{1,2,0:T(8,128)(2,1)}, u32[]{:S(2)}, u32[]{:S(2)}) collective-permute-start(bf16[2,48,192]{1,2,0:T(8,128)(2,1)} %get-tuple-element.292), channel_id=1, source_target_pairs={{0,4},{4,12},{8,20},{12,28},{16,0},{20,8},{24,16},{28,24},{1,5},{5... | collective-permute-start | bytes 110600 | tf_op jit(solution)/shard_map/ppermute | solution.py:293
  12.4 27.6 %all-to-all-start = ((bf16[1,2,3,8,48,384]{5,4,2,1,0,3:T(8,128)(2,1)}), bf16[1,2,3,8,48,384]{5,4,2,1,0,3:T(8,128)(2,1)}, u32[]{:S(2)}, u32[]{:S(2)}) async-start(bf16[1,2,3,8,48,384]{5,4,2,1,0,3:T(8,128)(2,1)} %copy.1104), calls=%async_computation | async-start | bytes 3538944 | tf_op jit(solution)/shard_map/all_to_all | solution.py:273
  51.7 18.6 %collective-permute-start.3 = (bf16[96,960]{0,1:T(8,128)(2,1)}, bf16[96,960]{0,1:T(8,128)(2,1)S(1)}, u32[]{:S(2)}, u32[]{:S(2)}) collective-permute-start(bf16[96,960]{0,1:T(8,128)(2,1)} %get-tuple-element.270), channel_id=1, source_target_pairs={{0,2},{1,3},{2,0},{3,1},{4,6},{5,7},{6,4},{7,5},{8,10},{9,11},{10,... | collective-permute-start | bytes 552968 | tf_op jit(solution)/shard_map/ppermute | solution.py:182
  51.7 18.6 %collective-permute-start.2 = (bf16[96,960]{0,1:T(8,128)(2,1)}, bf16[96,960]{0,1:T(8,128)(2,1)S(1)}, u32[]{:S(2)}, u32[]{:S(2)}) collective-permute-start(bf16[96,960]{0,1:T(8,128)(2,1)} %get-tuple-element.269), channel_id=1, source_target_pairs={{0,1},{1,0},{2,3},{3,2},{4,5},{5,4},{6,7},{7,6},{8,9},{9,8},{10,11... | collective-permute-start | bytes 552968 | tf_op jit(solution)/shard_map/ppermute | solution.py:182
  96.1 75.0 %collective-permute-start.6 = (bf16[4,192,960]{2,1,0:T(8,128)(2,1)}, bf16[4,192,960]{2,1,0:T(8,128)(2,1)}, u32[]{:S(2)}, u32[]{:S(2)}) collective-permute-start(bf16[4,192,960]{2,1,0:T(8,128)(2,1)} %copy.1116), channel_id=1, source_target_pairs={{0,16},{1,17},{2,18},{3,19},{4,12},{5,13},{6,14},{7,15},{8,24},{9,... | collective-permute-start | bytes 4423688 | tf_op jit(solution)/shard_map/ppermute | solution.py:170
  99.0 14.2 %collective-permute-start.26 = (bf16[48,2688]{1,0:T(8,128)(2,1)}, bf16[48,2688]{1,0:T(8,128)(2,1)}, u32[]{:S(2)}, u32[]{:S(2)}) collective-permute-start(bf16[48,2688]{1,0:T(8,128)(2,1)} %bitcast.265), channel_id=1, source_target_pairs={{0,3},{1,2},{4,7},{5,6},{8,11},{9,10},{12,15},{13,14},{16,19},{17,... | collective-permute-start | bytes 774152 | tf_op jit(solution)/shard_map/ppermute | solution.py:182
  115.8 63.5 %collective-permute-start.27 = (bf16[4,48,2688]{2,1,0:T(8,128)(2,1)}, bf16[4,48,2688]{2,1,0:T(8,128)(2,1)}, u32[]{:S(2)}, u32[]{:S(2)}) collective-permute-start(bf16[4,48,2688]{2,1,0:T(8,128)(2,1)} %pad_maximum_fusion.18), channel_id=1, source_target_pairs={{2,10},{3,11},{6,22},{7,23},{10,2},{11,3},{14,30},{15,31},{18,26},... | collective-permute-start | bytes 3096584 | tf_op jit(solution)/shard_map/ppermute | solution.py:170
  119.1 22.4 %collective-permute-start.19 = (bf16[96,768]{1,0:T(8,128)(2,1)}, bf16[96,768]{1,0:T(8,128)(2,1)}, u32[]{:S(2)}, u32[]{:S(2)}) collective-permute-start(bf16[96,768]{1,0:T(8,128)(2,1)} %bitcast.301), channel_id=1, source_target_pairs={{0,3},{1,2},{2,1},{3,0},{4,7},{5,6},{6,5},{7,4},{8,11},{9,10},{10,... | collective-permute-start | bytes 442376 | tf_op jit(solution)/shard_map/ppermute | solution.py:182
  132.3 13.1 %collective-permute-start.18 = (bf16[96,768]{1,0:T(8,128)(2,1)}, bf16[96,768]{1,0:T(8,128)(2,1)}, u32[]{:S(2)}, u32[]{:S(2)}) collective-permute-start(bf16[96,768]{1,0:T(8,128)(2,1)} %bitcast.301), channel_id=1, source_target_pairs={{0,2},{1,3},{2,0},{3,1},{4,6},{5,7},{6,4},{7,5},{8,10},{9,11},{10,... | collective-permute-start | bytes 442376 | tf_op jit(solution)/shard_map/ppermute | solution.py:182
  145.4 19.1 %collective-permute-start.12 = (bf16[96,768]{0,1:T(8,128)(2,1)}, bf16[96,768]{0,1:T(8,128)(2,1)}, u32[]{:S(2)}, u32[]{:S(2)}) collective-permute-start(bf16[96,768]{0,1:T(8,128)(2,1)} %copy.1134), channel_id=1, source_target_pairs={{0,2},{1,3},{2,0},{3,1},{4,6},{5,7},{6,4},{7,5},{8,10},{9,11},{10,... | collective-permute-start | bytes 442376 | tf_op jit(solution)/shard_map/ppermute | solution.py:182
  145.4 19.1 %collective-permute-start.11 = (bf16[96,768]{0,1:T(8,128)(2,1)}, bf16[96,768]{0,1:T(8,128)(2,1)}, u32[]{:S(2)}, u32[]{:S(2)}) collective-permute-start(bf16[96,768]{0,1:T(8,128)(2,1)} %copy.1132), channel_id=1, source_target_pairs={{0,1},{1,0},{2,3},{3,2},{4,5},{5,4},{6,7},{7,6},{8,9},{9,8},{10,11... | collective-permute-start | bytes 442376 | tf_op jit(solution)/shard_map/ppermute | solution.py:182
  153.8 95.8 %collective-permute-start.10 = (bf16[512,192]{0,1:T(8,128)(2,1)}, bf16[512,192]{0,1:T(8,128)(2,1)}, u32[]{:S(2)}, u32[]{:S(2)}) collective-permute-start(bf16[512,192]{0,1:T(8,128)(2,1)} %pad_select_fusion), channel_id=1, source_target_pairs={{0,3},{1,2},{2,1},{3,0},{4,7},{5,6},{6,5},{7,4},{8,11},{9,10},{10,... | collective-permute-start | bytes 589832 | tf_op jit(solution)/shard_map/ppermute | solution.py:182
  164.5 29.6 %collective-permute-start.20 = (bf16[4,96,768]{2,1,0:T(8,128)(2,1)}, bf16[4,96,768]{2,1,0:T(8,128)(2,1)}, u32[]{:S(2)}, u32[]{:S(2)}) collective-permute-start(bf16[4,96,768]{2,1,0:T(8,128)(2,1)} %pad_maximum_fusion.25), channel_id=1, source_target_pairs={{0,8},{1,9},{2,10},{3,11},{4,20},{5,21},{6,22},{7,23},{8,0},{9,1},... | collective-permute-start | bytes 1769480 | tf_op jit(solution)/shard_map/ppermute | solution.py:170
  169.1 15.2 %collective-permute-start.14 = (bf16[4,96,768]{2,1,0:T(8,128)(2,1)}, bf16[4,96,768]{2,1,0:T(8,128)(2,1)}, u32[]{:S(2)}, u32[]{:S(2)}) collective-permute-start(bf16[4,96,768]{2,1,0:T(8,128)(2,1)} %copy.1137), channel_id=1, source_target_pairs={{0,8},{1,9},{2,10},{3,11},{4,20},{5,21},{6,22},{7,23},{8,0},{9,1},... | collective-permute-start | bytes 1769480 | tf_op jit(solution)/shard_map/ppermute | solution.py:170
  179.3 73.4 %collective-permute-start.7 = (bf16[4,384,960]{1,2,0:T(8,128)(2,1)}, bf16[4,384,960]{1,2,0:T(8,128)(2,1)}, u32[]{:S(2)}, u32[]{:S(2)}) collective-permute-start(bf16[4,384,960]{1,2,0:T(8,128)(2,1)} %pad_maximum_fusion.6), channel_id=1, source_target_pairs={{0,4},{1,5},{2,6},{3,7},{4,0},{5,1},{6,2},{7,3},{8,12},{9,13},{10,... | collective-permute-start | bytes 8847368 | tf_op jit(solution)/shard_map/ppermute | solution.py:170
  182.3 58.4 %collective-permute-start.28 = (bf16[4,96,2688]{2,1,0:T(8,128)(2,1)}, bf16[4,96,2688]{2,1,0:T(8,128)(2,1)}, u32[]{:S(2)}, u32[]{:S(2)}) collective-permute-start(bf16[4,96,2688]{2,1,0:T(8,128)(2,1)} %pad_maximum_fusion.9), channel_id=1, source_target_pairs={{2,18},{3,19},{6,14},{7,15},{10,26},{11,27},{14,6},{15,7},{18,2},{... | collective-permute-start | bytes 6193160 | tf_op jit(solution)/shard_map/ppermute | solution.py:170
  192.2 34.1 %collective-permute-start.15 = (bf16[4,192,768]{2,1,0:T(8,128)(2,1)}, bf16[4,192,768]{2,1,0:T(8,128)(2,1)}, u32[]{:S(2)}, u32[]{:S(2)}) collective-permute-start(bf16[4,192,768]{2,1,0:T(8,128)(2,1)} %copy.1139), channel_id=1, source_target_pairs={{0,16},{1,17},{2,18},{3,19},{4,12},{5,13},{6,14},{7,15},{8,24},{9,... | collective-permute-start | bytes 3538952 | tf_op jit(solution)/shard_map/ppermute | solution.py:170
  196.4 37.0 %collective-permute-start.21 = (bf16[4,192,768]{2,1,0:T(8,128)(2,1)}, bf16[4,192,768]{2,1,0:T(8,128)(2,1)}, u32[]{:S(2)}, u32[]{:S(2)}) collective-permute-start(bf16[4,192,768]{2,1,0:T(8,128)(2,1)} %pad_maximum_fusion.16), channel_id=1, source_target_pairs={{0,16},{1,17},{2,18},{3,19},{4,12},{5,13},{6,14},{7,15},{8,24},{9,... | collective-permute-start | bytes 3538952 | tf_op jit(solution)/shard_map/ppermute | solution.py:170
  226.3 23.7 %collective-permute-start.9 = (bf16[512,192]{0,1:T(8,128)(2,1)}, bf16[512,192]{0,1:T(8,128)(2,1)}, u32[]{:S(2)}, u32[]{:S(2)}) collective-permute-start(bf16[512,192]{0,1:T(8,128)(2,1)} %pad_select_fusion.1), channel_id=1, source_target_pairs={{0,2},{1,3},{2,0},{3,1},{4,6},{5,7},{6,4},{7,5},{8,10},{9,11},{10,... | collective-permute-start | bytes 589832 | tf_op jit(solution)/shard_map/ppermute | solution.py:182
  233.4 19.2 %collective-permute-start.8 = (bf16[512,192]{0,1:T(8,128)(2,1)}, bf16[512,192]{0,1:T(8,128)(2,1)}, u32[]{:S(2)}, u32[]{:S(2)}) collective-permute-start(bf16[512,192]{0,1:T(8,128)(2,1)} %pad_select_fusion.2), channel_id=1, source_target_pairs={{0,1},{1,0},{2,3},{3,2},{4,5},{5,4},{6,7},{7,6},{8,9},{9,8},{10,11... | collective-permute-start | bytes 589832 | tf_op jit(solution)/shard_map/ppermute | solution.py:182
  240.7 73.8 %collective-permute-start.22 = (bf16[4,384,768]{2,1,0:T(8,128)(2,1)}, bf16[4,384,768]{2,1,0:T(8,128)(2,1)}, u32[]{:S(2)}, u32[]{:S(2)}) collective-permute-start(bf16[4,384,768]{2,1,0:T(8,128)(2,1)} %pad_maximum_fusion.8), channel_id=1, source_target_pairs={{0,4},{1,5},{2,6},{3,7},{4,0},{5,1},{6,2},{7,3},{8,12},{9,13},{10,... | collective-permute-start | bytes 7077896 | tf_op jit(solution)/shard_map/ppermute | solution.py:170
  249.5 58.1 %collective-permute-start.16 = (bf16[4,384,768]{1,2,0:T(8,128)(2,1)}, bf16[4,384,768]{1,2,0:T(8,128)(2,1)}, u32[]{:S(2)}, u32[]{:S(2)}) collective-permute-start(bf16[4,384,768]{1,2,0:T(8,128)(2,1)} %pad_maximum_fusion.7), channel_id=1, source_target_pairs={{0,4},{1,5},{2,6},{3,7},{4,0},{5,1},{6,2},{7,3},{8,12},{9,13},{10,... | collective-permute-start | bytes 7077896 | tf_op jit(solution)/shard_map/ppermute | solution.py:170
  250.0 113.3 %collective-permute-start.29 = (bf16[4,192,2688]{2,1,0:T(8,128)(2,1)}, bf16[4,192,2688]{2,1,0:T(8,128)(2,1)}, u32[]{:S(2)}, u32[]{:S(2)}) collective-permute-start(bf16[4,192,2688]{2,1,0:T(8,128)(2,1)} %pad_maximum_fusion.5), channel_id=1, source_target_pairs={{2,6},{3,7},{6,2},{7,3},{10,14},{11,15},{14,10},{15,11},{18,22},{1... | collective-permute-start | bytes 12386312 | tf_op jit(solution)/shard_map/ppermute | solution.py:170
  338.8 22.6 %collective-permute-start.23 = (bf16[256,768]{1,0:T(8,128)(2,1)}, bf16[256,768]{1,0:T(8,128)(2,1)}, u32[]{:S(2)}, u32[]{:S(2)}) collective-permute-start(bf16[256,768]{1,0:T(8,128)(2,1)} %slice.908), channel_id=1, source_target_pairs={{0,2},{1,3},{4,6},{5,7},{8,10},{9,11},{12,14},{13,15},{16,18},{17,... | collective-permute-start | bytes 1179656 | tf_op jit(solution)/shard_map/ppermute | solution.py:182
  635.9 35.7 %collective-permute-start.30 = (bf16[256,768]{1,0:T(8,128)(2,1)}, bf16[256,768]{1,0:T(8,128)(2,1)S(1)}, u32[]{:S(2)}, u32[]{:S(2)}) collective-permute-start(bf16[256,768]{1,0:T(8,128)(2,1)} %fusion.117), channel_id=1, source_target_pairs={{2,0},{3,1},{6,4},{7,5},{10,8},{11,9},{14,12},{15,13},{18,16},{19,... | collective-permute-start | bytes 1179656 | tf_op jit(solution)/shard_map/ppermute | solution.py:182
  669.0 120.5 %collective-permute-start.54 = (bf16[4,192,2688]{2,1,0:T(8,128)(2,1)}, bf16[4,192,2688]{2,1,0:T(8,128)(2,1)}, u32[]{:S(2)}, u32[]{:S(2)}) collective-permute-start(bf16[4,192,2688]{2,1,0:T(8,128)(2,1)} %slice.896), channel_id=1, source_target_pairs={{2,6},{3,7},{6,2},{7,3},{10,14},{11,15},{14,10},{15,11},{18,22},{1... | collective-permute-start | bytes 12386312 | tf_op jit(solution)/shard_map/ppermute | solution.py:170
  701.0 48.2 %collective-permute-start.42 = (bf16[4,384,768]{2,1,0:T(8,128)(2,1)}, bf16[4,384,768]{2,1,0:T(8,128)(2,1)}, u32[]{:S(2)}, u32[]{:S(2)}) collective-permute-start(bf16[4,384,768]{2,1,0:T(8,128)(2,1)} %slice.899), channel_id=1, source_target_pairs={{0,4},{1,5},{4,0},{5,1},{8,12},{9,13},{12,8},{13,9},{16,20},{17,21... | collective-permute-start | bytes 7077896 | tf_op jit(solution)/shard_map/ppermute | solution.py:170
  708.6 59.5 %collective-permute-start.36 = (bf16[4,384,960]{1,2,0:T(8,128)(2,1)}, bf16[4,384,960]{1,2,0:T(8,128)(2,1)}, u32[]{:S(2)}, u32[]{:S(2)}) collective-permute-start(bf16[4,384,960]{1,2,0:T(8,128)(2,1)} %slice.897), channel_id=1, source_target_pairs={{0,4},{1,5},{4,0},{5,1},{8,12},{9,13},{12,8},{13,9},{16,20},{17,21... | collective-permute-start | bytes 8847368 | tf_op jit(solution)/shard_map/ppermute | solution.py:170
  720.7 39.2 %collective-permute-start.48 = (bf16[4,384,768]{2,1,0:T(8,128)(2,1)}, bf16[4,384,768]{2,1,0:T(8,128)(2,1)}, u32[]{:S(2)}, u32[]{:S(2)}) collective-permute-start(bf16[4,384,768]{2,1,0:T(8,128)(2,1)} %slice.898), channel_id=1, source_target_pairs={{0,4},{1,5},{4,0},{5,1},{8,12},{9,13},{12,8},{13,9},{16,20},{17,21... | collective-permute-start | bytes 7077896 | tf_op jit(solution)/shard_map/ppermute | solution.py:170
  756.1 27.0 %collective-permute-start.43 = (bf16[4,192,768]{2,1,0:T(8,128)(2,1)}, bf16[4,192,768]{2,1,0:T(8,128)(2,1)}, u32[]{:S(2)}, u32[]{:S(2)}) collective-permute-start(bf16[4,192,768]{2,1,0:T(8,128)(2,1)} %slice.903), channel_id=1, source_target_pairs={{0,16},{1,17},{4,12},{5,13},{8,24},{9,25},{12,4},{13,5},{16,0},{17... | collective-permute-start | bytes 3538952 | tf_op jit(solution)/shard_map/ppermute | solution.py:170
  764.7 34.5 %collective-permute-start.49 = (bf16[4,192,768]{2,1,0:T(8,128)(2,1)}, bf16[4,192,768]{2,1,0:T(8,128)(2,1)}, u32[]{:S(2)}, u32[]{:S(2)}) collective-permute-start(bf16[4,192,768]{2,1,0:T(8,128)(2,1)} %slice.902), channel_id=1, source_target_pairs={{0,16},{1,17},{4,12},{5,13},{8,24},{9,25},{12,4},{13,5},{16,0},{17... | collective-permute-start | bytes 3538952 | tf_op jit(solution)/shard_map/ppermute | solution.py:170
  780.6 35.9 %collective-permute-start.37 = (bf16[4,192,960]{2,1,0:T(8,128)(2,1)}, bf16[4,192,960]{2,1,0:T(8,128)(2,1)S(1)}, u32[]{:S(2)}, u32[]{:S(2)}) collective-permute-start(bf16[4,192,960]{2,1,0:T(8,128)(2,1)} %copy.1210), channel_id=1, source_target_pairs={{0,16},{1,17},{4,12},{5,13},{8,24},{9,25},{12,4},{13,5},{16,0},{17... | collective-permute-start | bytes 4423688 | tf_op jit(solution)/shard_map/ppermute | solution.py:170
  786.2 18.7 %collective-permute-start.44 = (bf16[4,96,768]{2,1,0:T(8,128)(2,1)}, bf16[4,96,768]{2,1,0:T(8,128)(2,1)}, u32[]{:S(2)}, u32[]{:S(2)}) collective-permute-start(bf16[4,96,768]{2,1,0:T(8,128)(2,1)} %slice.907), channel_id=1, source_target_pairs={{0,8},{1,9},{4,20},{5,21},{8,0},{9,1},{12,28},{13,29},{16,24},{17,... | collective-permute-start | bytes 1769480 | tf_op jit(solution)/shard_map/ppermute | solution.py:170
  796.5 48.8 %collective-permute-start.55 = (bf16[4,96,2688]{2,1,0:T(8,128)(2,1)}, bf16[4,96,2688]{2,1,0:T(8,128)(2,1)}, u32[]{:S(2)}, u32[]{:S(2)}) collective-permute-start(bf16[4,96,2688]{2,1,0:T(8,128)(2,1)} %slice.900), channel_id=1, source_target_pairs={{2,18},{3,19},{6,14},{7,15},{10,26},{11,27},{14,6},{15,7},{18,2},{... | collective-permute-start | bytes 6193160 | tf_op jit(solution)/shard_map/ppermute | solution.py:170
  802.4 26.2 %collective-permute-start.50 = (bf16[4,96,768]{2,1,0:T(8,128)(2,1)}, bf16[4,96,768]{2,1,0:T(8,128)(2,1)}, u32[]{:S(2)}, u32[]{:S(2)}) collective-permute-start(bf16[4,96,768]{2,1,0:T(8,128)(2,1)} %slice.906), channel_id=1, source_target_pairs={{0,8},{1,9},{4,20},{5,21},{8,0},{9,1},{12,28},{13,29},{16,24},{17,... | collective-permute-start | bytes 1769480 | tf_op jit(solution)/shard_map/ppermute | solution.py:170
  807.9 27.5 %collective-permute-start.47 = (bf16[96,768]{1,0:T(8,128)(2,1)}, bf16[96,768]{1,0:T(8,128)(2,1)}, u32[]{:S(2)}, u32[]{:S(2)}) collective-permute-start(bf16[96,768]{1,0:T(8,128)(2,1)} %get-tuple-element.267), channel_id=1, source_target_pairs={{0,3},{1,2},{4,7},{5,6},{8,11},{9,10},{12,15},{13,14},{16,19},{17,... | collective-permute-start | bytes 442376 | tf_op jit(solution)/shard_map/ppermute | solution.py:182
  809.8 27.5 %collective-permute-start.46 = (bf16[96,768]{1,0:T(8,128)(2,1)}, bf16[96,768]{1,0:T(8,128)(2,1)}, u32[]{:S(2)}, u32[]{:S(2)}) collective-permute-start(bf16[96,768]{1,0:T(8,128)(2,1)} %get-tuple-element.268), channel_id=1, source_target_pairs={{0,2},{1,3},{4,6},{5,7},{8,10},{9,11},{12,14},{13,15},{16,18},{17,... | collective-permute-start | bytes 442376 | tf_op jit(solution)/shard_map/ppermute | solution.py:182
  816.5 22.8 %collective-permute-start.45 = (bf16[96,768]{1,0:T(8,128)(2,1)}, bf16[96,768]{1,0:T(8,128)(2,1)}, u32[]{:S(2)}, u32[]{:S(2)}) collective-permute-start(bf16[96,768]{1,0:T(8,128)(2,1)} %get-tuple-element.266), channel_id=1, source_target_pairs={{0,1},{1,0},{4,5},{5,4},{8,9},{9,8},{12,13},{13,12},{16,17},{17,16... | collective-permute-start | bytes 442376 | tf_op jit(solution)/shard_map/ppermute | solution.py:182
  828.6 15.0 %collective-permute-start.38 = (bf16[4,96,960]{2,1,0:T(8,128)(2,1)S(1)}, bf16[4,96,960]{2,1,0:T(8,128)(2,1)}, u32[]{:S(2)}, u32[]{:S(2)}) collective-permute-start(bf16[4,96,960]{2,1,0:T(8,128)(2,1)S(1)} %copy.1212), channel_id=1, source_target_pairs={{0,8},{1,9},{4,20},{5,21},{8,0},{9,1},{12,28},{13,29},{16,24},{17,... | collective-permute-start | bytes 2211848 | tf_op jit(solution)/shard_map/ppermute | solution.py:170
  835.4 19.7 %collective-permute-start.53 = (bf16[96,768]{1,0:T(8,128)(2,1)}, bf16[96,768]{1,0:T(8,128)(2,1)}, u32[]{:S(2)}, u32[]{:S(2)}) collective-permute-start(bf16[96,768]{1,0:T(8,128)(2,1)} %get-tuple-element.264), channel_id=1, source_target_pairs={{0,3},{1,2},{4,7},{5,6},{8,11},{9,10},{12,15},{13,14},{16,19},{17,... | collective-permute-start | bytes 442376 | tf_op jit(solution)/shard_map/ppermute | solution.py:182
  837.4 19.0 %collective-permute-start.52 = (bf16[96,768]{1,0:T(8,128)(2,1)}, bf16[96,768]{1,0:T(8,128)(2,1)}, u32[]{:S(2)}, u32[]{:S(2)}) collective-permute-start(bf16[96,768]{1,0:T(8,128)(2,1)} %get-tuple-element.265), channel_id=1, source_target_pairs={{0,2},{1,3},{4,6},{5,7},{8,10},{9,11},{12,14},{13,15},{16,18},{17,... | collective-permute-start | bytes 442376 | tf_op jit(solution)/shard_map/ppermute | solution.py:182
  839.3 20.6 %collective-permute-start.51 = (bf16[96,768]{1,0:T(8,128)(2,1)}, bf16[96,768]{1,0:T(8,128)(2,1)}, u32[]{:S(2)}, u32[]{:S(2)}) collective-permute-start(bf16[96,768]{1,0:T(8,128)(2,1)} %get-tuple-element.263), channel_id=1, source_target_pairs={{0,1},{1,0},{4,5},{5,4},{8,9},{9,8},{12,13},{13,12},{16,17},{17,16... | collective-permute-start | bytes 442376 | tf_op jit(solution)/shard_map/ppermute | solution.py:182
  849.8 16.9 %collective-permute-start.56 = (bf16[4,48,2688]{2,1,0:T(8,128)(2,1)}, bf16[4,48,2688]{2,1,0:T(8,128)(2,1)}, u32[]{:S(2)}, u32[]{:S(2)}) collective-permute-start(bf16[4,48,2688]{2,1,0:T(8,128)(2,1)} %slice.904), channel_id=1, source_target_pairs={{2,10},{3,11},{6,22},{7,23},{10,2},{11,3},{14,30},{15,31},{18,26},... | collective-permute-start | bytes 3096584 | tf_op jit(solution)/shard_map/ppermute | solution.py:170
  871.0 16.0 %collective-permute-start.59 = (bf16[48,2688]{1,0:T(8,128)(2,1)}, bf16[48,2688]{1,0:T(8,128)(2,1)}, u32[]{:S(2)}, u32[]{:S(2)}) collective-permute-start(bf16[48,2688]{1,0:T(8,128)(2,1)} %get-tuple-element.255), channel_id=1, source_target_pairs={{2,1},{3,0},{6,5},{7,4},{10,9},{11,8},{14,13},{15,12},{18,17},{19,... | collective-permute-start | bytes 774152 | tf_op jit(solution)/shard_map/ppermute | solution.py:182
  872.3 25.0 %collective-permute-start.58 = (bf16[48,2688]{1,0:T(8,128)(2,1)}, bf16[48,2688]{1,0:T(8,128)(2,1)}, u32[]{:S(2)}, u32[]{:S(2)}) collective-permute-start(bf16[48,2688]{1,0:T(8,128)(2,1)} %get-tuple-element.256), channel_id=1, source_target_pairs={{2,0},{3,1},{6,4},{7,5},{10,8},{11,9},{14,12},{15,13},{18,16},{19,... | collective-permute-start | bytes 774152 | tf_op jit(solution)/shard_map/ppermute | solution.py:182
  873.6 23.7 %collective-permute-start.57 = (bf16[48,2688]{1,0:T(8,128)(2,1)}, bf16[48,2688]{1,0:T(8,128)(2,1)}, u32[]{:S(2)}, u32[]{:S(2)}) collective-permute-start(bf16[48,2688]{1,0:T(8,128)(2,1)} %get-tuple-element.254), channel_id=1, source_target_pairs={{2,3},{3,2},{6,7},{7,6},{10,11},{11,10},{14,15},{15,14},{18,19},{1... | collective-permute-start | bytes 774152 | tf_op jit(solution)/shard_map/ppermute | solution.py:182
  900.6 17.9 %all-to-all-start.1 = ((bf16[8,3,1,48,384]{4,3,1,2,0:T(8,128)(2,1)}), bf16[8,3,1,48,384]{4,3,1,2,0:T(8,128)(2,1)S(1)}, u32[]{:S(2)}, u32[]{:S(2)}) async-start(bf16[8,3,1,48,384]{4,3,1,2,0:T(8,128)(2,1)} %bitcast.216), calls=%async_computation.1 | async-start | bytes 1769472 | tf_op jit(solution)/shard_map/all_to_all | solution.py:514
  (269 other events, 2927.8 us)

commit v2 on v1

v2 whole, which is shorter than its diff:
```python
import functools
import math

import jax
import jax.numpy as jnp
from jax import lax
from jax.experimental import pallas as pl
from jax.experimental.pallas import tpu as pltpu
from jax.sharding import PartitionSpec as P

HD = 64
PHD = 32
SIDE = 16
STEP = 10
KERNEL_BYTES = 60 * 1024 * 1024

AXES = ("dp", "tensor")
exact = lax.Precision.HIGHEST
f32 = jnp.float32
bf16 = jnp.bfloat16
VMEM = pltpu.VMEM


def nn(first, second):
    return lax.dot_general(first, second, (((1,), (0,)), ((), ())), preferred_element_type=f32)


def nt_(first, second):
    return lax.dot_general(first, second, (((1,), (1,)), ((), ())), preferred_element_type=f32)


def tn(first, second):
    return lax.dot_general(first, second, (((0,), (0,)), ((), ())), preferred_element_type=f32)


def norm_parts(values):
    centre = values - jnp.mean(values, -1, keepdims=True)
    scale = lax.rsqrt(jnp.mean(centre * centre, -1, keepdims=True) + 1e-06)
    return centre * scale, scale


def layer_norm(values, gain_row, shift_row):
    return norm_parts(values)[0] * gain_row + shift_row


def norm_backward(grad, values, gain_row):
    unit, scale = norm_parts(values)
    weighted = grad * gain_row
    inner = (
        weighted
        - jnp.mean(weighted, -1, keepdims=True)
        - unit * jnp.mean(weighted * unit, -1, keepdims=True)
    )
    return (
        inner * scale,
        jnp.sum(grad * unit, 0, keepdims=True),
        jnp.sum(grad, 0, keepdims=True),
    )


def gelu_parts(values):
    below = 0.5 * (1.0 + lax.erf(values * math.sqrt(0.5)))
    density = jnp.exp(-0.5 * values * values) * (1.0 / math.sqrt(2.0 * math.pi))
    return values * below, below + values * density


def softened(queries, keys, head_size, allowed):
    scores = nt_(queries, keys) * (1.0 / math.sqrt(head_size))
    if allowed is not None:
        scores = jnp.where(allowed, scores, -1e30)
    expo = jnp.exp(scores - jnp.max(scores, -1, keepdims=True))
    return expo * (1.0 / jnp.sum(expo, -1, keepdims=True))


def attend(rows, head_size, length, allowed):
    columns = rows.shape[1] // 3
    images = []
    for at in range(0, rows.shape[0], length):
        outs = []
        for h in range(0, columns, head_size):
            q, k, v = (
                rows[at : at + length, j * columns + h : j * columns + h + head_size]
                for j in range(3)
            )
            soft = softened(q, k, head_size, allowed)
            outs.append(nn(soft.astype(bf16), v).astype(bf16))
        images.append(jnp.concatenate(outs, 1))
    return jnp.concatenate(images, 0) if len(images) > 1 else images[0]


def attend_back(rows, grad, head_size, length, allowed):
    columns = rows.shape[1] // 3
    factor = 1.0 / math.sqrt(head_size)
    images = []
    for at in range(0, rows.shape[0], length):
        outs = [[], [], []]
        for h in range(0, columns, head_size):
            q, k, v = (
                rows[at : at + length, j * columns + h : j * columns + h + head_size]
                for j in range(3)
            )
            g = grad[at : at + length, h : h + head_size]
            soft = softened(q, k, head_size, allowed)
            outs[2].append(tn(soft.astype(bf16), g).astype(bf16))
            ds = nt_(g, v)
            ds = (soft * (ds - jnp.sum(ds * soft, -1, keepdims=True))).astype(bf16)
            outs[0].append((nn(ds, k) * factor).astype(bf16))
            outs[1].append((tn(ds, q) * factor).astype(bf16))
        images.append(jnp.concatenate(outs[0] + outs[1] + outs[2], 1))
    return jnp.concatenate(images, 0) if len(images) > 1 else images[0]


def same_image(role, length, context):
    row = lax.broadcasted_iota(jnp.int32, (length, length), 0) // context
    column = lax.broadcasted_iota(jnp.int32, (length, length), 1) // context
    return (row == column) | (role != 0)


def encoder_attend_kernel(
    edge, unit, context, head_size, kept, role_ref, patch_ref, base_ref, emb_ref, w_ref, vec_ref,
    mid_ref, resid_ref, normed_ref, rows_ref, att_ref, x_ref, h_ref,
):
    step = pl.program_id(0)
    groups = pl.num_programs(0) // 2
    side = 2
    wide = side * edge
    pix = patch_ref.shape[2]
    columns = wide // 4

    @pl.when(step == 0)
    def _():
        x_ref[...] = base_ref[...]

    @pl.when(step < groups)
    def _():
        for r in range(side):
            x_ref[:, r * edge : (r + 1) * edge] += nt_(
                patch_ref[0], emb_ref[0, :, r * pix : (r + 1) * pix]
            )

    @pl.when(step == groups - 1)
    def _():
        values = x_ref[...]
        resid_ref[...] = values[:kept]
        low = layer_norm(values, vec_ref[0:1], vec_ref[1:2]).astype(bf16)
        h_ref[...] = low
        normed_ref[...] = low[:kept]

    @pl.when(step >= groups)
    def _():
        rows = sum(
            nn(h_ref[:, r * edge : (r + 1) * edge], w_ref[0, :, r * wide : r * wide + 3 * columns])
            for r in range(side)
        ).astype(bf16)
        rows_ref[0] = rows[:kept]
        att = attend(rows, head_size, unit, same_image(role_ref[0], unit, context))
        att_ref[0] = att[:kept]
        for r in range(side):
            x_ref[:, r * edge : (r + 1) * edge] += nt_(
                att, w_ref[0, :, r * wide + 3 * columns : (r + 1) * wide]
            )

    @pl.when(step == 2 * groups - 1)
    def _():
        mid_ref[...] = x_ref[...]


def encoder_feed_kernel(
    edge, kept, mid_ref, up_ref, down_ref, vec_ref, pick_ref, swap_ref,
    out_ref, normed_ref, hidden_ref, feat_ref, target_ref, x_ref, h_ref,
):
    step = pl.program_id(0)
    groups = pl.num_programs(0)
    side = 2
    wide = side * edge

    @pl.when(step == 0)
    def _():
        values = mid_ref[...]
        x_ref[...] = values
        low = layer_norm(values, vec_ref[2:3], vec_ref[3:4]).astype(bf16)
        h_ref[...] = low
        normed_ref[...] = low[:kept]

    hidden = sum(
        nn(h_ref[:, r * edge : (r + 1) * edge], up_ref[0, :, r * wide : (r + 1) * wide])
        for r in range(side)
    )
    hidden_ref[0] = hidden[:kept]
    active = gelu_parts(hidden)[0].astype(bf16)
    for r in range(side):
        x_ref[:, r * edge : (r + 1) * edge] += nt_(
            active, down_ref[0, :, r * wide : (r + 1) * wide]
        )

    @pl.when(step == groups - 1)
    def _():
        values = x_ref[...]
        out_ref[...] = values[:kept]
        final = layer_norm(values, vec_ref[4:5], vec_ref[5:6])
        encoded = final[:kept].astype(bf16)
        target = norm_parts(final)[0].astype(bf16)
        picked = nn(pick_ref[...], target).astype(bf16)
        for t in range(swap_ref.shape[0]):
            feat_ref[t] = nn(encoded, swap_ref[t]).astype(bf16)
            target_ref[t] = nn(picked, swap_ref[t]).astype(bf16)


def put_halves(keep_ref, send_ref, t, columns, value):
    middle = value.shape[0] // 2
    low = value.astype(bf16)
    keep_ref[t, :, columns] = low[:middle]
    send_ref[t, :, columns] = low[middle:]


def predictor_kernel(
    share, context, players, head_size, denominator,
    feat_ref, target_ref, base_ref, w_ref, vec_ref, swap_ref,
    keep_ref, send_ref, vec_grad_ref, loss_ref, back_ref,
    x_ref, mid_ref, h_ref, h2_ref, rows_ref, att_ref, hidden_ref, acc_ref, d_ref, low_ref, f_ref,
):
    groups = w_ref.shape[0]
    edge = w_ref.shape[1]
    length = base_ref.shape[0] // share
    quarter = feat_ref.shape[2]
    columns = edge // 4
    last = 3 * players * edge
    in_cols = slice(last, last + quarter)
    out_cols = slice(last + quarter, last + 2 * quarter)

    def span(number):
        return slice(number * edge, (number + 1) * edge)

    vec_grad_ref[...] = jnp.zeros_like(vec_grad_ref)

    projected = sum(nt_(feat_ref[t], w_ref[t, :, in_cols]) for t in range(groups))
    x_ref[0] = base_ref[...]
    for i in range(share):
        x_ref[0, i * length : i * length + context] += projected[i * context : (i + 1) * context]

    for j in range(players):
        values = x_ref[j]
        h_ref[j] = layer_norm(values, vec_ref[4 * j : 4 * j + 1], vec_ref[4 * j + 1 : 4 * j + 2]).astype(bf16)
        mid_ref[j] = values

        @pl.loop(0, groups)
        def _(t, j=j):
            rows = nn(h_ref[j], w_ref[t, :, 3 * j * edge : 3 * j * edge + 3 * columns]).astype(bf16)
            rows_ref[j, t] = rows
            att = attend(rows, head_size, length, None)
            att_ref[j, t] = att
            mid_ref[j] += nt_(att, w_ref[t, :, 3 * j * edge + 3 * columns : (3 * j + 1) * edge])

        values = mid_ref[j]
        h2_ref[j] = layer_norm(values, vec_ref[4 * j + 2 : 4 * j + 3], vec_ref[4 * j + 3 : 4 * j + 4]).astype(bf16)
        x_ref[j + 1] = values

        @pl.loop(0, groups)
        def _(t, j=j):
            hidden = nn(h2_ref[j], w_ref[t, :, span(3 * j + 1)])
            hidden_ref[j, t] = hidden
            x_ref[j + 1] += nt_(gelu_parts(hidden)[0].astype(bf16), w_ref[t, :, span(3 * j + 2)])

    final_gain = vec_ref[4 * players : 4 * players + 1]
    final = layer_norm(x_ref[players], final_gain, vec_ref[4 * players + 1 : 4 * players + 2]).astype(bf16)
    f_ref[...] = jnp.concatenate(
        [final[i * length + context : (i + 1) * length] for i in range(share)], 0
    )
    total = jnp.zeros((1, 1), f32)
    grad_f = jnp.zeros(f_ref.shape, f32)
    for t in range(groups):
        out_w = w_ref[t, :, out_cols]
        gap = nn(f_ref[...], out_w) - target_ref[t].astype(f32)
        size = jnp.abs(gap)
        terms = jnp.where(size < 1.0, 0.5 * gap * gap, size - 0.5)
        total += jnp.sum(jnp.sum(terms, 1, keepdims=True), 0, keepdims=True)
        grad_pred = (jnp.clip(gap, -1.0, 1.0) * (1.0 / denominator)).astype(bf16)
        put_halves(keep_ref, send_ref, t, out_cols, tn(f_ref[...], grad_pred))
        grad_f += nt_(grad_pred, out_w)
    loss_ref[...] = jnp.broadcast_to(total * (1.0 / denominator), loss_ref.shape)
    d_ref[...] = jnp.zeros_like(d_ref)
    tail = length - context
    for i in range(share):
        d_ref[i * length + context : (i + 1) * length] = grad_f[i * tail : (i + 1) * tail]
    grad, gain_g, shift_g = norm_backward(d_ref[...], x_ref[players], final_gain)
    d_ref[...] = grad
    vec_grad_ref[4 * players : 4 * players + 1] = gain_g
    vec_grad_ref[4 * players + 1 : 4 * players + 2] = shift_g

    for j in reversed(range(players)):
        low_ref[...] = d_ref[...].astype(bf16)
        acc_ref[...] = jnp.zeros_like(acc_ref)

        @pl.loop(0, groups)
        def _(t, j=j):
            active, slope = gelu_parts(hidden_ref[j, t])
            low = low_ref[...]
            put_halves(keep_ref, send_ref, t, span(3 * j + 2), tn(low, active.astype(bf16)))
            grad_hidden = (nn(low, w_ref[t, :, span(3 * j + 2)]) * slope).astype(bf16)
            put_halves(keep_ref, send_ref, t, span(3 * j + 1), tn(h2_ref[j], grad_hidden))
            acc_ref[...] += nt_(grad_hidden, w_ref[t, :, span(3 * j + 1)])

        grad, gain_g, shift_g = norm_backward(acc_ref[...], mid_ref[j], vec_ref[4 * j + 2 : 4 * j + 3])
        vec_grad_ref[4 * j + 2 : 4 * j + 3] = gain_g
        vec_grad_ref[4 * j + 3 : 4 * j + 4] = shift_g
        grad = d_ref[...] + grad
        d_ref[...] = grad
        low_ref[...] = grad.astype(bf16)
        acc_ref[...] = jnp.zeros_like(acc_ref)

        @pl.loop(0, groups)
        def _(t, j=j):
            low = low_ref[...]
            attn_w = w_ref[t, :, span(3 * j)]
            grad_att = nn(low, attn_w[:, 3 * columns :]).astype(bf16)
            grad_rows = attend_back(rows_ref[j, t], grad_att, head_size, length, None)
            grad_w = jnp.concatenate([tn(h_ref[j], grad_rows), tn(low, att_ref[j, t])], 1)
            put_halves(keep_ref, send_ref, t, span(3 * j), grad_w)
            acc_ref[...] += nt_(grad_rows, attn_w[:, : 3 * columns])

        grad, gain_g, shift_g = norm_backward(acc_ref[...], x_ref[j], vec_ref[4 * j : 4 * j + 1])
        vec_grad_ref[4 * j : 4 * j + 1] = gain_g
        vec_grad_ref[4 * j + 1 : 4 * j + 2] = shift_g
        d_ref[...] += grad

    mask_grad = jnp.zeros((1, edge), f32)
    for i in range(share):
        mask_grad += jnp.sum(d_ref[i * length + context : (i + 1) * length], 0, keepdims=True)
    vec_grad_ref[4 * players + 2 : 4 * players + 3] = mask_grad
    low = jnp.concatenate(
        [d_ref[i * length : i * length + context] for i in range(share)], 0
    ).astype(bf16)
    back = jnp.zeros((low.shape[0], swap_ref.shape[1]), f32)
    for t in range(groups):
        put_halves(keep_ref, send_ref, t, in_cols, tn(low, feat_ref[t]))
        back += nt_(nn(low, w_ref[t, :, in_cols]).astype(bf16), swap_ref[t])
    back_ref[...] = back.astype(bf16)


def encoder_feed_back_kernel(
    edge, back_ref, out_ref, mid_ref, normed_ref, hidden_ref, up_ref, down_ref, vec_ref,
    up_keep, up_send, down_keep, down_send, grad_ref, vec_grad_ref, d_ref, low_ref, acc_ref,
):
    step = pl.program_id(0)
    groups = pl.num_programs(0)
    wide = 2 * edge

    @pl.when(step == 0)
    def _():
        grad, gain_g, shift_g = norm_backward(back_ref[...].astype(f32), out_ref[...], vec_ref[4:5])
        d_ref[...] = grad
        low_ref[...] = grad.astype(bf16)
        acc_ref[...] = jnp.zeros_like(acc_ref)
        vec_grad_ref[...] = jnp.zeros_like(vec_grad_ref)
        vec_grad_ref[4:5] = gain_g
        vec_grad_ref[5:6] = shift_g

    active, slope = gelu_parts(hidden_ref[0])
    active = active.astype(bf16)
    grad_hidden = sum(
        nn(low_ref[:, r * edge : (r + 1) * edge], down_ref[0, :, r * wide : (r + 1) * wide])
        for r in range(2)
    )
    grad_hidden = (grad_hidden * slope).astype(bf16)
    for r in range(2):
        mine = slice(r * edge, (r + 1) * edge)
        columns = slice(r * wide, (r + 1) * wide)
        put_halves(down_keep, down_send, 0, columns, tn(low_ref[:, mine], active))
        put_halves(up_keep, up_send, 0, columns, tn(normed_ref[:, mine], grad_hidden))
        acc_ref[:, mine] += nt_(grad_hidden, up_ref[0, :, columns])

    @pl.when(step == groups - 1)
    def _():
        grad, gain_g, shift_g = norm_backward(acc_ref[...], mid_ref[...], vec_ref[2:3])
        grad_ref[...] = d_ref[...] + grad
        vec_grad_ref[2:3] = gain_g
        vec_grad_ref[3:4] = shift_g


def encoder_attend_back_kernel(
    edge, unit, context, head_size,
    role_ref, grad_ref, resid_ref, normed_ref, rows_ref, att_ref, w_ref, patch_ref, vec_ref,
    keep_ref, send_ref, vec_grad_ref, low_ref, acc_ref,
):
    step = pl.program_id(0)
    groups = pl.num_programs(0) // 2
    wide = 2 * edge
    columns = wide // 4
    pix = patch_ref.shape[2]

    @pl.when(step == 0)
    def _():
        low_ref[...] = grad_ref[...].astype(bf16)
        acc_ref[...] = jnp.zeros_like(acc_ref)

    @pl.when(step < groups)
    def _():
        grad_att = sum(
            nn(
                low_ref[:, r * edge : (r + 1) * edge],
                w_ref[0, :, r * wide + 3 * columns : (r + 1) * wide],
            )
            for r in range(2)
        ).astype(bf16)
        allowed = same_image(role_ref[0], unit, context)
        grad_rows = attend_back(rows_ref[0], grad_att, head_size, unit, allowed)
        for r in range(2):
            mine = slice(r * edge, (r + 1) * edge)
            grad_w = jnp.concatenate(
                [tn(normed_ref[:, mine], grad_rows), tn(low_ref[:, mine], att_ref[0])], 1
            )
            put_halves(keep_ref, send_ref, step, slice(r * wide, (r + 1) * wide), grad_w)
            acc_ref[:, mine] += nt_(grad_rows, w_ref[0, :, r * wide : r * wide + 3 * columns])

    @pl.when(step == groups - 1)
    def _():
        grad, gain_g, shift_g = norm_backward(acc_ref[...], resid_ref[...], vec_ref[0:1])
        grad = grad_ref[...] + grad
        low_ref[...] = grad.astype(bf16)
        vec_grad_ref[...] = jnp.zeros_like(vec_grad_ref)
        vec_grad_ref[0:1] = gain_g
        vec_grad_ref[1:2] = shift_g
        vec_grad_ref[6:7] = jnp.sum(grad, 0, keepdims=True)

    @pl.when(step >= groups)
    def _():
        grad_w = jnp.concatenate(
            [tn(low_ref[:, r * edge : (r + 1) * edge], patch_ref[0]) for r in range(2)], 1
        )
        put_halves(keep_ref, send_ref, step - groups, slice(2 * wide, 2 * wide + 2 * pix), grad_w)


def split(values):
    high = values.astype(bf16)
    return high, (values - high.astype(f32)).astype(bf16)


def shampoo_kernel(
    grad_ref, weight_ref, left_ref, right_ref, root_left_ref, root_right_ref, teacher_ref,
    grad_out, weight_out, left_out, right_out, teacher_out,
):
    low = grad_ref[0]
    grad_out[0, 0] = low.astype(f32)
    left_out[0, 0] = 0.95 * left_ref[0, 0] + 0.05 * nt_(low, low)
    right_out[0, 0] = 0.95 * right_ref[0, 0] + 0.05 * tn(low, low)
    high, rest = split(root_left_ref[0, 0])
    side = nn(high, low) + nn(rest, low)
    high, rest = split(side)
    root_high, root_rest = split(root_right_ref[0, 0])
    step = nn(high, root_high) + nn(high, root_rest) + nn(rest, root_high)
    mean = jnp.mean(jnp.mean(step * step, 1, keepdims=True), 0, keepdims=True)
    step = step * lax.rsqrt(mean + 1e-06)
    weight = weight_ref[0, 0]
    new = weight - 0.05 * (step + 0.05 * weight)
    weight_out[0, 0] = new
    teacher_out[0, 0] = 0.7 * teacher_ref[0, 0] + 0.3 * new


def whole(shape):
    return pl.BlockSpec(shape, lambda *_: (0,) * len(shape))


def by_group(shape):
    return pl.BlockSpec((1,) + shape, lambda t: (t, 0, 0))


def compiled():
    return pltpu.CompilerParams(
        dimension_semantics=("arbitrary",), vmem_limit_bytes=KERNEL_BYTES
    )


def cost(flops, moved):
    return pl.CostEstimate(flops=int(flops), bytes_accessed=int(moved), transcendentals=0)


def sincos(cell_index, columns):
    quarter = columns // 4
    frequency = 1.0 / 10000.0 ** (jnp.arange(quarter).astype(f32) / quarter)
    col_angle = (cell_index % SIDE).astype(f32)[..., None] * frequency
    row_angle = (cell_index // SIDE).astype(f32)[..., None] * frequency
    return jnp.concatenate(
        [jnp.sin(col_angle), jnp.cos(col_angle), jnp.sin(row_angle), jnp.cos(row_angle)], -1
    )


def adamw(master, moment, second, gradient, step_rate, weight_decay):
    moment = 0.9 * moment + 0.1 * gradient
    second = 0.999 * second + 0.001 * gradient * gradient
    unbiased_first = moment / (1.0 - 0.9**STEP)
    unbiased_second = second / (1.0 - 0.999**STEP)
    return (
        master
        - step_rate
        * (unbiased_first / (jnp.sqrt(unbiased_second) + 1e-08) + weight_decay * master),
        moment,
        second,
    )


class Routes:
    def __init__(self, nd, nt):
        self.nd, self.nt, self.half = nd, nt, nt // 2
        self.low_bits = [1 << s for s in range(1, nd.bit_length() - 1)]
        self.stages = len(self.low_bits)

    def order(self, core):
        return self.low_bits if core == 0 else self.low_bits[::-1]

    def pairs(self, target, keep):
        found = []
        for d in range(self.nd):
            for z in range(self.nt):
                if keep(d, z):
                    d2, z2 = target(d, z)
                    found.append((d * self.nt + z, d2 * self.nt + z2))
        return found

    def stage(self, number, values, role):
        def target(d, z):
            if number == self.stages:
                return d ^ 1, z
            return d ^ self.order(d & 1)[number], z

        return lax.ppermute(
            values,
            AXES,
            self.pairs(target, lambda d, z: role is None or z // self.half == role),
        )

    def across(self, r, values, from_role=None, to_role=None):
        def keep(d, z):
            return (from_role is None or z // self.half == from_role) and (
                to_role is None or (z ^ r) // self.half == to_role
            )

        return lax.ppermute(values, AXES, self.pairs(lambda d, z: (d, z ^ r), keep))

    def holders(self, d):
        place = jnp.arange(self.nd, dtype=jnp.int32)
        held = d ^ (place >> self.stages)
        core = held & 1
        for s in range(self.stages):
            bit = (place >> s) & 1
            held = held ^ (bit * jnp.where(core == 0, self.order(0)[s], self.order(1)[s]))
        return held

    def spread(self, stack, role):
        for number in range(self.stages + 1):
            stack = jnp.concatenate([stack, self.stage(number, stack, role)], 1)
        return stack

    def reduce(self, keep, send, role, is_role):
        for number in reversed(range(self.stages + 1)):
            got = self.stage(number, send, role)
            keep = (keep.astype(f32) + got.astype(f32)).astype(bf16)
            if number:
                middle = keep.shape[1] // 2
                keep, send = keep[:, :middle], keep[:, middle:]
        total = jnp.where(is_role, keep[0].astype(f32), 0.0)
        for r in range(1, self.nt):
            total = total + self.across(r, keep[r], from_role=role).astype(f32)
        return total

    def total(self, values):
        for bit in [1] + self.low_bits:
            values = values + lax.ppermute(
                values, AXES, self.pairs(lambda d, z, b=bit: (d ^ b, z), lambda d, z: True)
            )
        r = 1
        while r < self.nt:
            values = values + self.across(r, values)
            r *= 2
        return values


def shards(
    patches,
    ctx_idx,
    tgt_idx,
    owner,
    weights,
    stats_left,
    stats_right,
    root_left,
    root_right,
    teacher_slot_blocks,
    embed,
    embed_m,
    embed_v,
    teacher_embed,
    enc_vectors,
    enc_m,
    enc_v,
    pred_vectors,
    pred_m,
    pred_v,
    teacher_vectors,
):
    nt = lax.axis_size("tensor")
    nd = lax.axis_size("dp")
    routes = Routes(nd, nt)
    half = nt // 2
    d = lax.axis_index("dp")
    z = lax.axis_index("tensor")
    role = z // half
    student_role = role == 0
    images, npatches, pix_part = patches.shape
    slots = weights.shape[1]
    edge = weights.shape[-1]
    slot_count = slots * nd
    block_count = owner.shape[0]
    width = enc_vectors.shape[1]
    narrow = pred_vectors.shape[1]
    players = (pred_vectors.shape[0] - 3) // 4
    side = width // edge
    teach_count = 3 * side * side
    quarter = width // nt
    context_len = ctx_idx.shape[1]
    target_len = tgt_idx.shape[1]
    seq_len = context_len + target_len
    share = images // half
    rows_part = edge // nd

    both = jnp.stack([weights[0], teacher_slot_blocks[0]]).astype(bf16)
    both = both.reshape(2, slots, nd, rows_part, edge)
    both = lax.all_to_all(both, "dp", split_axis=2, concat_axis=0, tiled=False)
    by_slot = both.transpose(1, 0, 2, 3, 4).reshape(2, slot_count, rows_part, edge)
    mine = by_slot[0][owner].transpose(1, 0, 2).reshape(rows_part, -1)
    teach = by_slot[1][owner[:teach_count]].transpose(1, 0, 2).reshape(rows_part, -1)

    chunk = rows_part
    wide_t = jnp.stack([embed, teacher_embed]).astype(bf16).transpose(0, 2, 1)
    high = d // (nd // 2)
    first = lax.dynamic_slice_in_dim(wide_t, high * chunk, chunk, 1)
    second = lax.dynamic_slice_in_dim(wide_t, (1 - high) * chunk, chunk, 1)

    def swap_pairs(flip, inverse):
        found = []
        for a in range(nd):
            h = a // (nd // 2)
            b = 2 * (a % (nd // 2)) + (h if not flip else 1 - h)
            found.append((b, a) if inverse else (a, b))
        return found

    got_first = lax.ppermute(first, "dp", swap_pairs(False, False))
    got_second = lax.ppermute(second, "dp", swap_pairs(True, False))
    odd = d % 2
    emb_rows = jnp.concatenate(
        [
            jnp.where(odd == 0, got_first, got_second),
            jnp.where(odd == 0, got_second, got_first),
        ],
        2,
    )

    def gather_encoder(of_student, of_teacher):
        own = jnp.where(student_role, of_student, of_teacher)
        other = jnp.where(student_role, of_teacher, of_student)
        parts = [own]
        for r in range(1, nt):
            parts.append(routes.across(r, own if r < half else other))
        return routes.spread(jnp.stack(parts), None)

    mat = side * width
    attn_emb = gather_encoder(
        jnp.concatenate([mine[:, :mat], emb_rows[0]], 1),
        jnp.concatenate([teach[:, :mat], emb_rows[1]], 1),
    )
    up_w = gather_encoder(mine[:, mat : 2 * mat], teach[:, mat : 2 * mat])
    down_t = gather_encoder(mine[:, 2 * mat : 3 * mat], teach[:, 2 * mat :])
    pred_own = mine[:, 3 * mat :]
    pred_parts = [pred_own]
    for r in range(1, nt):
        pred_parts.append(routes.across(r, pred_own, to_role=1))
    pred_all = routes.spread(jnp.stack(pred_parts), 1)

    holder = routes.holders(d)
    inside = jnp.arange(rows_part, dtype=jnp.int32)
    feat_p = (holder[:, None] * rows_part + inside[None, :]).reshape(-1)
    feat = jnp.concatenate([r * edge + feat_p for r in range(side)])
    one_hot = (feat[:, None] == jnp.arange(width)[None, :]).astype(f32)
    one_hot_p = (feat_p[:, None] == jnp.arange(narrow)[None, :]).astype(f32)

    def to_local(rows, hot):
        return jnp.einsum("nf,lf->nl", rows, hot, precision=exact, preferred_element_type=f32)

    def to_global(rows, hot):
        return jnp.einsum("nl,lf->nf", rows, hot, precision=exact, preferred_element_type=f32)

    vec = to_local(jnp.where(student_role, enc_vectors, teacher_vectors), one_hot)
    vec = jnp.pad(vec, ((0, 1), (0, 0)))
    pvec = to_local(pred_vectors, one_hot_p)
    pvec = jnp.pad(pvec, ((0, 16 - pvec.shape[0]), (0, 0)))
    pred_z = half + z % half
    group_feat = (pred_z ^ jnp.arange(nt, dtype=jnp.int32))[:, None] * quarter + jnp.arange(
        quarter, dtype=jnp.int32
    )
    swap = (feat[None, :, None] == group_feat[:, None, :]).astype(bf16)

    part = z % half
    picked = jnp.take_along_axis(patches, ctx_idx[:, :, None], 1)

    def rows_for(target_z):
        where = (target_z % half) * share
        ctx_rows = lax.dynamic_slice_in_dim(picked, where, share, 0).reshape(-1, pix_part)
        all_rows = lax.dynamic_slice_in_dim(patches, where, share, 0).reshape(-1, pix_part)
        padded = jnp.pad(ctx_rows, ((0, all_rows.shape[0] - ctx_rows.shape[0]), (0, 0)))
        return jnp.where(target_z // half == 0, padded, all_rows)

    patch_rows = jnp.stack(
        [rows_for(z)] + [routes.across(r, rows_for(z ^ r)) for r in range(1, nt)]
    )
    my_ctx = lax.dynamic_slice_in_dim(ctx_idx, part * share, share, 0)
    my_tgt = lax.dynamic_slice_in_dim(tgt_idx, part * share, share, 0)
    full_rows = share * npatches
    ctx_rows = share * context_len
    tgt_rows = share * target_len
    ctx_places = jnp.pad(my_ctx.reshape(-1), (0, full_rows - ctx_rows))
    places = jnp.where(student_role, ctx_places, jnp.arange(full_rows) % npatches)
    table = to_local(sincos(jnp.arange(npatches), width), one_hot)
    table_p = to_local(sincos(jnp.arange(npatches), narrow), one_hot_p)
    base = table[places] + vec[6]
    tgt_places = (my_tgt + npatches * jnp.arange(share, dtype=jnp.int32)[:, None]).reshape(-1)
    pick = (tgt_places[:, None] == jnp.arange(full_rows)[None, :]).astype(bf16)
    role_word = role.astype(jnp.int32).reshape(1)

    attn_cols = side * width
    columns = width // nt
    resid, normed_a, rows_a, att_a, middle = [None] * 5
    middle, resid, normed_a, rows_a, att_a = pl.pallas_call(
        functools.partial(encoder_attend_kernel, edge, npatches, context_len, HD, ctx_rows),
        grid=(2 * nt,),
        in_specs=[
            pl.BlockSpec(memory_space=pltpu.SMEM),
            pl.BlockSpec((1, full_rows, pix_part), lambda i: (jnp.minimum(i, nt - 1), 0, 0)),
            whole((full_rows, width)),
            pl.BlockSpec(
                (1, edge, side * pix_part),
                lambda i: (jnp.minimum(i, nt - 1), 0, attn_cols // (side * pix_part)),
            ),
            pl.BlockSpec((1, edge, attn_cols), lambda i: (jnp.maximum(i - nt, 0), 0, 0)),
            whole((8, width)),
        ],
        out_specs=[
            whole((full_rows, width)),
            whole((ctx_rows, width)),
            whole((ctx_rows, width)),
            pl.BlockSpec((1, ctx_rows, 3 * columns), lambda i: (jnp.maximum(i - nt, 0), 0, 0)),
            pl.BlockSpec((1, ctx_rows, columns), lambda i: (jnp.maximum(i - nt, 0), 0, 0)),
        ],
        out_shape=[
            jax.ShapeDtypeStruct((full_rows, width), f32),
            jax.ShapeDtypeStruct((ctx_rows, width), f32),
            jax.ShapeDtypeStruct((ctx_rows, width), bf16),
            jax.ShapeDtypeStruct((nt, ctx_rows, 3 * columns), bf16),
            jax.ShapeDtypeStruct((nt, ctx_rows, columns), bf16),
        ],
        scratch_shapes=[VMEM((full_rows, width), f32), VMEM((full_rows, width), bf16)],
        compiler_params=compiled(),
        cost_estimate=cost(6e9, 12e6),
        name="encoder_attend",
    )(role_word, patch_rows, base, attn_emb, attn_emb, vec)
    output, normed_f, hidden, enc_feat, target = pl.pallas_call(
        functools.partial(encoder_feed_kernel, edge, ctx_rows),
        grid=(nt,),
        in_specs=[
            whole((full_rows, width)),
            by_group((edge, mat)),
            by_group((edge, mat)),
            whole((8, width)),
            whole((tgt_rows, full_rows)),
            whole((nt, width, quarter)),
        ],
        out_specs=[
            whole((ctx_rows, width)),
            whole((ctx_rows, width)),
            by_group((ctx_rows, width)),
            whole((nt, ctx_rows, quarter)),
            whole((nt, tgt_rows, quarter)),
        ],
        out_shape=[
            jax.ShapeDtypeStruct((ctx_rows, width), f32),
            jax.ShapeDtypeStruct((ctx_rows, width), bf16),
            jax.ShapeDtypeStruct((nt, ctx_rows, width), f32),
            jax.ShapeDtypeStruct((nt, ctx_rows, quarter), bf16),
            jax.ShapeDtypeStruct((nt, tgt_rows, quarter), bf16),
        ],
        scratch_shapes=[VMEM((full_rows, width), f32), VMEM((full_rows, width), bf16)],
        compiler_params=compiled(),
        cost_estimate=cost(8e9, 14e6),
        name="encoder_feed",
    )(middle, up_w, down_t, vec, pick, swap)

    feat_in = routes.across(half, enc_feat, from_role=0)
    tokens_at = table_p[jnp.concatenate([my_ctx, my_tgt], 1)]
    mask_rows = jnp.arange(seq_len)[None, :, None] >= context_len
    tokens_at = jnp.where(mask_rows, tokens_at + pvec[4 * players + 2], tokens_at)
    tokens_at = tokens_at.reshape(-1, narrow)
    token_rows = share * seq_len
    pred_cols = (3 * players + 1) * edge
    denominator = images * nd * target_len * width
    pred_columns = narrow // nt
    in_vmem = pl.BlockSpec(memory_space=VMEM)
    pred_keep, pred_send, pred_vec_g, loss_tile, back = pl.pallas_call(
        functools.partial(predictor_kernel, share, context_len, players, PHD, denominator),
        in_specs=[in_vmem] * 6,
        out_specs=[in_vmem] * 5,
        out_shape=[
            jax.ShapeDtypeStruct((nt, edge // 2, pred_cols), bf16),
            jax.ShapeDtypeStruct((nt, edge // 2, pred_cols), bf16),
            jax.ShapeDtypeStruct((16, narrow), f32),
            jax.ShapeDtypeStruct((8, 128), f32),
            jax.ShapeDtypeStruct((ctx_rows, width), bf16),
        ],
        scratch_shapes=[
            VMEM((players + 1, token_rows, narrow), f32),
            VMEM((players, token_rows, narrow), f32),
            VMEM((players, token_rows, narrow), bf16),
            VMEM((players, token_rows, narrow), bf16),
            VMEM((players, nt, token_rows, 3 * pred_columns), bf16),
            VMEM((players, nt, token_rows, pred_columns), bf16),
            VMEM((players, nt, token_rows, edge), f32),
            VMEM((token_rows, narrow), f32),
            VMEM((token_rows, narrow), f32),
            VMEM((token_rows, narrow), bf16),
            VMEM((tgt_rows, narrow), bf16),
        ],
        compiler_params=pltpu.CompilerParams(vmem_limit_bytes=KERNEL_BYTES),
        cost_estimate=cost(16e9, 30e6),
        name="predictor",
    )(feat_in, target, tokens_at, pred_all, pvec, swap)
    back = routes.across(half, back, from_role=1)

    half_shape = jax.ShapeDtypeStruct((nt, edge // 2, mat), bf16)
    up_keep, up_send, down_keep, down_send, grad_mid, vec_g1 = pl.pallas_call(
        functools.partial(encoder_feed_back_kernel, edge),
        grid=(nt,),
        in_specs=[
            whole((ctx_rows, width)),
            whole((ctx_rows, width)),
            whole((ctx_rows, width)),
            whole((ctx_rows, width)),
            by_group((ctx_rows, width)),
            by_group((edge, mat)),
            by_group((edge, mat)),
            whole((8, width)),
        ],
        out_specs=[by_group((edge // 2, mat))] * 4 + [whole((ctx_rows, width)), whole((8, width))],
        out_shape=[half_shape] * 4
        + [
            jax.ShapeDtypeStruct((ctx_rows, width), f32),
            jax.ShapeDtypeStruct((8, width), f32),
        ],
        scratch_shapes=[
            VMEM((ctx_rows, width), f32),
            VMEM((ctx_rows, width), bf16),
            VMEM((ctx_rows, width), f32),
        ],
        compiler_params=compiled(),
        cost_estimate=cost(8e9, 25e6),
        name="encoder_feed_back",
    )(back, output, middle, normed_f, hidden, up_w, down_t, vec)
    all_cols = attn_cols + side * pix_part
    attn_keep, attn_send, vec_g2 = pl.pallas_call(
        functools.partial(encoder_attend_back_kernel, edge, npatches, context_len, HD),
        grid=(2 * nt,),
        in_specs=[
            pl.BlockSpec(memory_space=pltpu.SMEM),
            whole((ctx_rows, width)),
            whole((ctx_rows, width)),
            whole((ctx_rows, width)),
            pl.BlockSpec((1, ctx_rows, 3 * columns), lambda i: (jnp.minimum(i, nt - 1), 0, 0)),
            pl.BlockSpec((1, ctx_rows, columns), lambda i: (jnp.minimum(i, nt - 1), 0, 0)),
            pl.BlockSpec((1, edge, attn_cols), lambda i: (jnp.minimum(i, nt - 1), 0, 0)),
            pl.BlockSpec((1, ctx_rows, pix_part), lambda i: (jnp.maximum(i - nt, 0), 0, 0)),
            whole((8, width)),
        ],
        out_specs=[
            whole((nt, edge // 2, all_cols)),
            whole((nt, edge // 2, all_cols)),
            whole((8, width)),
        ],
        out_shape=[
            jax.ShapeDtypeStruct((nt, edge // 2, all_cols), bf16),
            jax.ShapeDtypeStruct((nt, edge // 2, all_cols), bf16),
            jax.ShapeDtypeStruct((8, width), f32),
        ],
        scratch_shapes=[VMEM((ctx_rows, width), bf16), VMEM((ctx_rows, width), f32)],
        compiler_params=compiled(),
        cost_estimate=cost(6e9, 20e6),
        name="encoder_attend_back",
    )(role_word, grad_mid, resid, normed_a, rows_a, att_a, attn_emb, patch_rows, vec)

    pred_sum = routes.reduce(pred_keep, pred_send, 1, role == 1)
    down_sum = routes.reduce(down_keep, down_send, 0, student_role)
    up_sum = routes.reduce(up_keep, up_send, 0, student_role)
    attn_emb_sum = routes.reduce(attn_keep, attn_send, 0, student_role)

    enc_rows = to_global(vec_g1[:7] + vec_g2[:7], one_hot)
    pred_rows = to_global(pred_vec_g[: 4 * players + 3], one_hot_p)
    enc_rows = jnp.where(student_role, enc_rows, 0.0)
    pred_rows = jnp.where(role == 1, pred_rows, 0.0)
    loss_row = jnp.where(role == 1, loss_tile[0, 0], 0.0)
    packed = jnp.concatenate([enc_rows.reshape(-1), pred_rows.reshape(-1), loss_row[None]])
    packed = jnp.pad(packed, (0, -packed.shape[0] % 1024)).reshape(-1, 128)
    packed = routes.total(packed).reshape(-1)
    enc_total = packed[: enc_rows.size].reshape(enc_rows.shape)
    pred_total = packed[enc_rows.size : enc_rows.size + pred_rows.size].reshape(pred_rows.shape)
    loss_total = packed[enc_rows.size + pred_rows.size]

    by_block = jnp.concatenate(
        [
            attn_emb_sum[:, :mat],
            up_sum,
            down_sum,
            pred_sum,
            jnp.zeros((rows_part, edge), f32),
        ],
        1,
    ).astype(bf16)
    by_block = by_block.reshape(rows_part, block_count + 1, edge).transpose(1, 0, 2)
    slot_of = (
        jnp.full((slot_count,), block_count, jnp.int32)
        .at[owner]
        .set(jnp.arange(block_count, dtype=jnp.int32))
    )
    slot_rows = by_block[slot_of].reshape(nd, slots, rows_part, edge)
    slot_rows = lax.all_to_all(slot_rows, "dp", split_axis=0, concat_axis=1, tiled=False)
    low_grads = slot_rows.reshape(slots, edge, edge)

    emb_sum = attn_emb_sum[:, mat:]
    emb_halves = jnp.stack([emb_sum[:, :pix_part], emb_sum[:, pix_part:]])
    send_first = lax.dynamic_index_in_dim(emb_halves, odd, 0, keepdims=False)
    send_second = lax.dynamic_index_in_dim(emb_halves, 1 - odd, 0, keepdims=False)
    back_first = lax.ppermute(send_first, "dp", swap_pairs(False, True))
    back_second = lax.ppermute(send_second, "dp", swap_pairs(True, True))
    embed_grad = jnp.concatenate(
        [
            jnp.where(high == 0, back_first, back_second),
            jnp.where(high == 0, back_second, back_first),
        ],
        0,
    ).T

    slot_spec = pl.BlockSpec((1, 1, edge, edge), lambda s: (0, s, 0, 0))
    slot_shape = jax.ShapeDtypeStruct(weights.shape, f32)
    slot_grads, new_weights, new_left, new_right, new_teacher_blocks = pl.pallas_call(
        shampoo_kernel,
        grid=(slots,),
        in_specs=[pl.BlockSpec((1, edge, edge), lambda s: (s, 0, 0))] + [slot_spec] * 6,
        out_specs=[slot_spec] * 5,
        out_shape=[slot_shape] * 5,
        compiler_params=compiled(),
        cost_estimate=cost(3e9, 22e6),
        name="shampoo",
    )(low_grads, weights, stats_left, stats_right, root_left, root_right, teacher_slot_blocks)
    new_embed, new_embed_m, new_embed_v = adamw(embed, embed_m, embed_v, embed_grad, 0.05, 0.05)
    new_enc, new_enc_m, new_enc_v = adamw(enc_vectors, enc_m, enc_v, enc_total, 0.5, 0.0)
    new_pred, new_pred_m, new_pred_v = adamw(pred_vectors, pred_m, pred_v, pred_total, 0.5, 0.0)
    new_teacher_embed = 0.7 * teacher_embed + 0.3 * new_embed
    new_teacher_vectors = 0.7 * teacher_vectors + 0.3 * new_enc
    return (
        loss_total,
        slot_grads,
        new_weights,
        new_left,
        new_right,
        new_teacher_blocks,
        new_embed,
        new_embed_m,
        new_embed_v,
        new_teacher_embed,
        new_enc,
        new_enc_m,
        new_enc_v,
        new_pred,
        new_pred_m,
        new_pred_v,
        new_teacher_vectors,
    )


def solution(mesh):
    blocks = P("tensor", "dp", None, None)
    table = P("tensor", "dp")
    in_specs = (
        (P("dp", None, "tensor"), P("dp", None), P("dp", None), P())
        + (blocks,) * 6
        + (table,) * 4
        + (P(),) * 7
    )
    out_specs = (P(),) + (blocks,) * 5 + (table,) * 4 + (P(),) * 7
    return jax.shard_map(shards, mesh=mesh, in_specs=in_specs, out_specs=out_specs, check_vma=False)
```

time: 951 us -> 635 us (0.67)
  the two profiles are of different devices: /device:TPU:0 before, /device:TPU:11 now
where the time goes in v2:
time: 635 us; the launch traced here: 623 us
  waiting for transfers between devices  178 us (28%)
  starting transfers between devices  167 us (26%)
  Pallas kernels  154 us (24%)
  other arithmetic  80.1 us (13%)
  local copies, waits for them, and re-layouts  31.9 us (5%)
  matrix products  7.94 us (1%)
    ppermute x31, waiting for transfers between devices, across(): return lax.ppermute(values, AXES, self.pairs(lambda d, z: (d, z ^ r), keep))  116 us
    pallas_call x1, Pallas kernels, shards(): pl.pallas_call(functools.partial(predictor_kernel, share, context_len, pl...  78.2 us
    ppermute x24, starting transfers between devices, stage(): lax.ppermute(values, AXES, self.pairs(target, lambda d, z: role is None o...  65.8 us
    ppermute x31, starting transfers between devices, across(): return lax.ppermute(values, AXES, self.pairs(lambda d, z: (d, z ^ r), keep))  60.5 us
    ppermute x24, waiting for transfers between devices, stage(): lax.ppermute(values, AXES, self.pairs(target, lambda d, z: role is None o...  49.9 us
    concatenate x12, other arithmetic, spread(): stack = jnp.concatenate([stack, self.stage(number, stack, role)], 1)  35.6 us
    all_to_all x1, starting transfers between devices, shards(): lax.all_to_all(slot_rows, 'dp', split_axis=0, concat_axis=1, tiled=False)  22.2 us
    pallas_call x1, Pallas kernels, shards(): pl.pallas_call(functools.partial(encoder_attend_back_kernel, edge, npatch...  21.5 us
  transfers between devices with their start and end apart: 64, of which 29 were waited for; matrix products, arithmetic and copies ran while one was open for 17% of the time, Pallas kernels for 8%

profile of v2, /device:TPU:11, one launch (start us, length us, event | category | flops | bytes accessed | tf_op | source)
XLA Modules:
  0.0 623.2 jit_solution(9524203840869751643)
XLA Ops:
  4.4 4.7 all-to-all-start
  10.0 3.3 collective-permute-start.3
  17.9 3.2 gather_fusion.5
  54.2 11.4 %collective-permute-done.17 = bf16[48,1536]{1,0:T(8,128)(2,1)S(1)} collective-permute-done((bf16[48,1536]{1,0:T(8,128)(2,1)S(1)}, bf16[48,1536]{1,0:T(8,128)(2,1)S(1)}, u32[]{:S(2)}, u32[]{:S(2)}) %collective-permute-start.17) | collective-permute-done | bytes 147488 | tf_op jit(solution)/shard_map/ppermute | solution.py:537
  73.5 10.4 %collective-permute-done.13 = bf16[48,1536]{1,0:T(8,128)(2,1)S(1)} collective-permute-done((bf16[48,1536]{1,0:T(8,128)(2,1)S(1)}, bf16[48,1536]{1,0:T(8,128)(2,1)S(1)}, u32[]{:S(2)}, u32[]{:S(2)}) %collective-permute-start.13) | collective-permute-done | bytes 147488 | tf_op jit(solution)/shard_map/ppermute | solution.py:537
  85.2 4.1 collective-permute-start.26
  91.0 17.5 %collective-permute-done.7 = bf16[48,1920]{1,0:T(8,128)(2,1)S(1)} collective-permute-done((bf16[48,1920]{1,0:T(8,128)(2,1)S(1)}, bf16[48,1920]{1,0:T(8,128)(2,1)S(1)}, u32[]{:S(2)}, u32[]{:S(2)}) %collective-permute-start.7) | collective-permute-done | bytes 184352 | tf_op jit(solution)/shard_map/ppermute | solution.py:537
  108.5 5.1 collective-permute-start.20
  114.6 5.7 collective-permute-start.14
  125.4 8.2 %collective-permute-start.21 = (bf16[4,96,1536]{2,1,0:T(8,128)(2,1)}, bf16[4,96,1536]{2,1,0:T(8,128)(2,1)}, u32[]{:S(2)}, u32[]{:S(2)}) collective-permute-start(bf16[4,96,1536]{2,1,0:T(8,128)(2,1)} %pad_maximum_fusion.12), channel_id=1, source_target_pairs={{0,16},{1,17},{2,18},{3,19},{4,12},{5,13},{6,14},{7,15},{8,24},{9,... | collective-permute-start | bytes 3538952 | tf_op jit(solution)/shard_map/ppermute | solution.py:525
  142.2 5.8 collective-permute-start.15
  149.2 5.7 collective-permute-start.9
  170.2 8.0 %collective-permute-done.9 = bf16[4,96,1920]{2,1,0:T(8,128)(2,1)} collective-permute-done((bf16[4,96,1920]{2,1,0:T(8,128)(2,1)}, bf16[4,96,1920]{2,1,0:T(8,128)(2,1)}, u32[]{:S(2)}, u32[]{:S(2)}) %collective-permute-start.9) | collective-permute-done | bytes 1474592 | tf_op jit(solution)/shard_map/ppermute | solution.py:525
  181.8 11.0 %collective-permute-start.2 = (bf16[512,192]{1,0:T(8,128)(2,1)S(1)}, bf16[512,192]{1,0:T(8,128)(2,1)S(1)}, u32[]{:S(2)}, u32[]{:S(2)}) collective-permute-start(bf16[512,192]{1,0:T(8,128)(2,1)S(1)} %copy-done.52), channel_id=1, source_target_pairs={{0,3},{1,2},{2,1},{3,0},{4,7},{5,6},{6,5},{7,4},{8,11},{9,10},{10,... | collective-permute-start | bytes 589832 | tf_op jit(solution)/shard_map/ppermute | solution.py:537
  193.9 11.2 %collective-permute-done.2 = bf16[512,192]{1,0:T(8,128)(2,1)S(1)} collective-permute-done((bf16[512,192]{1,0:T(8,128)(2,1)S(1)}, bf16[512,192]{1,0:T(8,128)(2,1)S(1)}, u32[]{:S(2)}, u32[]{:S(2)}) %collective-permute-start.2) | collective-permute-done | bytes 196640 | tf_op jit(solution)/shard_map/ppermute | solution.py:537
  207.4 3.6 pad_maximum_fusion.4
  213.6 4.9 pad_maximum_fusion.3.down_ref
  218.6 4.1 pad_maximum_fusion.2.up_ref
  222.6 4.2 pad_maximum_fusion.1.emb_ref.w_ref
  226.8 15.5 %encoder_attend.1 = (f32[512,768]{1,0:T(8,128)}, f32[256,768]{1,0:T(8,128)}, bf16[256,768]{1,0:T(8,128)(2,1)}, bf16[4,256,576]{2,1,0:T(8,128)(2,1)}, bf16[4,256,192]{2,1,0:T(8,128)(2,1)}) custom-call(s32[1]{0:T(128)} %bitcast.role_ref, bf16[4,512,192]{2,1,0:T(8,128)(2,1)} %pad_maximum_fusion.13.patch_ref, f32[512,768]{1,0:T(8,128)} %broadcast_add_fusion.base_ref, ...), custom_call_target="tpu_custom_call" | custom-call | flops 6000000000 | bytes 12000000 | tf_op jit(solution)/shard_map/encoder_attend/pallas_call | solution.py:731
  242.3 14.8 %encoder_feed.1 = (f32[256,768]{1,0:T(8,128)}, bf16[256,768]{1,0:T(8,128)(2,1)}, f32[4,256,768]{2,1,0:T(8,128)}, bf16[4,256,192]{2,1,0:T(8,128)(2,1)}, bf16[4,128,192]{2,1,0:T(8,128)(2,1)}) custom-call(f32[512,768]{1,0:T(8,128)} %get-tuple-element.46.mid_ref, bf16[4,384,1536]{2,1,0:T(8,128)(2,1)} %pad_maximum_fusion.2.up_ref, ...), custom_call_target="tpu_custom_call" | custom-call | flops 8000000000 | bytes 14000000 | tf_op jit(solution)/shard_map/encoder_feed/pallas_call | solution.py:764
  257.1 8.1 %collective-permute-start.23 = (bf16[4,256,192]{2,1,0:T(8,128)(2,1)}, bf16[4,256,192]{2,1,0:T(8,128)(2,1)S(1)}, u32[]{:S(2)}, u32[]{:S(2)}) collective-permute-start(bf16[4,256,192]{2,1,0:T(8,128)(2,1)} %get-tuple-element.47), channel_id=1, source_target_pairs={{0,2},{1,3},{4,6},{5,7},{8,10},{9,11},{12,14},{13,15},{16,18},{17,... | collective-permute-start | bytes 1179656 | tf_op jit(solution)/shard_map/ppermute | solution.py:537
  265.2 6.8 %pad_maximum_fusion.w_ref = bf16[4,384,2688]{2,1,0:T(8,128)(2,1)} fusion(bf16[4,192,2688]{2,1,0:T(8,128)(2,1)} %collective-permute-done.29, bf16[4,96,2688]{2,1,0:T(8,128)(2,1)} %collective-permute-done.28, bf16[4,48,2688]{2,1,0:T(8,128)(2,1)S(1)} %collective-permute-done.27, bf16[1,48,2688]{2,1,0:T(8,128)(2,1)S(1)} %bitcast.196, ...), kind=kLoop, calls=%fused_computation.7 | loop fusion | flops 57802752 | bytes 16515072 | tf_op jit(solution)/shard_map/concatenate | solution.py:550
  272.0 16.2 %collective-permute-done.23.feat_ref = bf16[4,256,192]{2,1,0:T(8,128)(2,1)S(1)} collective-permute-done((bf16[4,256,192]{2,1,0:T(8,128)(2,1)}, bf16[4,256,192]{2,1,0:T(8,128)(2,1)S(1)}, u32[]{:S(2)}, u32[]{:S(2)}) %collective-permute-start.23) | collective-permute-done | bytes 393248 | tf_op jit(solution)/shard_map/ppermute | solution.py:537
  289.0 78.2 %predictor.1 = (bf16[4,192,2688]{2,1,0:T(8,128)(2,1)}, bf16[4,192,2688]{2,1,0:T(8,128)(2,1)}, f32[16,384]{1,0:T(8,128)}, f32[8,128]{1,0:T(8,128)}, bf16[256,768]{1,0:T(8,128)(2,1)}) custom-call(bf16[4,256,192]{2,1,0:T(8,128)(2,1)} %copy-done.74, bf16[4,128,192]{2,1,0:T(8,128)(2,1)} %get-tuple-element.48.target_ref, f32[384,384]{1,0:T(8,128)} %add_select_fusion.base_ref, ...), custom_call_target="tpu_custom_call" | custom-call | flops 16000000000 | bytes 30000000 | tf_op jit(solution)/shard_map/predictor/pallas_call | solution.py:805
  368.4 12.0 %collective-permute-done.30.back_ref = bf16[256,768]{1,0:T(8,128)(2,1)S(1)} collective-permute-done((bf16[256,768]{1,0:T(8,128)(2,1)}, bf16[256,768]{1,0:T(8,128)(2,1)S(1)}, u32[]{:S(2)}, u32[]{:S(2)}) %collective-permute-start.30) | collective-permute-done | bytes 393248 | tf_op jit(solution)/shard_map/ppermute | solution.py:537
  381.2 13.8 %encoder_feed_back.1 = (bf16[4,192,1536]{2,1,0:T(8,128)(2,1)}, bf16[4,192,1536]{2,1,0:T(8,128)(2,1)}, bf16[4,192,1536]{2,1,0:T(8,128)(2,1)}, bf16[4,192,1536]{2,...) custom-call(bf16[256,768]{1,0:T(8,128)(2,1)} %copy-done.75, f32[256,768]{1,0:T(8,128)} %get-tuple-element.50.out_ref, ...), custom_call_target="tpu_custom_call" | custom-call | flops 8000000000 | bytes 25000000 | tf_op jit(solution)/shard_map/encoder_feed_back/pallas_call | solution.py:836
  395.0 3.2 collective-permute-start.48
  400.2 21.5 %encoder_attend_back.1 = (bf16[4,192,1920]{2,1,0:T(8,128)(2,1)}, bf16[4,192,1920]{2,1,0:T(8,128)(2,1)}, f32[8,768]{1,0:T(8,128)}) custom-call(s32[1]{0:T(128)} %bitcast.role_ref, f32[256,768]{1,0:T(8,128)} %get-tuple-element.54.grad_ref, f32[256,768]{1,0:T(8,128)} %get-tuple-element.55.resid_ref, bf16[256,768]{1,0:T(8,128)(2,1)} %get-tuple-element.56.normed_ref, ...), custom_call_target="tpu_custom_call" | custom-call | flops 6000000000 | bytes 20000000 | tf_op jit(solution)/shard_map/encoder_attend_back/pallas_call | solution.py:865
  434.9 3.9 collective-permute-start.33
  448.8 3.0 add_convert_fusion.2
  456.8 3.1 collective-permute-start.43
  462.9 6.3 %collective-permute-done.49 = bf16[4,96,1536]{2,1,0:T(8,128)(2,1)S(1)} collective-permute-done((bf16[4,96,1536]{2,1,0:T(8,128)(2,1)S(1)}, bf16[4,96,1536]{2,1,0:T(8,128)(2,1)S(1)}, u32[]{:S(2)}, u32[]{:S(2)}) %collective-permute-start.49) | collective-permute-done | bytes 1179680 | tf_op jit(solution)/shard_map/ppermute | solution.py:525
  472.1 12.3 %collective-permute-done.43 = bf16[4,96,1536]{2,1,0:T(8,128)(2,1)S(1)} collective-permute-done((bf16[4,96,1536]{2,1,0:T(8,128)(2,1)S(1)}, bf16[4,96,1536]{2,1,0:T(8,128)(2,1)S(1)}, u32[]{:S(2)}, u32[]{:S(2)}) %collective-permute-start.43) | collective-permute-done | bytes 1179680 | tf_op jit(solution)/shard_map/ppermute | solution.py:525
  487.0 3.3 add_convert_fusion
  493.7 13.4 %collective-permute-done.37 = bf16[4,96,1920]{2,1,0:T(8,128)(2,1)S(1)} collective-permute-done((bf16[4,96,1920]{2,1,0:T(8,128)(2,1)S(1)}, bf16[4,96,1920]{2,1,0:T(8,128)(2,1)S(1)}, u32[]{:S(2)}, u32[]{:S(2)}) %collective-permute-start.37) | collective-permute-done | bytes 1474592 | tf_op jit(solution)/shard_map/ppermute | solution.py:525
  512.2 9.8 %collective-permute-done.38 = bf16[4,48,1920]{2,1,0:T(8,128)(2,1)S(1)} collective-permute-done((bf16[4,48,1920]{2,1,0:T(8,128)(2,1)S(1)}, bf16[4,48,1920]{2,1,0:T(8,128)(2,1)S(1)}, u32[]{:S(2)}, u32[]{:S(2)}) %collective-permute-start.38) | collective-permute-done | bytes 737312 | tf_op jit(solution)/shard_map/ppermute | solution.py:525
  530.0 3.6 collective-permute-done.40
  536.8 5.2 collective-permute-start.52
  542.0 5.8 collective-permute-done.46
  554.7 5.8 collective-permute-done.53
  560.6 2.8 collective-permute-done.58
  563.5 6.7 %collective-permute-done.59 = bf16[48,2688]{1,0:T(8,128)(2,1)S(1)} collective-permute-done((bf16[48,2688]{1,0:T(8,128)(2,1)S(1)}, bf16[48,2688]{1,0:T(8,128)(2,1)S(1)}, u32[]{:S(2)}, u32[]{:S(2)}) %collective-permute-start.59) | collective-permute-done | bytes 258080 | tf_op jit(solution)/shard_map/ppermute | solution.py:537
  572.2 22.2 %all-to-all-start.1 = ((bf16[8,3,1,48,384]{4,3,1,2,0:T(8,128)(2,1)}), bf16[8,3,1,48,384]{4,3,1,2,0:T(8,128)(2,1)S(1)}, u32[]{:S(2)}, u32[]{:S(2)}) async-start(bf16[8,3,1,48,384]{4,3,1,2,0:T(8,128)(2,1)} %bitcast.79), calls=%async_computation.1 | async-start | bytes 1769472 | tf_op jit(solution)/shard_map/all_to_all | solution.py:929
  594.4 3.1 collective-permute-start.60
  597.5 3.3 collective-permute-start.61
  601.9 6.4 %collective-permute-done.60 = f32[48,192]{1,0:T(8,128)S(1)} collective-permute-done((f32[48,192]{1,0:T(8,128)S(1)}, f32[48,192]{1,0:T(8,128)S(1)}, u32[]{:S(2)}, u32[]{:S(2)}) %collective-permute-start.60) | collective-permute-done | bytes 36896 | tf_op jit(solution)/shard_map/ppermute | solution.py:936
  612.4 10.6 %shampoo.1 = (f32[1,3,384,384]{3,2,1,0:T(8,128)}, f32[1,3,384,384]{3,2,1,0:T(8,128)}, f32[1,3,384,384]{3,2,1,0:T(8,128)}, f32[1,3,384,384]{3,2,1,0:T(8,128)}, f32[1,3,384,384]{3,2,1,0:T(8,128)}) custom-call(bf16[3,384,384]{2,1,0:T(8,128)(2,1)} %bitcast.206, f32[1,3,384,384]{3,2,1,0:T(8,128)} %weight_ref.1, f32[1,3,384,384]{3,2,1,0:T(8,128)} %left_ref.1, ...), custom_call_target="tpu_custom_call" | custom-call | flops 3000000000 | bytes 22000000 | tf_op jit(solution)/shard_map/shampoo/pallas_call | solution.py:948
  (401 shorter events, 167.2 us)
Async XLA Ops:
  4.4 39.3 %all-to-all-start = ((bf16[1,2,3,8,48,384]{5,4,2,1,0,3:T(8,128)(2,1)}), bf16[1,2,3,8,48,384]{5,4,2,1,0,3:T(8,128)(2,1)S(1)}, u32[]{:S(2)}, u32[]{:S(2)}) async-start(bf16[1,2,3,8,48,384]{5,4,2,1,0,3:T(8,128)(2,1)} %copy.92), calls=%async_computation | async-start | bytes 3538944 | tf_op jit(solution)/shard_map/all_to_all | solution.py:627
  10.0 32.1 %collective-permute-start.3 = (bf16[2,48,192]{2,1,0:T(8,128)(2,1)}, bf16[2,48,192]{2,1,0:T(8,128)(2,1)}, u32[]{:S(2)}, u32[]{:S(2)}) collective-permute-start(bf16[2,48,192]{2,1,0:T(8,128)(2,1)} %get-tuple-element.181), channel_id=1, source_target_pairs={{0,0},{4,8},{8,16},{12,24},{16,4},{20,12},{24,20},{28,28},{1,1},{5... | collective-permute-start | bytes 110600 | tf_op jit(solution)/shard_map/ppermute | solution.py:646
  13.4 28.8 %collective-permute-start.4 = (bf16[2,48,192]{2,1,0:T(8,128)(2,1)}, bf16[2,48,192]{2,1,0:T(8,128)(2,1)}, u32[]{:S(2)}, u32[]{:S(2)}) collective-permute-start(bf16[2,48,192]{2,1,0:T(8,128)(2,1)} %get-tuple-element.182), channel_id=1, source_target_pairs={{0,4},{4,12},{8,20},{12,28},{16,0},{20,8},{24,16},{28,24},{1,5},{5... | collective-permute-start | bytes 110600 | tf_op jit(solution)/shard_map/ppermute | solution.py:647
  48.0 18.5 %collective-permute-start.18 = (bf16[48,1536]{1,0:T(8,128)(2,1)S(1)}, bf16[48,1536]{1,0:T(8,128)(2,1)S(1)}, u32[]{:S(2)}, u32[]{:S(2)}) collective-permute-start(bf16[48,1536]{1,0:T(8,128)(2,1)S(1)} %get-tuple-element.141), channel_id=1, source_target_pairs={{0,2},{1,3},{2,0},{3,1},{4,6},{5,7},{6,4},{7,5},{8,10},{9,11},{10,... | collective-permute-start | bytes 442376 | tf_op jit(solution)/shard_map/ppermute | solution.py:537
  50.4 19.3 %collective-permute-start.19 = (bf16[48,1536]{1,0:T(8,128)(2,1)S(1)}, bf16[48,1536]{1,0:T(8,128)(2,1)S(1)}, u32[]{:S(2)}, u32[]{:S(2)}) collective-permute-start(bf16[48,1536]{1,0:T(8,128)(2,1)S(1)} %get-tuple-element.141), channel_id=1, source_target_pairs={{0,3},{1,2},{2,1},{3,0},{4,7},{5,6},{6,5},{7,4},{8,11},{9,10},{10,... | collective-permute-start | bytes 442376 | tf_op jit(solution)/shard_map/ppermute | solution.py:537
  50.4 22.5 %collective-permute-start.12 = (bf16[48,1536]{1,0:T(8,128)(2,1)S(1)}, bf16[48,1536]{1,0:T(8,128)(2,1)S(1)}, u32[]{:S(2)}, u32[]{:S(2)}) collective-permute-start(bf16[48,1536]{1,0:T(8,128)(2,1)S(1)} %get-tuple-element.140), channel_id=1, source_target_pairs={{0,2},{1,3},{2,0},{3,1},{4,6},{5,7},{6,4},{7,5},{8,10},{9,11},{10,... | collective-permute-start | bytes 442376 | tf_op jit(solution)/shard_map/ppermute | solution.py:537
  52.6 31.3 %collective-permute-start.13 = (bf16[48,1536]{1,0:T(8,128)(2,1)S(1)}, bf16[48,1536]{1,0:T(8,128)(2,1)S(1)}, u32[]{:S(2)}, u32[]{:S(2)}) collective-permute-start(bf16[48,1536]{1,0:T(8,128)(2,1)S(1)} %get-tuple-element.140), channel_id=1, source_target_pairs={{0,3},{1,2},{2,1},{3,0},{4,7},{5,6},{6,5},{7,4},{8,11},{9,10},{10,... | collective-permute-start | bytes 442376 | tf_op jit(solution)/shard_map/ppermute | solution.py:537
  66.5 18.7 %collective-permute-start.5 = (bf16[48,1920]{1,0:T(8,128)(2,1)S(1)}, bf16[48,1920]{1,0:T(8,128)(2,1)S(1)}, u32[]{:S(2)}, u32[]{:S(2)}) collective-permute-start(bf16[48,1920]{1,0:T(8,128)(2,1)S(1)} %get-tuple-element.167), channel_id=1, source_target_pairs={{0,1},{1,0},{2,3},{3,2},{4,5},{5,4},{6,7},{7,6},{8,9},{9,8},{10,11... | collective-permute-start | bytes 552968 | tf_op jit(solution)/shard_map/ppermute | solution.py:537
  69.6 20.6 %collective-permute-start.6 = (bf16[48,1920]{1,0:T(8,128)(2,1)S(1)}, bf16[48,1920]{1,0:T(8,128)(2,1)S(1)}, u32[]{:S(2)}, u32[]{:S(2)}) collective-permute-start(bf16[48,1920]{1,0:T(8,128)(2,1)S(1)} %get-tuple-element.168), channel_id=1, source_target_pairs={{0,2},{1,3},{2,0},{3,1},{4,6},{5,7},{6,4},{7,5},{8,10},{9,11},{10,... | collective-permute-start | bytes 552968 | tf_op jit(solution)/shard_map/ppermute | solution.py:537
  69.8 38.7 %collective-permute-start.7 = (bf16[48,1920]{1,0:T(8,128)(2,1)S(1)}, bf16[48,1920]{1,0:T(8,128)(2,1)S(1)}, u32[]{:S(2)}, u32[]{:S(2)}) collective-permute-start(bf16[48,1920]{1,0:T(8,128)(2,1)S(1)} %get-tuple-element.168), channel_id=1, source_target_pairs={{0,3},{1,2},{2,1},{3,0},{4,7},{5,6},{6,5},{7,4},{8,11},{9,10},{10,... | collective-permute-start | bytes 552968 | tf_op jit(solution)/shard_map/ppermute | solution.py:537
  72.8 41.8 %collective-permute-start.24 = (bf16[48,2688]{1,0:T(8,128)(2,1)S(1)}, bf16[48,2688]{1,0:T(8,128)(2,1)S(1)}, u32[]{:S(2)}, u32[]{:S(2)}) collective-permute-start(bf16[48,2688]{1,0:T(8,128)(2,1)S(1)} %get-tuple-element.150), channel_id=1, source_target_pairs={{2,3},{3,2},{6,7},{7,6},{10,11},{11,10},{14,15},{15,14},{18,19},{1... | collective-permute-start | bytes 774152 | tf_op jit(solution)/shard_map/ppermute | solution.py:537
  83.9 36.4 %collective-permute-start.25 = (bf16[48,2688]{1,0:T(8,128)(2,1)S(1)}, bf16[48,2688]{1,0:T(8,128)(2,1)S(1)}, u32[]{:S(2)}, u32[]{:S(2)}) collective-permute-start(bf16[48,2688]{1,0:T(8,128)(2,1)S(1)} %get-tuple-element.150), channel_id=1, source_target_pairs={{0,2},{1,3},{4,6},{5,7},{8,10},{9,11},{12,14},{13,15},{16,18},{17,... | collective-permute-start | bytes 774152 | tf_op jit(solution)/shard_map/ppermute | solution.py:537
  85.2 36.3 %collective-permute-start.26 = (bf16[48,2688]{1,0:T(8,128)(2,1)S(1)}, bf16[48,2688]{1,0:T(8,128)(2,1)S(1)}, u32[]{:S(2)}, u32[]{:S(2)}) collective-permute-start(bf16[48,2688]{1,0:T(8,128)(2,1)S(1)} %get-tuple-element.150), channel_id=1, source_target_pairs={{0,3},{1,2},{4,7},{5,6},{8,11},{9,10},{12,15},{13,14},{16,19},{17,... | collective-permute-start | bytes 774152 | tf_op jit(solution)/shard_map/ppermute | solution.py:537
  90.2 91.6 %collective-permute-start.1 = (bf16[512,192]{1,0:T(8,128)(2,1)}, bf16[512,192]{1,0:T(8,128)(2,1)}, u32[]{:S(2)}, u32[]{:S(2)}) collective-permute-start(bf16[512,192]{1,0:T(8,128)(2,1)} %bitcast_select_fusion.1), channel_id=1, source_target_pairs={{0,2},{1,3},{2,0},{3,1},{4,6},{5,7},{6,4},{7,5},{8,10},{9,11},{10,... | collective-permute-start | bytes 589832 | tf_op jit(solution)/shard_map/ppermute | solution.py:537
  108.5 14.9 %collective-permute-start.20 = (bf16[4,48,1536]{2,1,0:T(8,128)(2,1)S(1)}, bf16[4,48,1536]{2,1,0:T(8,128)(2,1)S(1)}, u32[]{:S(2)}, u32[]{:S(2)}) collective-permute-start(bf16[4,48,1536]{2,1,0:T(8,128)(2,1)S(1)} %pad_maximum_fusion.17), channel_id=1, source_target_pairs={{0,8},{1,9},{2,10},{3,11},{4,20},{5,21},{6,22},{7,23},{8,0},{9,1},... | collective-permute-start | bytes 1769480 | tf_op jit(solution)/shard_map/ppermute | solution.py:525
  114.6 25.2 %collective-permute-start.14 = (bf16[4,48,1536]{2,1,0:T(8,128)(2,1)}, bf16[4,48,1536]{2,1,0:T(8,128)(2,1)}, u32[]{:S(2)}, u32[]{:S(2)}) collective-permute-start(bf16[4,48,1536]{2,1,0:T(8,128)(2,1)} %pad_maximum_fusion.16), channel_id=1, source_target_pairs={{0,8},{1,9},{2,10},{3,11},{4,20},{5,21},{6,22},{7,23},{8,0},{9,1},... | collective-permute-start | bytes 1769480 | tf_op jit(solution)/shard_map/ppermute | solution.py:525
  120.3 27.6 %collective-permute-start.8 = (bf16[4,48,1920]{2,1,0:T(8,128)(2,1)}, bf16[4,48,1920]{2,1,0:T(8,128)(2,1)S(1)}, u32[]{:S(2)}, u32[]{:S(2)}) collective-permute-start(bf16[4,48,1920]{2,1,0:T(8,128)(2,1)} %pad_maximum_fusion.15), channel_id=1, source_target_pairs={{0,8},{1,9},{2,10},{3,11},{4,20},{5,21},{6,22},{7,23},{8,0},{9,1},... | collective-permute-start | bytes 2211848 | tf_op jit(solution)/shard_map/ppermute | solution.py:525
  122.7 32.2 %collective-permute-start.27 = (bf16[4,48,2688]{2,1,0:T(8,128)(2,1)}, bf16[4,48,2688]{2,1,0:T(8,128)(2,1)S(1)}, u32[]{:S(2)}, u32[]{:S(2)}) collective-permute-start(bf16[4,48,2688]{2,1,0:T(8,128)(2,1)} %pad_maximum_fusion.14), channel_id=1, source_target_pairs={{2,10},{3,11},{6,22},{7,23},{10,2},{11,3},{14,30},{15,31},{18,26},... | collective-permute-start | bytes 3096584 | tf_op jit(solution)/shard_map/ppermute | solution.py:525
  125.4 33.2 %collective-permute-start.21 = (bf16[4,96,1536]{2,1,0:T(8,128)(2,1)}, bf16[4,96,1536]{2,1,0:T(8,128)(2,1)}, u32[]{:S(2)}, u32[]{:S(2)}) collective-permute-start(bf16[4,96,1536]{2,1,0:T(8,128)(2,1)} %pad_maximum_fusion.12), channel_id=1, source_target_pairs={{0,16},{1,17},{2,18},{3,19},{4,12},{5,13},{6,14},{7,15},{8,24},{9,... | collective-permute-start | bytes 3538952 | tf_op jit(solution)/shard_map/ppermute | solution.py:525
  142.2 26.1 %collective-permute-start.15 = (bf16[4,96,1536]{2,1,0:T(8,128)(2,1)}, bf16[4,96,1536]{2,1,0:T(8,128)(2,1)}, u32[]{:S(2)}, u32[]{:S(2)}) collective-permute-start(bf16[4,96,1536]{2,1,0:T(8,128)(2,1)} %pad_maximum_fusion.11), channel_id=1, source_target_pairs={{0,16},{1,17},{2,18},{3,19},{4,12},{5,13},{6,14},{7,15},{8,24},{9,... | collective-permute-start | bytes 3538952 | tf_op jit(solution)/shard_map/ppermute | solution.py:525
  149.2 29.0 %collective-permute-start.9 = (bf16[4,96,1920]{2,1,0:T(8,128)(2,1)}, bf16[4,96,1920]{2,1,0:T(8,128)(2,1)}, u32[]{:S(2)}, u32[]{:S(2)}) collective-permute-start(bf16[4,96,1920]{2,1,0:T(8,128)(2,1)} %pad_maximum_fusion.10), channel_id=1, source_target_pairs={{0,16},{1,17},{2,18},{3,19},{4,12},{5,13},{6,14},{7,15},{8,24},{9,... | collective-permute-start | bytes 4423688 | tf_op jit(solution)/shard_map/ppermute | solution.py:525
  156.5 50.9 %collective-permute-start.28 = (bf16[4,96,2688]{2,1,0:T(8,128)(2,1)}, bf16[4,96,2688]{2,1,0:T(8,128)(2,1)}, u32[]{:S(2)}, u32[]{:S(2)}) collective-permute-start(bf16[4,96,2688]{2,1,0:T(8,128)(2,1)} %pad_maximum_fusion.8), channel_id=1, source_target_pairs={{2,18},{3,19},{6,14},{7,15},{10,26},{11,27},{14,6},{15,7},{18,2},{... | collective-permute-start | bytes 6193160 | tf_op jit(solution)/shard_map/ppermute | solution.py:525
  161.2 52.4 %collective-permute-start.22 = (bf16[4,192,1536]{2,1,0:T(8,128)(2,1)}, bf16[4,192,1536]{2,1,0:T(8,128)(2,1)}, u32[]{:S(2)}, u32[]{:S(2)}) collective-permute-start(bf16[4,192,1536]{2,1,0:T(8,128)(2,1)} %pad_maximum_fusion.7), channel_id=1, source_target_pairs={{0,4},{1,5},{2,6},{3,7},{4,0},{5,1},{6,2},{7,3},{8,12},{9,13},{10,... | collective-permute-start | bytes 7077896 | tf_op jit(solution)/shard_map/ppermute | solution.py:525
  168.3 24.6 %collective-permute-start = (bf16[512,192]{1,0:T(8,128)(2,1)S(1)}, bf16[512,192]{1,0:T(8,128)(2,1)S(1)}, u32[]{:S(2)}, u32[]{:S(2)}) collective-permute-start(bf16[512,192]{1,0:T(8,128)(2,1)S(1)} %copy-done.51), channel_id=1, source_target_pairs={{0,1},{1,0},{2,3},{3,2},{4,5},{5,4},{6,7},{7,6},{8,9},{9,8},{10,11... | collective-permute-start | bytes 589832 | tf_op jit(solution)/shard_map/ppermute | solution.py:537
  178.2 40.3 %collective-permute-start.16 = (bf16[4,192,1536]{2,1,0:T(8,128)(2,1)S(1)}, bf16[4,192,1536]{2,1,0:T(8,128)(2,1)S(1)}, u32[]{:S(2)}, u32[]{:S(2)}) collective-permute-start(bf16[4,192,1536]{2,1,0:T(8,128)(2,1)S(1)} %pad_maximum_fusion.6), channel_id=1, source_target_pairs={{0,4},{1,5},{2,6},{3,7},{4,0},{5,1},{6,2},{7,3},{8,12},{9,13},{10,... | collective-permute-start | bytes 7077896 | tf_op jit(solution)/shard_map/ppermute | solution.py:525
  181.8 23.3 %collective-permute-start.2 = (bf16[512,192]{1,0:T(8,128)(2,1)S(1)}, bf16[512,192]{1,0:T(8,128)(2,1)S(1)}, u32[]{:S(2)}, u32[]{:S(2)}) collective-permute-start(bf16[512,192]{1,0:T(8,128)(2,1)S(1)} %copy-done.52), channel_id=1, source_target_pairs={{0,3},{1,2},{2,1},{3,0},{4,7},{5,6},{6,5},{7,4},{8,11},{9,10},{10,... | collective-permute-start | bytes 589832 | tf_op jit(solution)/shard_map/ppermute | solution.py:537
  192.9 29.8 %collective-permute-start.10 = (bf16[4,192,1920]{2,1,0:T(8,128)(2,1)S(1)}, bf16[4,192,1920]{2,1,0:T(8,128)(2,1)S(1)}, u32[]{:S(2)}, u32[]{:S(2)}) collective-permute-start(bf16[4,192,1920]{2,1,0:T(8,128)(2,1)S(1)} %pad_maximum_fusion.5), channel_id=1, source_target_pairs={{0,4},{1,5},{2,6},{3,7},{4,0},{5,1},{6,2},{7,3},{8,12},{9,13},{10,... | collective-permute-start | bytes 8847368 | tf_op jit(solution)/shard_map/ppermute | solution.py:525
  211.0 54.2 %collective-permute-start.29 = (bf16[4,192,2688]{2,1,0:T(8,128)(2,1)}, bf16[4,192,2688]{2,1,0:T(8,128)(2,1)}, u32[]{:S(2)}, u32[]{:S(2)}) collective-permute-start(bf16[4,192,2688]{2,1,0:T(8,128)(2,1)} %pad_maximum_fusion.4), channel_id=1, source_target_pairs={{2,6},{3,7},{6,2},{7,3},{10,14},{11,15},{14,10},{15,11},{18,22},{1... | collective-permute-start | bytes 12386312 | tf_op jit(solution)/shard_map/ppermute | solution.py:525
  257.1 31.1 %collective-permute-start.23 = (bf16[4,256,192]{2,1,0:T(8,128)(2,1)}, bf16[4,256,192]{2,1,0:T(8,128)(2,1)S(1)}, u32[]{:S(2)}, u32[]{:S(2)}) collective-permute-start(bf16[4,256,192]{2,1,0:T(8,128)(2,1)} %get-tuple-element.47), channel_id=1, source_target_pairs={{0,2},{1,3},{4,6},{5,7},{8,10},{9,11},{12,14},{13,15},{16,18},{17,... | collective-permute-start | bytes 1179656 | tf_op jit(solution)/shard_map/ppermute | solution.py:537
  395.0 53.8 %collective-permute-start.48 = (bf16[4,192,1536]{2,1,0:T(8,128)(2,1)}, bf16[4,192,1536]{2,1,0:T(8,128)(2,1)}, u32[]{:S(2)}, u32[]{:S(2)}) collective-permute-start(bf16[4,192,1536]{2,1,0:T(8,128)(2,1)} %get-tuple-element.67), channel_id=1, source_target_pairs={{0,4},{1,5},{4,0},{5,1},{8,12},{9,13},{12,8},{13,9},{16,20},{17,21... | collective-permute-start | bytes 7077896 | tf_op jit(solution)/shard_map/ppermute | solution.py:525
  398.1 56.1 %collective-permute-start.42 = (bf16[4,192,1536]{2,1,0:T(8,128)(2,1)}, bf16[4,192,1536]{2,1,0:T(8,128)(2,1)}, u32[]{:S(2)}, u32[]{:S(2)}) collective-permute-start(bf16[4,192,1536]{2,1,0:T(8,128)(2,1)} %get-tuple-element.65), channel_id=1, source_target_pairs={{0,4},{1,5},{4,0},{5,1},{8,12},{9,13},{12,8},{13,9},{16,20},{17,21... | collective-permute-start | bytes 7077896 | tf_op jit(solution)/shard_map/ppermute | solution.py:525
  421.7 38.2 %collective-permute-start.36 = (bf16[4,192,1920]{2,1,0:T(8,128)(2,1)}, bf16[4,192,1920]{2,1,0:T(8,128)(2,1)S(1)}, u32[]{:S(2)}, u32[]{:S(2)}) collective-permute-start(bf16[4,192,1920]{2,1,0:T(8,128)(2,1)} %get-tuple-element.63), channel_id=1, source_target_pairs={{0,4},{1,5},{4,0},{5,1},{8,12},{9,13},{12,8},{13,9},{16,20},{17,21... | collective-permute-start | bytes 8847368 | tf_op jit(solution)/shard_map/ppermute | solution.py:525
  424.1 62.8 %collective-permute-start.54 = (bf16[4,192,2688]{2,1,0:T(8,128)(2,1)}, bf16[4,192,2688]{2,1,0:T(8,128)(2,1)}, u32[]{:S(2)}, u32[]{:S(2)}) collective-permute-start(bf16[4,192,2688]{2,1,0:T(8,128)(2,1)} %get-tuple-element.69), channel_id=1, source_target_pairs={{2,6},{3,7},{6,2},{7,3},{10,14},{11,15},{14,10},{15,11},{18,22},{1... | collective-permute-start | bytes 12386312 | tf_op jit(solution)/shard_map/ppermute | solution.py:525
  451.9 17.4 %collective-permute-start.49 = (bf16[4,96,1536]{2,1,0:T(8,128)(2,1)S(1)}, bf16[4,96,1536]{2,1,0:T(8,128)(2,1)S(1)}, u32[]{:S(2)}, u32[]{:S(2)}) collective-permute-start(bf16[4,96,1536]{2,1,0:T(8,128)(2,1)S(1)} %slice.278), channel_id=1, source_target_pairs={{0,16},{1,17},{4,12},{5,13},{8,24},{9,25},{12,4},{13,5},{16,0},{17... | collective-permute-start | bytes 3538952 | tf_op jit(solution)/shard_map/ppermute | solution.py:525
  456.8 27.6 %collective-permute-start.43 = (bf16[4,96,1536]{2,1,0:T(8,128)(2,1)S(1)}, bf16[4,96,1536]{2,1,0:T(8,128)(2,1)S(1)}, u32[]{:S(2)}, u32[]{:S(2)}) collective-permute-start(bf16[4,96,1536]{2,1,0:T(8,128)(2,1)S(1)} %slice.270), channel_id=1, source_target_pairs={{0,16},{1,17},{4,12},{5,13},{8,24},{9,25},{12,4},{13,5},{16,0},{17... | collective-permute-start | bytes 3538952 | tf_op jit(solution)/shard_map/ppermute | solution.py:525
  460.7 46.4 %collective-permute-start.37 = (bf16[4,96,1920]{2,1,0:T(8,128)(2,1)S(1)}, bf16[4,96,1920]{2,1,0:T(8,128)(2,1)S(1)}, u32[]{:S(2)}, u32[]{:S(2)}) collective-permute-start(bf16[4,96,1920]{2,1,0:T(8,128)(2,1)S(1)} %slice.261), channel_id=1, source_target_pairs={{0,16},{1,17},{4,12},{5,13},{8,24},{9,25},{12,4},{13,5},{16,0},{17... | collective-permute-start | bytes 4423688 | tf_op jit(solution)/shard_map/ppermute | solution.py:525
  469.6 21.6 %collective-permute-start.50 = (bf16[4,48,1536]{2,1,0:T(8,128)(2,1)S(1)}, bf16[4,48,1536]{2,1,0:T(8,128)(2,1)S(1)}, u32[]{:S(2)}, u32[]{:S(2)}) collective-permute-start(bf16[4,48,1536]{2,1,0:T(8,128)(2,1)S(1)} %slice.280), channel_id=1, source_target_pairs={{0,8},{1,9},{4,20},{5,21},{8,0},{9,1},{12,28},{13,29},{16,24},{17,... | collective-permute-start | bytes 1769480 | tf_op jit(solution)/shard_map/ppermute | solution.py:525
  484.7 25.0 %collective-permute-start.44 = (bf16[4,48,1536]{2,1,0:T(8,128)(2,1)S(1)}, bf16[4,48,1536]{2,1,0:T(8,128)(2,1)S(1)}, u32[]{:S(2)}, u32[]{:S(2)}) collective-permute-start(bf16[4,48,1536]{2,1,0:T(8,128)(2,1)S(1)} %slice.272), channel_id=1, source_target_pairs={{0,8},{1,9},{4,20},{5,21},{8,0},{9,1},{12,28},{13,29},{16,24},{17,... | collective-permute-start | bytes 1769480 | tf_op jit(solution)/shard_map/ppermute | solution.py:525
  490.4 35.3 %collective-permute-start.55 = (bf16[4,96,2688]{2,1,0:T(8,128)(2,1)S(1)}, bf16[4,96,2688]{2,1,0:T(8,128)(2,1)S(1)}, u32[]{:S(2)}, u32[]{:S(2)}) collective-permute-start(bf16[4,96,2688]{2,1,0:T(8,128)(2,1)S(1)} %slice.286), channel_id=1, source_target_pairs={{2,18},{3,19},{6,14},{7,15},{10,26},{11,27},{14,6},{15,7},{18,2},{... | collective-permute-start | bytes 6193160 | tf_op jit(solution)/shard_map/ppermute | solution.py:525
  491.4 62.0 %collective-permute-start.51 = (bf16[48,1536]{1,0:T(8,128)(2,1)S(1)}, bf16[48,1536]{1,0:T(8,128)(2,1)S(1)}, u32[]{:S(2)}, u32[]{:S(2)}) collective-permute-start(bf16[48,1536]{1,0:T(8,128)(2,1)S(1)} %get-tuple-element.153), channel_id=1, source_target_pairs={{0,1},{1,0},{4,5},{5,4},{8,9},{9,8},{12,13},{13,12},{16,17},{17,16... | collective-permute-start | bytes 442376 | tf_op jit(solution)/shard_map/ppermute | solution.py:537
  507.6 14.3 %collective-permute-start.38 = (bf16[4,48,1920]{2,1,0:T(8,128)(2,1)S(1)}, bf16[4,48,1920]{2,1,0:T(8,128)(2,1)S(1)}, u32[]{:S(2)}, u32[]{:S(2)}) collective-permute-start(bf16[4,48,1920]{2,1,0:T(8,128)(2,1)S(1)} %slice.263), channel_id=1, source_target_pairs={{0,8},{1,9},{4,20},{5,21},{8,0},{9,1},{12,28},{13,29},{16,24},{17,... | collective-permute-start | bytes 2211848 | tf_op jit(solution)/shard_map/ppermute | solution.py:525
  510.0 26.8 %collective-permute-start.45 = (bf16[48,1536]{1,0:T(8,128)(2,1)S(1)}, bf16[48,1536]{1,0:T(8,128)(2,1)S(1)}, u32[]{:S(2)}, u32[]{:S(2)}) collective-permute-start(bf16[48,1536]{1,0:T(8,128)(2,1)S(1)} %get-tuple-element.156), channel_id=1, source_target_pairs={{0,1},{1,0},{4,5},{5,4},{8,9},{9,8},{12,13},{13,12},{16,17},{17,16... | collective-permute-start | bytes 442376 | tf_op jit(solution)/shard_map/ppermute | solution.py:537
  528.8 19.0 %collective-permute-start.46 = (bf16[48,1536]{1,0:T(8,128)(2,1)S(1)}, bf16[48,1536]{1,0:T(8,128)(2,1)S(1)}, u32[]{:S(2)}, u32[]{:S(2)}) collective-permute-start(bf16[48,1536]{1,0:T(8,128)(2,1)S(1)} %get-tuple-element.158), channel_id=1, source_target_pairs={{0,2},{1,3},{4,6},{5,7},{8,10},{9,11},{12,14},{13,15},{16,18},{17,... | collective-permute-start | bytes 442376 | tf_op jit(solution)/shard_map/ppermute | solution.py:537
  533.7 17.3 %collective-permute-start.47 = (bf16[48,1536]{1,0:T(8,128)(2,1)S(1)}, bf16[48,1536]{1,0:T(8,128)(2,1)S(1)}, u32[]{:S(2)}, u32[]{:S(2)}) collective-permute-start(bf16[48,1536]{1,0:T(8,128)(2,1)S(1)} %get-tuple-element.157), channel_id=1, source_target_pairs={{0,3},{1,2},{4,7},{5,6},{8,11},{9,10},{12,15},{13,14},{16,19},{17,... | collective-permute-start | bytes 442376 | tf_op jit(solution)/shard_map/ppermute | solution.py:537
  536.0 15.1 %collective-permute-start.56 = (bf16[4,48,2688]{2,1,0:T(8,128)(2,1)S(1)}, bf16[4,48,2688]{2,1,0:T(8,128)(2,1)S(1)}, u32[]{:S(2)}, u32[]{:S(2)}) collective-permute-start(bf16[4,48,2688]{2,1,0:T(8,128)(2,1)S(1)} %slice.288), channel_id=1, source_target_pairs={{2,10},{3,11},{6,22},{7,23},{10,2},{11,3},{14,30},{15,31},{18,26},... | collective-permute-start | bytes 3096584 | tf_op jit(solution)/shard_map/ppermute | solution.py:525
  536.8 17.9 %collective-permute-start.52 = (bf16[48,1536]{1,0:T(8,128)(2,1)S(1)}, bf16[48,1536]{1,0:T(8,128)(2,1)S(1)}, u32[]{:S(2)}, u32[]{:S(2)}) collective-permute-start(bf16[48,1536]{1,0:T(8,128)(2,1)S(1)} %get-tuple-element.155), channel_id=1, source_target_pairs={{0,2},{1,3},{4,6},{5,7},{8,10},{9,11},{12,14},{13,15},{16,18},{17,... | collective-permute-start | bytes 442376 | tf_op jit(solution)/shard_map/ppermute | solution.py:537
  553.4 16.8 %collective-permute-start.59 = (bf16[48,2688]{1,0:T(8,128)(2,1)S(1)}, bf16[48,2688]{1,0:T(8,128)(2,1)S(1)}, u32[]{:S(2)}, u32[]{:S(2)}) collective-permute-start(bf16[48,2688]{1,0:T(8,128)(2,1)S(1)} %get-tuple-element.144), channel_id=1, source_target_pairs={{2,1},{3,0},{6,5},{7,4},{10,9},{11,8},{14,13},{15,12},{18,17},{19,... | collective-permute-start | bytes 774152 | tf_op jit(solution)/shard_map/ppermute | solution.py:537
  572.2 39.2 %all-to-all-start.1 = ((bf16[8,3,1,48,384]{4,3,1,2,0:T(8,128)(2,1)}), bf16[8,3,1,48,384]{4,3,1,2,0:T(8,128)(2,1)S(1)}, u32[]{:S(2)}, u32[]{:S(2)}) async-start(bf16[8,3,1,48,384]{4,3,1,2,0:T(8,128)(2,1)} %bitcast.79), calls=%async_computation.1 | async-start | bytes 1769472 | tf_op jit(solution)/shard_map/all_to_all | solution.py:929
  (95 other events, 1661.4 us)

commit v3 on v2

--- a/solution.py
+++ b/solution.py
@@ -117,7 +117,8 @@
 
 
 def encoder_attend_kernel(
-    edge, unit, context, head_size, kept, role_ref, patch_ref, base_ref, emb_ref, w_ref, vec_ref,
+    edge, unit, context, head_size, kept,
+    role_ref, patch_ref, base_ref, emb_ref, order_ref, w_ref, vec_ref,
     mid_ref, resid_ref, normed_ref, rows_ref, att_ref, x_ref, h_ref,
 ):
     step = pl.program_id(0)
@@ -133,10 +134,11 @@
 
     @pl.when(step < groups)
     def _():
-        for r in range(side):
-            x_ref[:, r * edge : (r + 1) * edge] += nt_(
-                patch_ref[0], emb_ref[0, :, r * pix : (r + 1) * pix]
-            )
+        ordered = sum(
+            nn(order_ref[:, m * edge : (m + 1) * edge], emb_ref[0, :, m * pix : (m + 1) * pix])
+            for m in range(side)
+        ).astype(bf16)
+        x_ref[...] += nt_(patch_ref[0], ordered)
 
     @pl.when(step == groups - 1)
     def _():
@@ -206,17 +208,14 @@
             target_ref[t] = nn(picked, swap_ref[t]).astype(bf16)
 
 
-def put_halves(keep_ref, send_ref, t, columns, value):
-    middle = value.shape[0] // 2
-    low = value.astype(bf16)
-    keep_ref[t, :, columns] = low[:middle]
-    send_ref[t, :, columns] = low[middle:]
+def put(grad_ref, t, columns, value):
+    grad_ref[t, :, columns] = value.astype(bf16)
 
 
 def predictor_kernel(
     share, context, players, head_size, denominator,
     feat_ref, target_ref, base_ref, w_ref, vec_ref, swap_ref,
-    keep_ref, send_ref, vec_grad_ref, loss_ref, back_ref,
+    grad_ref, vec_grad_ref, loss_ref, back_ref,
     x_ref, mid_ref, h_ref, h2_ref, rows_ref, att_ref, hidden_ref, acc_ref, d_ref, low_ref, f_ref,
 ):
     groups = w_ref.shape[0]
@@ -275,7 +274,7 @@
         terms = jnp.where(size < 1.0, 0.5 * gap * gap, size - 0.5)
         total += jnp.sum(jnp.sum(terms, 1, keepdims=True), 0, keepdims=True)
         grad_pred = (jnp.clip(gap, -1.0, 1.0) * (1.0 / denominator)).astype(bf16)
-        put_halves(keep_ref, send_ref, t, out_cols, tn(f_ref[...], grad_pred))
+        put(grad_ref, t, out_cols, tn(f_ref[...], grad_pred))
         grad_f += nt_(grad_pred, out_w)
     loss_ref[...] = jnp.broadcast_to(total * (1.0 / denominator), loss_ref.shape)
     d_ref[...] = jnp.zeros_like(d_ref)
@@ -295,9 +294,9 @@
         def _(t, j=j):
             active, slope = gelu_parts(hidden_ref[j, t])
             low = low_ref[...]
-            put_halves(keep_ref, send_ref, t, span(3 * j + 2), tn(low, active.astype(bf16)))
+            put(grad_ref, t, span(3 * j + 2), tn(low, active.astype(bf16)))
             grad_hidden = (nn(low, w_ref[t, :, span(3 * j + 2)]) * slope).astype(bf16)
-            put_halves(keep_ref, send_ref, t, span(3 * j + 1), tn(h2_ref[j], grad_hidden))
+            put(grad_ref, t, span(3 * j + 1), tn(h2_ref[j], grad_hidden))
             acc_ref[...] += nt_(grad_hidden, w_ref[t, :, span(3 * j + 1)])
 
         grad, gain_g, shift_g = norm_backward(acc_ref[...], mid_ref[j], vec_ref[4 * j + 2 : 4 * j + 3])
@@ -315,7 +314,7 @@
             grad_att = nn(low, attn_w[:, 3 * columns :]).astype(bf16)
             grad_rows = attend_back(rows_ref[j, t], grad_att, head_size, length, None)
             grad_w = jnp.concatenate([tn(h_ref[j], grad_rows), tn(low, att_ref[j, t])], 1)
-            put_halves(keep_ref, send_ref, t, span(3 * j), grad_w)
+            put(grad_ref, t, span(3 * j), grad_w)
             acc_ref[...] += nt_(grad_rows, attn_w[:, : 3 * columns])
 
         grad, gain_g, shift_g = norm_backward(acc_ref[...], x_ref[j], vec_ref[4 * j : 4 * j + 1])
@@ -332,14 +331,14 @@
     ).astype(bf16)
     back = jnp.zeros((low.shape[0], swap_ref.shape[1]), f32)
     for t in range(groups):
-        put_halves(keep_ref, send_ref, t, in_cols, tn(low, feat_ref[t]))
+        put(grad_ref, t, in_cols, tn(low, feat_ref[t]))
         back += nt_(nn(low, w_ref[t, :, in_cols]).astype(bf16), swap_ref[t])
     back_ref[...] = back.astype(bf16)
 
 
 def encoder_feed_back_kernel(
     edge, back_ref, out_ref, mid_ref, normed_ref, hidden_ref, up_ref, down_ref, vec_ref,
-    up_keep, up_send, down_keep, down_send, grad_ref, vec_grad_ref, d_ref, low_ref, acc_ref,
+    up_grad, down_grad, grad_ref, vec_grad_ref, d_ref, low_ref, acc_ref,
 ):
     step = pl.program_id(0)
     groups = pl.num_programs(0)
@@ -365,8 +364,8 @@
     for r in range(2):
         mine = slice(r * edge, (r + 1) * edge)
         columns = slice(r * wide, (r + 1) * wide)
-        put_halves(down_keep, down_send, 0, columns, tn(low_ref[:, mine], active))
-        put_halves(up_keep, up_send, 0, columns, tn(normed_ref[:, mine], grad_hidden))
+        put(down_grad, 0, columns, tn(low_ref[:, mine], active))
+        put(up_grad, 0, columns, tn(normed_ref[:, mine], grad_hidden))
         acc_ref[:, mine] += nt_(grad_hidden, up_ref[0, :, columns])
 
     @pl.when(step == groups - 1)
@@ -379,8 +378,8 @@
 
 def encoder_attend_back_kernel(
     edge, unit, context, head_size,
-    role_ref, grad_ref, resid_ref, normed_ref, rows_ref, att_ref, w_ref, patch_ref, vec_ref,
-    keep_ref, send_ref, vec_grad_ref, low_ref, acc_ref,
+    role_ref, mid_grad_ref, resid_ref, normed_ref, rows_ref, att_ref, w_ref, patch_ref, order_ref,
+    vec_ref, grad_ref, vec_grad_ref, low_ref, acc_ref,
 ):
     step = pl.program_id(0)
     groups = pl.num_programs(0) // 2
@@ -390,7 +389,7 @@
 
     @pl.when(step == 0)
     def _():
-        low_ref[...] = grad_ref[...].astype(bf16)
+        low_ref[...] = mid_grad_ref[...].astype(bf16)
         acc_ref[...] = jnp.zeros_like(acc_ref)
 
     @pl.when(step < groups)
@@ -409,14 +408,14 @@
             grad_w = jnp.concatenate(
                 [tn(normed_ref[:, mine], grad_rows), tn(low_ref[:, mine], att_ref[0])], 1
             )
-            put_halves(keep_ref, send_ref, step, slice(r * wide, (r + 1) * wide), grad_w)
+            put(grad_ref, step, slice(r * wide, (r + 1) * wide), grad_w)
             acc_ref[:, mine] += nt_(grad_rows, w_ref[0, :, r * wide : r * wide + 3 * columns])
 
     @pl.when(step == groups - 1)
     def _():
         grad, gain_g, shift_g = norm_backward(acc_ref[...], resid_ref[...], vec_ref[0:1])
-        grad = grad_ref[...] + grad
-        low_ref[...] = grad.astype(bf16)
+        grad = mid_grad_ref[...] + grad
+        low_ref[...] = nn(grad.astype(bf16), order_ref[...]).astype(bf16)
         vec_grad_ref[...] = jnp.zeros_like(vec_grad_ref)
         vec_grad_ref[0:1] = gain_g
         vec_grad_ref[1:2] = shift_g
@@ -427,7 +426,7 @@
         grad_w = jnp.concatenate(
             [tn(low_ref[:, r * edge : (r + 1) * edge], patch_ref[0]) for r in range(2)], 1
         )
-        put_halves(keep_ref, send_ref, step - groups, slice(2 * wide, 2 * wide + 2 * pix), grad_w)
+        put(grad_ref, step - groups, slice(2 * wide, 2 * wide + 2 * pix), grad_w)
 
 
 def split(values):
@@ -456,6 +455,298 @@
     teacher_out[0, 0] = 0.7 * teacher_ref[0, 0] + 0.3 * new
 
 
+MESH = pl.DeviceIdType.MESH
+
+
+def flip(place, bits):
+    bit = 1
+    while bit <= bits:
+        if bits & bit:
+            place = place + bit * (1 - 2 * lax.rem(lax.div(place, bit), 2))
+        bit *= 2
+    return place
+
+
+def remote(source, target, send_sem, recv_sem, device):
+    return pltpu.make_async_remote_copy(
+        src_ref=source, dst_ref=target, send_sem=send_sem, recv_sem=recv_sem,
+        device_id=device, device_id_type=MESH,
+    )
+
+
+def greet(routes, d, z):
+    barrier = pltpu.get_barrier_semaphore()
+    peers = [(d, flip(z, r)) for r in range(1, routes.nt)]
+    peers += [routes.partner(s, d, z) for s in range(routes.stages + 1)]
+    for peer in peers:
+        pl.semaphore_signal(barrier, inc=1, device_id=peer, device_id_type=MESH)
+    pl.semaphore_wait(barrier, len(peers))
+
+
+def gather_kernel(
+    routes, widths, few_rows, own_ref, other_ref, pred_ref, patch_ref,
+    attn_ref, up_ref, down_ref, players_ref, rows_ref,
+    z_send, z_recv, local_sem, patch_send, patch_recv, stage_send, stage_recv,
+):
+    d, z = lax.axis_index("dp"), lax.axis_index("tensor")
+    nt, stages = routes.nt, routes.stages
+    role = lax.rem(z, 2)
+    mats = [attn_ref, up_ref, down_ref, players_ref]
+    starts = [sum(widths[:m]) for m in range(3)]
+    last = 3
+
+    def source(m, r):
+        if m == last:
+            return pred_ref
+        ref = own_ref if r % 2 == 0 else other_ref
+        return ref.at[:, pl.ds(starts[m], widths[m])]
+
+    def across(m, r):
+        return remote(
+            source(m, r), mats[m].at[r, 0], z_send.at[m, r], z_recv.at[m, r], (d, flip(z, r))
+        )
+
+    def local(m):
+        return pltpu.make_async_copy(source(m, 0), mats[m].at[0, 0], local_sem.at[m])
+
+    def patch(r, rows):
+        return remote(
+            patch_ref.at[r, pl.ds(0, rows)], rows_ref.at[r, pl.ds(0, rows)],
+            patch_send.at[r], patch_recv.at[r], (d, flip(z, r)),
+        )
+
+    def stage(m, r, s):
+        size = 1 << s
+        return remote(
+            mats[m].at[r, pl.ds(0, size)], mats[m].at[r, pl.ds(size, size)],
+            stage_send.at[m, r, s], stage_recv.at[m, r, s], routes.partner(s, d, z),
+        )
+
+    def when(m, r):
+        return role == 1 if m == last else None
+
+    def guarded(condition, body):
+        if condition is None:
+            body()
+        else:
+            pl.when(condition)(body)
+
+    greet(routes, d, z)
+    all_rows = patch_ref.shape[1]
+    own_patch = pltpu.make_async_copy(patch_ref.at[0], rows_ref.at[0], local_sem.at[last + 1])
+    for m in range(4):
+        guarded(when(m, 0), lambda m=m: local(m).start())
+        for r in range(1, nt):
+            to_role = lax.rem(flip(z, r), 2)
+            if m == last:
+                pl.when(to_role == 1)(lambda m=m, r=r: across(m, r).start())
+            else:
+                across(m, r).start()
+        if m == 0:
+            own_patch.start()
+            for r in range(1, nt):
+                to_role = lax.rem(flip(z, r), 2)
+                pl.when(to_role == 0)(lambda r=r: patch(r, few_rows).start())
+                pl.when(to_role == 1)(lambda r=r: patch(r, all_rows).start())
+
+    items = [(m, r) for m in range(4) for r in range(nt)]
+
+    def advance(m, r, s):
+        if s == 0:
+            if r == 0:
+                local(m).wait()
+            else:
+                across(m, r).wait_recv()
+        else:
+            stage(m, r, s - 1).wait_recv()
+        stage(m, r, s).start()
+
+    for n in range(len(items) + stages):
+        for s in reversed(range(stages + 1)):
+            if 0 <= n - s < len(items):
+                m, r = items[n - s]
+                guarded(when(m, r), lambda m=m, r=r, s=s: advance(m, r, s))
+
+    own_patch.wait()
+    for r in range(1, nt):
+        to_role = lax.rem(flip(z, r), 2)
+        pl.when(role == 0)(lambda r=r: patch(r, few_rows).wait_recv())
+        pl.when(role == 1)(lambda r=r: patch(r, all_rows).wait_recv())
+        pl.when(to_role == 0)(lambda r=r: patch(r, few_rows).wait_send())
+        pl.when(to_role == 1)(lambda r=r: patch(r, all_rows).wait_send())
+    for m, r in items:
+
+        def finish(m=m, r=r):
+            stage(m, r, stages).wait_recv()
+            for s in range(stages + 1):
+                stage(m, r, s).wait_send()
+
+        guarded(when(m, r), finish)
+        if r:
+            to_role = lax.rem(flip(z, r), 2)
+            if m == last:
+                pl.when(to_role == 1)(lambda m=m, r=r: across(m, r).wait_send())
+            else:
+                across(m, r).wait_send()
+
+
+def reduce_kernel(
+    routes, attn_cols, down_ref, up_ref, attn_ref, pred_ref, block_ref, emb_ref,
+    core0, core1, core2, later0, later1, later2, enc_in, pred_in, load,
+    load_sem, core_send, core_recv, stage_send, stage_recv, z_send, z_recv,
+):
+    d, z = lax.axis_index("dp"), lax.axis_index("tensor")
+    nt, stages = routes.nt, routes.stages
+    middle = routes.nd // 2
+    role = lax.rem(z, 2)
+    cores = [core0, core1, core2]
+    laters = [later0, later1, later2]
+    greet(routes, d, z)
+
+    def run(kind, sources, incoming, starts):
+        items = [(j, r) for j in range(len(sources)) for r in reversed(range(nt))]
+
+        def part(j, r, first):
+            ref, start, width = sources[j]
+            return ref.at[r, pl.ds(first, middle), :, pl.ds(start, width)]
+
+        def to_core(j, r):
+            return remote(
+                part(j, r, middle), cores[j].at[r, :, :, pl.ds(0, sources[j][2])],
+                core_send.at[j, r], core_recv.at[j, r], routes.partner(stages, d, z),
+            )
+
+        def own(i):
+            j, r = items[i]
+            return pltpu.make_async_copy(
+                part(j, r, 0), load.at[i % 2, :, :, pl.ds(0, sources[j][2])], load_sem.at[i % 2]
+            )
+
+        def stage(j, r, s):
+            size = 1 << s
+            return remote(
+                cores[j].at[r, pl.ds(size, size), :, pl.ds(0, sources[j][2])],
+                laters[j].at[r, pl.ds(size - 1, size), :, pl.ds(0, sources[j][2])],
+                stage_send.at[j, r, s], stage_recv.at[j, r, s], routes.partner(s, d, z),
+            )
+
+        def across(j, r):
+            return remote(
+                cores[j].at[r, 0, :, pl.ds(0, sources[j][2])],
+                incoming.at[r, :, pl.ds(starts[j], sources[j][2])],
+                z_send.at[kind, j, r], z_recv.at[kind, j, r], (d, flip(z, r)),
+            )
+
+        def add(i, q):
+            j, r = items[i]
+            width = sources[j][2]
+            if q == 0:
+                own(i).wait()
+                to_core(j, r).wait_recv()
+
+                @pl.loop(0, middle)
+                def _(k):
+                    total = cores[j][r, k, :, 0:width].astype(f32)
+                    total += load[i % 2, k, :, 0:width].astype(f32)
+                    cores[j][r, k, :, 0:width] = total.astype(bf16)
+
+                if i + 2 < len(items):
+                    own(i + 2).start()
+            else:
+                s = stages - q
+                stage(j, r, s).wait_recv()
+
+                @pl.loop(0, 1 << s)
+                def _(k):
+                    total = cores[j][r, k, :, 0:width].astype(f32)
+                    total += laters[j][r, k + ((1 << s) - 1), :, 0:width].astype(f32)
+                    cores[j][r, k, :, 0:width] = total.astype(bf16)
+
+            if q < stages:
+                stage(j, r, stages - q - 1).start()
+            elif r:
+                across(j, r).start()
+
+        for i in range(min(2, len(items))):
+            own(i).start()
+        for j, r in items:
+            to_core(j, r).start()
+        for n in range(len(items) + stages):
+            for q in reversed(range(stages + 1)):
+                if 0 <= n - q < len(items):
+                    add(n - q, q)
+        for j, r in items:
+            to_core(j, r).wait_send()
+            for s in range(stages):
+                stage(j, r, s).wait_send()
+            if r:
+                across(j, r).wait_send()
+
+    wide = down_ref.shape[3]
+    all_cols = attn_ref.shape[3]
+    pred_cols = pred_ref.shape[3]
+    encoder = [(down_ref, 0, wide), (up_ref, 0, wide), (attn_ref, 0, all_cols)]
+    encoder_at = [0, wide, 2 * wide]
+    players = [(pred_ref, 0, wide), (pred_ref, wide, pred_cols - wide)]
+    players_at = [0, wide]
+
+    @pl.when(role == 0)
+    def _():
+        run(0, encoder, enc_in, encoder_at)
+
+    @pl.when(role == 1)
+    def _():
+        run(1, players, pred_in, players_at)
+
+    def collect(kind, sources, incoming, starts, put):
+        for j, (_, _, width) in enumerate(sources):
+            place = incoming.at[:, :, pl.ds(starts[j], width)]
+
+            def arrive(r, j=j, width=width):
+                pltpu.make_async_remote_copy(
+                    src_ref=cores[j].at[r, 0, :, pl.ds(0, width)],
+                    dst_ref=incoming.at[r, :, pl.ds(starts[j], width)],
+                    send_sem=z_send.at[kind, j, r], recv_sem=z_recv.at[kind, j, r],
+                    device_id=(d, flip(z, r)), device_id_type=MESH,
+                ).wait_recv()
+
+            del place
+
+            @pl.when(role == kind)
+            def _(j=j, width=width, arrive=arrive):
+                total = cores[j][0, 0, :, 0:width].astype(f32)
+                for r in range(2, nt, 2):
+                    arrive(r)
+                    total += incoming[r, :, starts[j] : starts[j] + width].astype(f32)
+                put(j, total)
+
+            @pl.when(role != kind)
+            def _(j=j, width=width, arrive=arrive):
+                total = None
+                for r in range(1, nt, 2):
+                    arrive(r)
+                    got = incoming[r, :, starts[j] : starts[j] + width].astype(f32)
+                    total = got if total is None else total + got
+                put(j, total)
+
+    def put_encoder(j, total):
+        if j == 2:
+            block_ref[:, 0:attn_cols] = total[:, :attn_cols].astype(bf16)
+            emb_ref[...] = total[:, attn_cols:]
+        else:
+            first = attn_cols + (1 - j) * wide
+            block_ref[:, first : first + wide] = total.astype(bf16)
+
+    def put_players(j, total):
+        first = attn_cols + 2 * wide + players_at[j]
+        block_ref[:, first : first + total.shape[1]] = total.astype(bf16)
+
+    collect(1, players, pred_in, players_at, put_players)
+    collect(0, encoder, enc_in, encoder_at, put_encoder)
+    end = attn_cols + 2 * wide + pred_cols
+    block_ref[:, end:] = jnp.zeros((block_ref.shape[0], block_ref.shape[1] - end), bf16)
+
+
 def whole(shape):
     return pl.BlockSpec(shape, lambda *_: (0,) * len(shape))
 
@@ -500,7 +791,7 @@
 
 class Routes:
     def __init__(self, nd, nt):
-        self.nd, self.nt, self.half = nd, nt, nt // 2
+        self.nd, self.nt = nd, nt
         self.low_bits = [1 << s for s in range(1, nd.bit_length() - 1)]
         self.stages = len(self.low_bits)
 
@@ -516,23 +807,16 @@
                     found.append((d * self.nt + z, d2 * self.nt + z2))
         return found
 
-    def stage(self, number, values, role):
-        def target(d, z):
-            if number == self.stages:
-                return d ^ 1, z
-            return d ^ self.order(d & 1)[number], z
-
-        return lax.ppermute(
-            values,
-            AXES,
-            self.pairs(target, lambda d, z: role is None or z // self.half == role),
-        )
-
-    def across(self, r, values, from_role=None, to_role=None):
+    def partner(self, number, d, z):
+        if number == self.stages:
+            return flip(d, 1), z
+        core = lax.rem(d, 2)
+        ends = flip(d, self.order(0)[number]), flip(d, self.order(1)[number])
+        return ends[0] + core * (ends[1] - ends[0]), z
+
+    def across(self, r, values, from_role=None):
         def keep(d, z):
-            return (from_role is None or z // self.half == from_role) and (
-                to_role is None or (z ^ r) // self.half == to_role
-            )
+            return from_role is None or z % 2 == from_role
 
         return lax.ppermute(values, AXES, self.pairs(lambda d, z: (d, z ^ r), keep))
 
@@ -544,23 +828,6 @@
             bit = (place >> s) & 1
             held = held ^ (bit * jnp.where(core == 0, self.order(0)[s], self.order(1)[s]))
         return held
-
-    def spread(self, stack, role):
-        for number in range(self.stages + 1):
-            stack = jnp.concatenate([stack, self.stage(number, stack, role)], 1)
-        return stack
-
-    def reduce(self, keep, send, role, is_role):
-        for number in reversed(range(self.stages + 1)):
-            got = self.stage(number, send, role)
-            keep = (keep.astype(f32) + got.astype(f32)).astype(bf16)
-            if number:
-                middle = keep.shape[1] // 2
-                keep, send = keep[:, :middle], keep[:, middle:]
-        total = jnp.where(is_role, keep[0].astype(f32), 0.0)
-        for r in range(1, self.nt):
-            total = total + self.across(r, keep[r], from_role=role).astype(f32)
-        return total
 
     def total(self, values):
         for bit in [1] + self.low_bits:
@@ -603,7 +870,7 @@
     half = nt // 2
     d = lax.axis_index("dp")
     z = lax.axis_index("tensor")
-    role = z // half
+    role = z % 2
     student_role = role == 0
     images, npatches, pix_part = patches.shape
     slots = weights.shape[1]
@@ -629,51 +896,19 @@
     mine = by_slot[0][owner].transpose(1, 0, 2).reshape(rows_part, -1)
     teach = by_slot[1][owner[:teach_count]].transpose(1, 0, 2).reshape(rows_part, -1)
 
-    chunk = rows_part
-    wide_t = jnp.stack([embed, teacher_embed]).astype(bf16).transpose(0, 2, 1)
-    high = d // (nd // 2)
-    first = lax.dynamic_slice_in_dim(wide_t, high * chunk, chunk, 1)
-    second = lax.dynamic_slice_in_dim(wide_t, (1 - high) * chunk, chunk, 1)
-
-    def swap_pairs(flip, inverse):
-        found = []
-        for a in range(nd):
-            h = a // (nd // 2)
-            b = 2 * (a % (nd // 2)) + (h if not flip else 1 - h)
-            found.append((b, a) if inverse else (a, b))
-        return found
-
-    got_first = lax.ppermute(first, "dp", swap_pairs(False, False))
-    got_second = lax.ppermute(second, "dp", swap_pairs(True, False))
-    odd = d % 2
-    emb_rows = jnp.concatenate(
-        [
-            jnp.where(odd == 0, got_first, got_second),
-            jnp.where(odd == 0, got_second, got_first),
-        ],
-        2,
-    )
-
-    def gather_encoder(of_student, of_teacher):
-        own = jnp.where(student_role, of_student, of_teacher)
-        other = jnp.where(student_role, of_teacher, of_student)
-        parts = [own]
-        for r in range(1, nt):
-            parts.append(routes.across(r, own if r < half else other))
-        return routes.spread(jnp.stack(parts), None)
-
     mat = side * width
-    attn_emb = gather_encoder(
-        jnp.concatenate([mine[:, :mat], emb_rows[0]], 1),
-        jnp.concatenate([teach[:, :mat], emb_rows[1]], 1),
-    )
-    up_w = gather_encoder(mine[:, mat : 2 * mat], teach[:, mat : 2 * mat])
-    down_t = gather_encoder(mine[:, 2 * mat : 3 * mat], teach[:, 2 * mat :])
+
+    def embed_rows(values):
+        turned = values.astype(bf16).T.reshape(side, rows_part, pix_part)
+        return turned.transpose(1, 0, 2).reshape(rows_part, -1)
+
+    of_student = jnp.concatenate(
+        [mine[:, :mat], embed_rows(embed), mine[:, mat : 3 * mat]], 1
+    )
+    of_teacher = jnp.concatenate([teach[:, :mat], embed_rows(teacher_embed), teach[:, mat:]], 1)
+    own = jnp.where(student_role, of_student, of_teacher)
+    other = jnp.where(student_role, of_teacher, of_student)
     pred_own = mine[:, 3 * mat :]
-    pred_parts = [pred_own]
-    for r in range(1, nt):
-        pred_parts.append(routes.across(r, pred_own, to_role=1))
-    pred_all = routes.spread(jnp.stack(pred_parts), 1)
 
     holder = routes.holders(d)
     inside = jnp.arange(rows_part, dtype=jnp.int32)
@@ -692,25 +927,28 @@
     vec = jnp.pad(vec, ((0, 1), (0, 0)))
     pvec = to_local(pred_vectors, one_hot_p)
     pvec = jnp.pad(pvec, ((0, 16 - pvec.shape[0]), (0, 0)))
-    pred_z = half + z % half
+    pred_z = z - role + 1
     group_feat = (pred_z ^ jnp.arange(nt, dtype=jnp.int32))[:, None] * quarter + jnp.arange(
         quarter, dtype=jnp.int32
     )
+    emb_feat = jnp.concatenate(
+        [holder[:, None] * 2 * rows_part + m * rows_part + inside[None, :] for m in range(2)]
+    ).reshape(-1)
+    order = (feat[:, None] == emb_feat[None, :]).astype(bf16)
     swap = (feat[None, :, None] == group_feat[:, None, :]).astype(bf16)
 
-    part = z % half
-    picked = jnp.take_along_axis(patches, ctx_idx[:, :, None], 1)
+    part = z // 2
+    hot = (ctx_idx[:, :, None] == jnp.arange(npatches)[None, None, :]).astype(bf16)
+    picked = jnp.einsum("gcn,gnp->gcp", hot, patches, preferred_element_type=f32).astype(bf16)
 
     def rows_for(target_z):
-        where = (target_z % half) * share
-        ctx_rows = lax.dynamic_slice_in_dim(picked, where, share, 0).reshape(-1, pix_part)
-        all_rows = lax.dynamic_slice_in_dim(patches, where, share, 0).reshape(-1, pix_part)
-        padded = jnp.pad(ctx_rows, ((0, all_rows.shape[0] - ctx_rows.shape[0]), (0, 0)))
-        return jnp.where(target_z // half == 0, padded, all_rows)
-
-    patch_rows = jnp.stack(
-        [rows_for(z)] + [routes.across(r, rows_for(z ^ r)) for r in range(1, nt)]
-    )
+        where = (target_z // 2) * share
+        ctx = lax.dynamic_slice_in_dim(picked, where, share, 0).reshape(-1, pix_part)
+        every = lax.dynamic_slice_in_dim(patches, where, share, 0).reshape(-1, pix_part)
+        padded = jnp.pad(ctx, ((0, every.shape[0] - ctx.shape[0]), (0, 0)))
+        return jnp.where(target_z % 2 == 0, padded, every)
+
+    patch_out = jnp.stack([rows_for(z ^ r) for r in range(nt)])
     my_ctx = lax.dynamic_slice_in_dim(ctx_idx, part * share, share, 0)
     my_tgt = lax.dynamic_slice_in_dim(tgt_idx, part * share, share, 0)
     full_rows = share * npatches
@@ -723,11 +961,35 @@
     base = table[places] + vec[6]
     tgt_places = (my_tgt + npatches * jnp.arange(share, dtype=jnp.int32)[:, None]).reshape(-1)
     pick = (tgt_places[:, None] == jnp.arange(full_rows)[None, :]).astype(bf16)
+    widths = [mat + side * pix_part, mat, mat, mine.shape[1] - 3 * mat]
+    any_space = pl.BlockSpec(memory_space=pl.ANY)
+    dma = pltpu.SemaphoreType.DMA
+    attn_emb, up_w, down_t, pred_all, patch_rows = pl.pallas_call(
+        functools.partial(gather_kernel, routes, widths, ctx_rows),
+        in_specs=[any_space] * 4,
+        out_specs=[any_space] * 5,
+        out_shape=[jax.ShapeDtypeStruct((nt, nd, rows_part, c), bf16) for c in widths]
+        + [jax.ShapeDtypeStruct((nt, full_rows, pix_part), bf16)],
+        scratch_shapes=[
+            dma((4, nt)),
+            dma((4, nt)),
+            dma((5,)),
+            dma((nt,)),
+            dma((nt,)),
+            dma((4, nt, routes.stages + 1)),
+            dma((4, nt, routes.stages + 1)),
+        ],
+        compiler_params=pltpu.CompilerParams(collective_id=0, has_side_effects=True),
+        cost_estimate=cost(0, 50e6),
+        name="gather_weights",
+    )(own, other, pred_own, patch_out)
+    attn_emb, up_w, down_t, pred_all = (
+        value.reshape(nt, edge, -1) for value in (attn_emb, up_w, down_t, pred_all)
+    )
     role_word = role.astype(jnp.int32).reshape(1)
 
     attn_cols = side * width
     columns = width // nt
-    resid, normed_a, rows_a, att_a, middle = [None] * 5
     middle, resid, normed_a, rows_a, att_a = pl.pallas_call(
         functools.partial(encoder_attend_kernel, edge, npatches, context_len, HD, ctx_rows),
         grid=(2 * nt,),
@@ -739,6 +1001,7 @@
                 (1, edge, side * pix_part),
                 lambda i: (jnp.minimum(i, nt - 1), 0, attn_cols // (side * pix_part)),
             ),
+            whole((width, width)),
             pl.BlockSpec((1, edge, attn_cols), lambda i: (jnp.maximum(i - nt, 0), 0, 0)),
             whole((8, width)),
         ],
@@ -760,7 +1023,7 @@
         compiler_params=compiled(),
         cost_estimate=cost(6e9, 12e6),
         name="encoder_attend",
-    )(role_word, patch_rows, base, attn_emb, attn_emb, vec)
+    )(role_word, patch_rows, base, attn_emb, order, attn_emb, vec)
     output, normed_f, hidden, enc_feat, target = pl.pallas_call(
         functools.partial(encoder_feed_kernel, edge, ctx_rows),
         grid=(nt,),
@@ -792,7 +1055,7 @@
         name="encoder_feed",
     )(middle, up_w, down_t, vec, pick, swap)
 
-    feat_in = routes.across(half, enc_feat, from_role=0)
+    feat_in = routes.across(1, enc_feat, from_role=0)
     tokens_at = table_p[jnp.concatenate([my_ctx, my_tgt], 1)]
     mask_rows = jnp.arange(seq_len)[None, :, None] >= context_len
     tokens_at = jnp.where(mask_rows, tokens_at + pvec[4 * players + 2], tokens_at)
@@ -802,13 +1065,12 @@
     denominator = images * nd * target_len * width
     pred_columns = narrow // nt
     in_vmem = pl.BlockSpec(memory_space=VMEM)
-    pred_keep, pred_send, pred_vec_g, loss_tile, back = pl.pallas_call(
+    pred_grads, pred_vec_g, loss_tile, back = pl.pallas_call(
         functools.partial(predictor_kernel, share, context_len, players, PHD, denominator),
         in_specs=[in_vmem] * 6,
-        out_specs=[in_vmem] * 5,
+        out_specs=[in_vmem] * 4,
         out_shape=[
-            jax.ShapeDtypeStruct((nt, edge // 2, pred_cols), bf16),
-            jax.ShapeDtypeStruct((nt, edge // 2, pred_cols), bf16),
+            jax.ShapeDtypeStruct((nt, edge, pred_cols), bf16),
             jax.ShapeDtypeStruct((16, narrow), f32),
             jax.ShapeDtypeStruct((8, 128), f32),
             jax.ShapeDtypeStruct((ctx_rows, width), bf16),
@@ -830,10 +1092,10 @@
         cost_estimate=cost(16e9, 30e6),
         name="predictor",
     )(feat_in, target, tokens_at, pred_all, pvec, swap)
-    back = routes.across(half, back, from_role=1)
-
-    half_shape = jax.ShapeDtypeStruct((nt, edge // 2, mat), bf16)
-    up_keep, up_send, down_keep, down_send, grad_mid, vec_g1 = pl.pallas_call(
+    back = routes.across(1, back, from_role=1)
+
+    grad_shape = jax.ShapeDtypeStruct((nt, edge, mat), bf16)
+    up_g, down_g, grad_mid, vec_g1 = pl.pallas_call(
         functools.partial(encoder_feed_back_kernel, edge),
         grid=(nt,),
         in_specs=[
@@ -846,8 +1108,8 @@
             by_group((edge, mat)),
             whole((8, width)),
         ],
-        out_specs=[by_group((edge // 2, mat))] * 4 + [whole((ctx_rows, width)), whole((8, width))],
-        out_shape=[half_shape] * 4
+        out_specs=[by_group((edge, mat))] * 2 + [whole((ctx_rows, width)), whole((8, width))],
+        out_shape=[grad_shape] * 2
         + [
             jax.ShapeDtypeStruct((ctx_rows, width), f32),
             jax.ShapeDtypeStruct((8, width), f32),
@@ -862,7 +1124,7 @@
         name="encoder_feed_back",
     )(back, output, middle, normed_f, hidden, up_w, down_t, vec)
     all_cols = attn_cols + side * pix_part
-    attn_keep, attn_send, vec_g2 = pl.pallas_call(
+    attn_g, vec_g2 = pl.pallas_call(
         functools.partial(encoder_attend_back_kernel, edge, npatches, context_len, HD),
         grid=(2 * nt,),
         in_specs=[
@@ -874,28 +1136,57 @@
             pl.BlockSpec((1, ctx_rows, columns), lambda i: (jnp.minimum(i, nt - 1), 0, 0)),
             pl.BlockSpec((1, edge, attn_cols), lambda i: (jnp.minimum(i, nt - 1), 0, 0)),
             pl.BlockSpec((1, ctx_rows, pix_part), lambda i: (jnp.maximum(i - nt, 0), 0, 0)),
+            whole((width, width)),
             whole((8, width)),
         ],
         out_specs=[
-            whole((nt, edge // 2, all_cols)),
-            whole((nt, edge // 2, all_cols)),
+            whole((nt, edge, all_cols)),
             whole((8, width)),
         ],
         out_shape=[
-            jax.ShapeDtypeStruct((nt, edge // 2, all_cols), bf16),
-            jax.ShapeDtypeStruct((nt, edge // 2, all_cols), bf16),
+            jax.ShapeDtypeStruct((nt, edge, all_cols), bf16),
             jax.ShapeDtypeStruct((8, width), f32),
         ],
         scratch_shapes=[VMEM((ctx_rows, width), bf16), VMEM((ctx_rows, width), f32)],
         compiler_params=compiled(),
         cost_estimate=cost(6e9, 20e6),
         name="encoder_attend_back",
-    )(role_word, grad_mid, resid, normed_a, rows_a, att_a, attn_emb, patch_rows, vec)
-
-    pred_sum = routes.reduce(pred_keep, pred_send, 1, role == 1)
-    down_sum = routes.reduce(down_keep, down_send, 0, student_role)
-    up_sum = routes.reduce(up_keep, up_send, 0, student_role)
-    attn_emb_sum = routes.reduce(attn_keep, attn_send, 0, student_role)
+    )(role_word, grad_mid, resid, normed_a, rows_a, att_a, attn_emb, patch_rows, order, vec)
+
+    places = [g.reshape(nt, nd, rows_part, -1) for g in (down_g, up_g, attn_g, pred_grads)]
+    middle_size = nd // 2
+    by_block, emb_sum = pl.pallas_call(
+        functools.partial(reduce_kernel, routes, attn_cols),
+        in_specs=[any_space] * 4,
+        out_specs=[in_vmem] * 2,
+        out_shape=[
+            jax.ShapeDtypeStruct((rows_part, (block_count + 1) * edge), bf16),
+            jax.ShapeDtypeStruct((rows_part, side * pix_part), f32),
+        ],
+        scratch_shapes=[
+            VMEM((nt, middle_size, rows_part, mat), bf16),
+            VMEM((nt, middle_size, rows_part, mat), bf16),
+            VMEM((nt, middle_size, rows_part, all_cols), bf16),
+            VMEM((nt, middle_size - 1, rows_part, mat), bf16),
+            VMEM((nt, middle_size - 1, rows_part, mat), bf16),
+            VMEM((nt, middle_size - 1, rows_part, all_cols), bf16),
+            VMEM((nt, rows_part, 2 * mat + all_cols), bf16),
+            VMEM((nt, rows_part, pred_cols), bf16),
+            VMEM((2, middle_size, rows_part, all_cols), bf16),
+            dma((2,)),
+            dma((3, nt)),
+            dma((3, nt)),
+            dma((3, nt, routes.stages)),
+            dma((3, nt, routes.stages)),
+            dma((2, 3, nt)),
+            dma((2, 3, nt)),
+        ],
+        compiler_params=pltpu.CompilerParams(
+            collective_id=1, has_side_effects=True, vmem_limit_bytes=KERNEL_BYTES
+        ),
+        cost_estimate=cost(0, 60e6),
+        name="reduce_gradients",
+    )(*places)
 
     enc_rows = to_global(vec_g1[:7] + vec_g2[:7], one_hot)
     pred_rows = to_global(pred_vec_g[: 4 * players + 3], one_hot_p)
@@ -909,16 +1200,6 @@
     pred_total = packed[enc_rows.size : enc_rows.size + pred_rows.size].reshape(pred_rows.shape)
     loss_total = packed[enc_rows.size + pred_rows.size]
 
-    by_block = jnp.concatenate(
-        [
-            attn_emb_sum[:, :mat],
-            up_sum,
-            down_sum,
-            pred_sum,
-            jnp.zeros((rows_part, edge), f32),
-        ],
-        1,
-    ).astype(bf16)
     by_block = by_block.reshape(rows_part, block_count + 1, edge).transpose(1, 0, 2)
     slot_of = (
         jnp.full((slot_count,), block_count, jnp.int32)
@@ -929,19 +1210,8 @@
     slot_rows = lax.all_to_all(slot_rows, "dp", split_axis=0, concat_axis=1, tiled=False)
     low_grads = slot_rows.reshape(slots, edge, edge)
 
-    emb_sum = attn_emb_sum[:, mat:]
-    emb_halves = jnp.stack([emb_sum[:, :pix_part], emb_sum[:, pix_part:]])
-    send_first = lax.dynamic_index_in_dim(emb_halves, odd, 0, keepdims=False)
-    send_second = lax.dynamic_index_in_dim(emb_halves, 1 - odd, 0, keepdims=False)
-    back_first = lax.ppermute(send_first, "dp", swap_pairs(False, True))
-    back_second = lax.ppermute(send_second, "dp", swap_pairs(True, True))
-    embed_grad = jnp.concatenate(
-        [
-            jnp.where(high == 0, back_first, back_second),
-            jnp.where(high == 0, back_second, back_first),
-        ],
-        0,
-    ).T
+    embed_grad = emb_sum.reshape(rows_part, side, pix_part).transpose(1, 0, 2)
+    embed_grad = embed_grad.reshape(-1, pix_part).T
 
     slot_spec = pl.BlockSpec((1, 1, edge, edge), lambda s: (0, s, 0, 0))
     slot_shape = jax.ShapeDtypeStruct(weights.shape, f32)

time: 635 us -> 515 us (0.81)
  the two profiles are of different devices: /device:TPU:11 before, /device:TPU:0 now
where the time goes in v3:
time: 515 us; the launch traced here: 506 us
  Pallas kernels  362 us (70%)
  starting transfers between devices  56 us (11%)
  local copies, waits for them, and re-layouts  27.7 us (5%)
  waiting for transfers between devices  26.6 us (5%)
  other arithmetic  22.3 us (4%)
  matrix products  8.27 us (2%)
    pallas_call x1, Pallas kernels, shards(): pl.pallas_call(functools.partial(gather_kernel, routes, widths, ctx_rows)...  110 us
    pallas_call x1, Pallas kernels, shards(): pl.pallas_call(functools.partial(reduce_kernel, routes, attn_cols), in_sp...  95 us
    pallas_call x1, Pallas kernels, shards(): pl.pallas_call(functools.partial(predictor_kernel, share, context_len, pl...  78.2 us
    ppermute x4, starting transfers between devices, across(): return lax.ppermute(values, AXES, self.pairs(lambda d, z: (d, z ^ r), keep))  43.8 us
    pallas_call x1, Pallas kernels, shards(): pl.pallas_call(functools.partial(encoder_attend_back_kernel, edge, npatch...  21.9 us
    ppermute x4, waiting for transfers between devices, across(): return lax.ppermute(values, AXES, self.pairs(lambda d, z: (d, z ^ r), keep))  21.1 us
    pallas_call x1, Pallas kernels, shards(): pl.pallas_call(functools.partial(encoder_attend_kernel, edge, npatches, c...  18.5 us
    pallas_call x1, Pallas kernels, shards(): pl.pallas_call(functools.partial(encoder_feed_kernel, edge, ctx_rows), gr...  14.8 us
  transfers between devices with their start and end apart: 9, of which 7 were waited for; matrix products, arithmetic and copies ran while one was open for 9% of the time, Pallas kernels for 19%

profile of v3, /device:TPU:0, one launch (start us, length us, event | category | flops | bytes accessed | tf_op | source)
XLA Modules:
  0.0 505.8 jit_solution(16847224581580372600)
XLA Ops:
  0.7 1.7 convert.8
  3.0 1.4 copy.103
  4.4 5.3 %all-to-all-start = ((bf16[1,2,3,8,48,384]{5,4,2,1,0,3:T(8,128)(2,1)}), bf16[1,2,3,8,48,384]{5,4,2,1,0,3:T(8,128)(2,1)S(1)}, u32[]{:S(2)}, u32[]{:S(2)}) async-start(bf16[1,2,3,8,48,384]{5,4,2,1,0,3:T(8,128)(2,1)} %copy.103), calls=%async_computation | async-start | bytes 3538944 | tf_op jit(solution)/shard_map/all_to_all | solution.py:894
  14.5 1.0 copy.115
  15.6 1.0 copy.117
  19.0 1.2 fusion.1
  22.6 1.8 convolution_bitcast_fusion
  24.8 1.9 multiply_sine_fusion.1
  26.7 1.2 pad_maximum_fusion.1.patch_ref
  27.9 1.4 fusion.2
  31.9 2.6 gather_fusion.2
  35.3 1.0 multiply_sine_fusion.3
  37.0 1.3 compare_convert_fusion.1.order_ref
  38.3 1.5 compare_convert_fusion.swap_ref
  39.7 1.2 broadcast_add_fusion.base_ref
  41.4 0.8 gather_fusion
  42.3 0.8 gather_fusion.1
  44.0 1.9 broadcast_select_fusion
  45.8 109.6 %gather_weights.1 = (bf16[4,8,48,1920]{3,2,1,0:T(8,128)(2,1)}, bf16[4,8,48,1536]{3,2,1,0:T(8,128)(2,1)}, bf16[4,8,48,1536]{3,2,1,0:T(8,128)(2,1)}, bf16[4,8,48,2688]{3,2,1,0:T(8,128)(2,1)}, bf16[4,512,192]{2,1,0:T(8,128)(2,1)}) custom-call(bf16[48,4992]{1,0:T(8,128)(2,1)} %get-tuple-element.146.own_ref, bf16[48,4992]{1,0:T(8,128)(2,1)} %get-tuple-element.145.other_ref, ...), custom_call_target="tpu_custom_call" | custom-call | bytes 50000000 | tf_op jit(solution)/shard_map/gather_weights/pallas_call | solution.py:967
  155.4 18.5 %encoder_attend.1 = (f32[512,768]{1,0:T(8,128)}, f32[256,768]{1,0:T(8,128)}, bf16[256,768]{1,0:T(8,128)(2,1)}, bf16[4,256,576]{2,1,0:T(8,128)(2,1)}, bf16[4,256,192]{2,1,0:T(8,128)(2,1)}) custom-call(s32[1]{0:T(128)} %bitcast.role_ref, bf16[4,512,192]{2,1,0:T(8,128)(2,1)} %get-tuple-element.49.patch_ref, f32[512,768]{1,0:T(8,128)} %broadcast_add_fusion.base_ref, ...), custom_call_target="tpu_custom_call" | custom-call | flops 6000000000 | bytes 12000000 | tf_op jit(solution)/shard_map/encoder_attend/pallas_call | solution.py:993
  173.9 14.8 %encoder_feed.1 = (f32[256,768]{1,0:T(8,128)}, bf16[256,768]{1,0:T(8,128)(2,1)}, f32[4,256,768]{2,1,0:T(8,128)}, bf16[4,256,192]{2,1,0:T(8,128)(2,1)}, bf16[4,128,192]{2,1,0:T(8,128)(2,1)}) custom-call(f32[512,768]{1,0:T(8,128)} %get-tuple-element.51.mid_ref, bf16[4,384,1536]{2,1,0:T(8,128)(2,1)} %bitcast.136, bf16[4,384,1536]{2,1,0:T(8,128)(2,1)} %bitcast.138, ...), custom_call_target="tpu_custom_call" | custom-call | flops 8000000000 | bytes 14000000 | tf_op jit(solution)/shard_map/encoder_feed/pallas_call | solution.py:1027
  188.7 41.4 %collective-permute-start = (bf16[4,256,192]{2,1,0:T(8,128)(2,1)}, bf16[4,256,192]{2,1,0:T(8,128)(2,1)S(1)}, u32[]{:S(2)}, u32[]{:S(2)}) collective-permute-start(bf16[4,256,192]{2,1,0:T(8,128)(2,1)} %get-tuple-element.54), channel_id=1, source_target_pairs={{0,1},{2,3},{4,5},{6,7},{8,9},{10,11},{12,13},{14,15},{16,17},{18,... | collective-permute-start | bytes 1179656 | tf_op jit(solution)/shard_map/ppermute | solution.py:821
  230.8 1.7 gather_fusion.3
  232.6 0.9 add_select_fusion.base_ref
  233.5 8.2 %collective-permute-done.feat_ref = bf16[4,256,192]{2,1,0:T(8,128)(2,1)S(1)} collective-permute-done((bf16[4,256,192]{2,1,0:T(8,128)(2,1)}, bf16[4,256,192]{2,1,0:T(8,128)(2,1)S(1)}, u32[]{:S(2)}, u32[]{:S(2)}) %collective-permute-start) | collective-permute-done | bytes 393248 | tf_op jit(solution)/shard_map/ppermute | solution.py:821
  241.7 0.8 copy-done.24
  242.5 78.2 %predictor.1 = (bf16[4,384,2688]{2,1,0:T(8,128)(2,1)}, f32[16,384]{1,0:T(8,128)}, f32[8,128]{1,0:T(8,128)}, bf16[256,768]{1,0:T(8,128)(2,1)}) custom-call(bf16[4,256,192]{2,1,0:T(8,128)(2,1)} %copy-done.24, bf16[4,128,192]{2,1,0:T(8,128)(2,1)} %get-tuple-element.55.target_ref, f32[384,384]{1,0:T(8,128)} %add_select_fusion.base_ref, ...), custom_call_target="tpu_custom_call" | custom-call | flops 16000000000 | bytes 30000000 | tf_op jit(solution)/shard_map/predictor/pallas_call | solution.py:1068
  320.7 1.3 collective-permute-start.1
  322.0 1.1 convolution_select_fusion
  323.1 1.2 slice.70
  324.9 8.4 %collective-permute-done.1.back_ref = bf16[256,768]{1,0:T(8,128)(2,1)S(1)} collective-permute-done((bf16[256,768]{1,0:T(8,128)(2,1)}, bf16[256,768]{1,0:T(8,128)(2,1)S(1)}, u32[]{:S(2)}, u32[]{:S(2)}) %collective-permute-start.1) | collective-permute-done | bytes 393248 | tf_op jit(solution)/shard_map/ppermute | solution.py:821
  334.1 13.9 %encoder_feed_back.1 = (bf16[4,384,1536]{2,1,0:T(8,128)(2,1)}, bf16[4,384,1536]{2,1,0:T(8,128)(2,1)}, f32[256,768]{1,0:T(8,128)}, f32[8,768]{1,0:T(8,128)}) custom-call(bf16[256,768]{1,0:T(8,128)(2,1)} %copy-done.25, f32[256,768]{1,0:T(8,128)} %get-tuple-element.58.out_ref, f32[512,768]{1,0:T(8,128)} %get-tuple-element.51.mid_ref, ...), custom_call_target="tpu_custom_call" | custom-call | flops 8000000000 | bytes 25000000 | tf_op jit(solution)/shard_map/encoder_feed_back/pallas_call | solution.py:1098
  348.0 21.9 %encoder_attend_back.1 = (bf16[4,384,1920]{2,1,0:T(8,128)(2,1)}, f32[8,768]{1,0:T(8,128)}) custom-call(s32[1]{0:T(128)} %bitcast.role_ref, f32[256,768]{1,0:T(8,128)} %get-tuple-element.62.mid_grad_ref, f32[256,768]{1,0:T(8,128)} %get-tuple-element.63.resid_ref, bf16[256,768]{1,0:T(8,128)(2,1)} %get-tuple-element.64.normed_ref, ...), custom_call_target="tpu_custom_call" | custom-call | flops 6000000000 | bytes 20000000 | tf_op jit(solution)/shard_map/encoder_attend_back/pallas_call | solution.py:1127
  369.9 1.6 fusion.6
  371.7 0.8 scatter_custom_fusion
  372.9 1.5 collective-permute-start.3
  374.4 2.5 collective-permute-done.3
  377.0 1.5 collective-permute-start.4
  378.5 95.0 %reduce_gradients.1 = (bf16[48,7680]{1,0:T(8,128)(2,1)}, f32[48,384]{1,0:T(8,128)}) custom-call(bf16[4,8,48,1536]{3,2,1,0:T(8,128)(2,1)} %bitcast.105, bf16[4,8,48,1536]{3,2,1,0:T(8,128)(2,1)} %bitcast.104, bf16[4,8,48,1920]{3,2,1,0:T(8,128)(2,1)} %bitcast.103, bf16[4,8,48,2688]{3,2,1,0:T(8,128)(2,1)} %bitcast.101), custom_call_target="tpu_custom_call" | custom-call | bytes 60000000 | tf_op jit(solution)/shard_map/reduce_gradients/pallas_call | solution.py:1158
  473.5 1.2 copy.138
  474.7 1.6 gather_fusion.4
  476.4 3.8 all-to-all-start.1
  480.7 3.6 collective-permute-done.5
  484.4 1.0 collective-permute-start.6
  488.5 0.9 collective-permute-done.6
  491.2 2.5 all-to-all-done.1
  493.8 1.0 copy.121
  494.8 10.6 %shampoo.1 = (f32[1,3,384,384]{3,2,1,0:T(8,128)}, f32[1,3,384,384]{3,2,1,0:T(8,128)}, f32[1,3,384,384]{3,2,1,0:T(8,128)}, f32[1,3,384,384]{3,2,1,0:T(8,128)}, f32[1,3,384,384]{3,2,1,0:T(8,128)}) custom-call(bf16[3,384,384]{2,1,0:T(8,128)(2,1)} %bitcast.107, f32[1,3,384,384]{3,2,1,0:T(8,128)} %weight_ref.1, f32[1,3,384,384]{3,2,1,0:T(8,128)} %left_ref.1, ...), custom_call_target="tpu_custom_call" | custom-call | flops 3000000000 | bytes 22000000 | tf_op jit(solution)/shard_map/shampoo/pallas_call | solution.py:1218
  (156 shorter events, 23.2 us)
Async XLA Ops:
  0.7 2.0 copy-start
  4.4 5.3 %copy-start.26 = (s32[19]{0:T(128)S(1)}, s32[19]{0:T(128)}, u32[]{:S(2)}) copy-start(s32[19]{0:T(128)} %param.24) | copy-start | bytes 232
  4.4 8.0 %copy-start.2 = (bf16[4,256,192]{1,2,0:T(8,128)(2,1)S(1)}, bf16[4,256,192]{1,2,0:T(8,128)(2,1)}, u32[]{:S(2)}) copy-start(bf16[4,256,192]{1,2,0:T(8,128)(2,1)} %param.21) | copy-start | bytes 1179652
  4.4 8.0 %copy-start.21 = (s32[4,128]{1,0:T(4,128)S(1)}, s32[4,128]{1,0:T(4,128)}, u32[]{:S(2)}) copy-start(s32[4,128]{1,0:T(4,128)} %param.22) | copy-start | bytes 6148
  4.4 36.6 %all-to-all-start = ((bf16[1,2,3,8,48,384]{5,4,2,1,0,3:T(8,128)(2,1)}), bf16[1,2,3,8,48,384]{5,4,2,1,0,3:T(8,128)(2,1)S(1)}, u32[]{:S(2)}, u32[]{:S(2)}) async-start(bf16[1,2,3,8,48,384]{5,4,2,1,0,3:T(8,128)(2,1)} %copy.103), calls=%async_computation | async-start | bytes 3538944 | tf_op jit(solution)/shard_map/all_to_all | solution.py:894
  9.7 7.2 %copy-start.22 = (s32[19]{0:T(128)}, s32[19]{0:T(128)S(1)}, u32[]{:S(2)}) copy-start(s32[19]{0:T(128)S(1)} %compare_select_fusion.4) | copy-start | bytes 232
  10.2 14.6 %copy-start.18 = (f32[256]{0:T(256)}, f32[256]{0:T(256)S(1)}, u32[]{:S(2)}) copy-start(f32[256]{0:T(256)S(1)} %get-tuple-element.172) | copy-start | bytes 3076
  13.3 4.2 copy-start.23
  13.3 5.6 %copy-start.10 = (f32[7,768]{1,0:T(8,128)S(1)}, f32[7,768]{1,0:T(8,128)}, u32[]{:S(2)}) copy-start(f32[7,768]{1,0:T(8,128)} %param.35) | copy-start | bytes 64516
  16.9 7.9 %copy-start.20 = (f32[192]{0:T(256)S(1)}, f32[192]{0:T(256)}, u32[]{:S(2)}) copy-start(f32[192]{0:T(256)} %negate_power_fusion) | copy-start | bytes 2308
  27.9 1.5 copy-start.4
  27.9 2.4 copy-start.5
  31.9 3.3 copy-start.19
  36.3 3.5 copy-start.1
  42.3 1.7 copy-start.3
  173.9 56.3 %copy-start.9 = (f32[11,384]{1,0:T(8,128)S(1)}, f32[11,384]{1,0:T(8,128)}, u32[]{:S(2)}) copy-start(f32[11,384]{1,0:T(8,128)} %convolution_bitcast_fusion) | copy-start | bytes 50692
  188.7 53.0 %collective-permute-start = (bf16[4,256,192]{2,1,0:T(8,128)(2,1)}, bf16[4,256,192]{2,1,0:T(8,128)(2,1)S(1)}, u32[]{:S(2)}, u32[]{:S(2)}) collective-permute-start(bf16[4,256,192]{2,1,0:T(8,128)(2,1)} %get-tuple-element.54), channel_id=1, source_target_pairs={{0,1},{2,3},{4,5},{6,7},{8,9},{10,11},{12,13},{14,15},{16,17},{18,... | collective-permute-start | bytes 1179656 | tf_op jit(solution)/shard_map/ppermute | solution.py:821
  241.7 0.8 copy-start.24
  320.7 12.7 %collective-permute-start.1 = (bf16[256,768]{1,0:T(8,128)(2,1)}, bf16[256,768]{1,0:T(8,128)(2,1)S(1)}, u32[]{:S(2)}, u32[]{:S(2)}) collective-permute-start(bf16[256,768]{1,0:T(8,128)(2,1)} %get-tuple-element.57), channel_id=1, source_target_pairs={{1,0},{3,2},{5,4},{7,6},{9,8},{11,10},{13,12},{15,14},{17,16},{19,... | collective-permute-start | bytes 1179656 | tf_op jit(solution)/shard_map/ppermute | solution.py:821
  333.4 0.8 copy-start.25
  348.0 21.9 %copy-start.27 = (f32[8,768]{1,0:T(8,128)S(1)}, f32[8,768]{1,0:T(8,128)}, u32[]{:S(2)}) copy-start(f32[8,768]{1,0:T(8,128)} %get-tuple-element.61) | copy-start | bytes 73732
  371.6 1.3 collective-permute-start.2
  372.9 4.1 collective-permute-start.3
  377.0 103.3 %collective-permute-start.4 = (f32[80,128]{1,0:T(8,128)S(1)}, f32[80,128]{1,0:T(8,128)S(1)}, u32[]{:S(2)}, u32[]{:S(2)}) collective-permute-start(f32[80,128]{1,0:T(8,128)S(1)} %fusion.65), channel_id=1, source_target_pairs={{0,16},{1,17},{2,18},{3,19},{4,20},{5,21},{6,22},{7,23},{8,24},{9,... | collective-permute-start | bytes 122888 | tf_op jit(solution)/shard_map/ppermute | solution.py:834
  474.7 5.7 %copy-start.6 = (f32[192,96]{1,0:T(8,128)S(1)}, f32[192,96]{1,0:T(8,128)}, u32[]{:S(2)}) copy-start(f32[192,96]{1,0:T(8,128)} %param.32) | copy-start | bytes 221188
  474.7 5.8 %copy-start.7 = (f32[192,96]{1,0:T(8,128)S(1)}, f32[192,96]{1,0:T(8,128)}, u32[]{:S(2)}) copy-start(f32[192,96]{1,0:T(8,128)} %param.33) | copy-start | bytes 221188
  474.7 5.8 %copy-start.8 = (f32[48,384]{1,0:T(8,128)S(1)}, f32[48,384]{1,0:T(8,128)}, u32[]{:S(2)}) copy-start(f32[48,384]{1,0:T(8,128)} %get-tuple-element.80) | copy-start | bytes 221188
  476.4 17.4 %all-to-all-start.1 = ((bf16[8,3,1,48,384]{4,3,1,2,0:T(8,128)(2,1)}), bf16[8,3,1,48,384]{4,3,1,2,0:T(8,128)(2,1)S(1)}, u32[]{:S(2)}, u32[]{:S(2)}) async-start(bf16[8,3,1,48,384]{4,3,1,2,0:T(8,128)(2,1)} %bitcast.51), calls=%async_computation.1 | async-start | bytes 1769472 | tf_op jit(solution)/shard_map/all_to_all | solution.py:1210
  480.2 9.7 %copy-start.15 = (f32[11,384]{1,0:T(8,128)S(1)}, f32[11,384]{1,0:T(8,128)}, u32[]{:S(2)}) copy-start(f32[11,384]{1,0:T(8,128)} %param.38) | copy-start | bytes 50692
  480.2 9.7 %copy-start.16 = (f32[11,384]{1,0:T(8,128)S(1)}, f32[11,384]{1,0:T(8,128)}, u32[]{:S(2)}) copy-start(f32[11,384]{1,0:T(8,128)} %param.39) | copy-start | bytes 50692
  480.2 9.7 %copy-start.17 = (f32[11,384]{1,0:T(8,128)S(1)}, f32[11,384]{1,0:T(8,128)}, u32[]{:S(2)}) copy-start(f32[11,384]{1,0:T(8,128)} %param.40) | copy-start | bytes 50692
  480.2 10.3 %copy-start.11 = (f32[7,768]{1,0:T(8,128)S(1)}, f32[7,768]{1,0:T(8,128)}, u32[]{:S(2)}) copy-start(f32[7,768]{1,0:T(8,128)} %param.35) | copy-start | bytes 64516
  480.2 10.3 %copy-start.12 = (f32[7,768]{1,0:T(8,128)S(1)}, f32[7,768]{1,0:T(8,128)}, u32[]{:S(2)}) copy-start(f32[7,768]{1,0:T(8,128)} %param.41) | copy-start | bytes 64516
  480.2 10.3 %copy-start.13 = (f32[7,768]{1,0:T(8,128)S(1)}, f32[7,768]{1,0:T(8,128)}, u32[]{:S(2)}) copy-start(f32[7,768]{1,0:T(8,128)} %param.36) | copy-start | bytes 64516
  480.3 10.3 %copy-start.14 = (f32[7,768]{1,0:T(8,128)S(1)}, f32[7,768]{1,0:T(8,128)}, u32[]{:S(2)}) copy-start(f32[7,768]{1,0:T(8,128)} %param.37) | copy-start | bytes 64516
  480.3 4.1 collective-permute-start.5
  484.4 5.0 collective-permute-start.6
